TPU v7x, 128 devices: a whole 4x4x4 slice. The times are simulated.
128 devices in a mesh: tm: 16 (over x_lo, y, core), seq: 8 (over x_hi, z).
Axes of the slice: x: 4 (x_hi: 2, x_lo: 2; x = x_hi * 2 + x_lo), y: 4, z: 4, core: 2. Of those that a mesh axis runs over, the one named last changes fastest.
Arguments:
- states: float32 [16, 512, 5120], P('tm', 'seq'), may hold values from -6 to 6
- start: float32 [512, 5120], P('seq'), may hold values from -6 to 6
- t_index: int32 [16], P('tm'), may hold values from 0 to 49
- coef: float32 [50], replicated, may hold values from 0.05 to 0.5
- mod_table: float32 [50, 3, 5120], replicated, may hold values from -3 to 3
- wqkv: bfloat16 [3, 5120, 5120], P(None, 'tm', 'seq'), may hold values from -0.078125 to 0.078125
- wo: bfloat16 [5120, 5120], P('seq'), may hold values from -0.078125 to 0.078125
Outputs:
- new_states: float32 [16, 512, 5120], P('tm', 'seq')
All inputs are finite; a program needn't handle non-finite values.
Results may differ from a plain program's by a relative error of at most 0.0023.
Values may be sent and summed in bfloat16 or wider, within the bound.
No kernel may reach another device: no remote copies, remote signals or barrier semaphores. Data moves between devices by JAX's collectives and lax.ppermute only.
A program may use at most 128 MiB of HBM per device.

v0:
```python
import jax
import jax.numpy as jnp
from jax import lax
from jax.sharding import PartitionSpec as P

HEAD_DIM = 128


def entering(array, axis, combine, identity):
    size, here = (lax.axis_size(axis), lax.axis_index(axis))
    everything = lax.all_gather(array, axis)
    start = jnp.broadcast_to(jnp.asarray(identity, array.dtype), array.shape)

    def step(k, before):
        reached = k < here
        new = combine(before, everything[k])
        return jnp.where(reached, new, before)

    return lax.fori_loop(0, size, step, start)


def prepare(projected):
    count = projected.shape[1]
    per_head = projected.reshape(3, count, -1, HEAD_DIM)
    query_key = per_head[:2]
    query_key = query_key * lax.rsqrt(
        jnp.mean(query_key * query_key, axis=-1, keepdims=True) + 1e-06
    )
    return jnp.concatenate([query_key, per_head[2:]], axis=0).astype(jnp.bfloat16)


def add_terms(earlier, later):
    return earlier + later


def on_device(states, start, t_index, coef, mod_table, wqkv, wo):
    state = states[0]
    plan = mod_table.shape[0]
    selector = (jnp.arange(plan, dtype=jnp.int32)[None, :] == t_index[:, None]).astype(jnp.float32)
    modulation = jnp.einsum("ws,sjd->wjd", selector, mod_table, precision=lax.Precision.HIGHEST)[0]
    factor = jnp.dot(selector, coef, precision=lax.Precision.HIGHEST)[0]
    shift_row, scale_row, gate_row = (modulation[0], modulation[1], modulation[2])
    center = jnp.mean(state, axis=-1, keepdims=True)
    spread = jnp.mean((state - center) * (state - center), axis=-1, keepdims=True)
    modded = ((state - center) * lax.rsqrt(spread + 1e-06) * (1.0 + scale_row) + shift_row).astype(
        jnp.bfloat16
    )
    own_weights = lax.all_gather(wqkv, "tm", axis=1, tiled=True)
    projected = jnp.einsum(
        "td,jdc->jtc",
        lax.all_gather(modded, "seq", axis=0, tiled=True),
        own_weights,
        preferred_element_type=jnp.float32,
    )
    prepared = prepare(projected)
    query, keys, values = (prepared[0], prepared[1], prepared[2])
    scores = jnp.einsum(
        "qhc,khc->hqk", query, keys, preferred_element_type=jnp.float32
    ) * HEAD_DIM ** (-0.5)
    expo = jnp.exp(scores)
    weights = (expo / jnp.sum(expo, axis=-1, keepdims=True)).astype(jnp.bfloat16)
    attended = jnp.einsum(
        "hqk,khc->qhc", weights, values, preferred_element_type=jnp.float32
    ).astype(jnp.bfloat16)
    attended = attended.reshape(attended.shape[0], -1)
    output = lax.psum_scatter(
        jnp.dot(attended, wo, preferred_element_type=jnp.float32),
        "seq",
        scatter_dimension=0,
        tiled=True,
    )
    drift = (gate_row * output).astype(jnp.bfloat16)
    term = factor * drift.astype(jnp.float32)
    earlier = entering(term, "tm", add_terms, jnp.zeros_like(term))
    result = (start + earlier + term)[None]
    return result


def solution(mesh):
    placed = (
        P("tm", "seq", None),
        P("seq", None),
        P("tm"),
        P(),
        P(),
        P(None, "tm", "seq"),
        P("seq", None),
    )
    return jax.shard_map(
        on_device, mesh=mesh, in_specs=placed, out_specs=P("tm", "seq", None), check_vma=False
    )
```

profile of v0, /device:TPU:1, one launch (start us, length us, event | category | flops | bytes accessed | tf_op | source)
XLA Modules:
  0.0 548.9 jit_solution(13774040472437087007)
XLA Ops:
  7.3 1.2 copy-done
  8.5 1.2 fusion.9
  9.8 1.6 reduce_sum.36
  11.4 0.0 copy-done.2
  11.5 0.3 multiply_reduce_fusion.1
  11.8 1.1 add_convert_fusion
  12.9 0.0 all-gather.7.cloned.1.call-start
  13.0 0.7 all-gather.7.cloned.1.call-update
  13.7 0.0 reduce-scatter.2.cloned.1.call-start
  13.7 82.5 %all-gather.5.cloned.1.call-done = bf16[512,5120]{1,0:T(8,128)(2,1)} async-done(((bf16[64,5120]{1,0:T(8,128)(2,1)}), bf16[512,5120]{1,0:T(8,128)(2,1)}) %all-gather.5.cloned.1.call-update) | async-done | bytes 5242896 | tf_op jit(solution)/shard_map/all_gather | solution.py:51
  96.2 105.4 %all-gather.7.cloned.1.call-done = bf16[3,5120,640]{2,1,0:T(8,128)(2,1)} async-done(((bf16[3,320,640]{2,1,0:T(8,128)(2,1)}), bf16[3,5120,640]{2,1,0:T(8,128)(2,1)}) %all-gather.7.cloned.1.call-update) | async-done | bytes 19660816 | tf_op jit(solution)/shard_map/all_gather | solution.py:48
  201.6 15.8 %fusion.4 = f32[3,512,640]{2,1,0:T(8,128)S(1)} fusion(bf16[3,5120,640]{2,1,0:T(8,128)(2,1)} %all-gather.7.cloned.1.call-done, bf16[512,5120]{1,0:T(8,128)(2,1)} %all-gather.5.cloned.1.call-done), kind=kOutput, calls=%fused_computation.9 | convolution fusion | flops 10066329600 | bytes 28835840 | tf_op jit(solution)/shard_map/td,jdc->jtc/dot_general | solution.py:49
  217.5 1.8 copy-done.4
  219.3 1.7 slice.42
  221.0 2.1 copy.12
  223.1 2.1 copy.13
  225.3 0.3 multiply_reduce_fusion
  225.6 1.6 slice.51
  227.2 0.2 copy-done.3
  227.4 0.8 multiply_convert_fusion
  228.2 3.2 fusion.2
  231.4 0.3 copy.11
  231.7 3.6 fusion.7
  235.3 9.7 %fusion.17 = f32[512,5120]{1,0:T(8,128)} fusion(bf16[512,640]{0,1:T(8,128)(2,1)S(1)} %bitcast.55, bf16[640,5120]{1,0:T(8,128)(2,1)} %param.15), kind=kOutput, calls=%fused_computation.35 | convolution fusion | flops 3355443200 | bytes 17694720 | tf_op jit(solution)/shard_map/dot_general | solution.py:67
  245.0 0.0 all-gather.9.cloned.1.call-start
  245.1 0.6 copy-done.5
  245.6 0.6 fusion.13
  246.2 132.3 %reduce-scatter.2.cloned.1.call-done = f32[64,5120]{1,0:T(8,128)} async-done(((f32[512,5120]{1,0:T(8,128)}), f32[64,5120]{1,0:T(8,128)}) %reduce-scatter.2.cloned.1.call-update) | async-done | bytes 1310736 | tf_op jit(solution)/shard_map/reduce_scatter | solution.py:66
  378.5 3.1 convert_multiply_fusion
  381.7 110.3 %all-gather.9.cloned.1.call-done = f32[1024,5120]{1,0:T(8,128)} async-done(((f32[64,5120]{1,0:T(8,128)}), f32[1024,5120]{1,0:T(8,128)}) %all-gather.9.cloned.1.call-update) | async-done | bytes 20971536 | tf_op jit(solution)/shard_map/all_gather | solution.py:11
  492.0 46.0 %while.14 = (s32[]{:T(128)}, f32[64,5120]{1,0:T(8,128)}, s32[]{:T(128)}, f32[16,64,5120]{2,1,0:T(8,128)}, s32[]{:T(128)}, /*index=5*/s32[]{:T(128)}) while((s32[]{:T(128)}, f32[64,5120]{1,0:T(8,128)}, s32[]{:T(128)}, f32[16,64,5120]{2,1,0:T(8,128)}, s32[]{:T(128)}, /*index=5*/s32[]{:T(128)}) %tuple.46), condition=%wide.region_6.7_spmd.clone, body=%wide.region_5.6_spmd.clone.sunk | while | flops 983044 | bytes 3932253 | solution.py:19
  492.0 2.5 add_select_fusion.2
  494.5 2.9 add_select_fusion.2
  497.4 2.9 add_select_fusion.2
  500.3 2.9 add_select_fusion.2
  503.2 2.9 add_select_fusion.2
  506.1 2.9 add_select_fusion.2
  509.0 2.9 add_select_fusion.2
  511.9 2.9 add_select_fusion.2
  514.8 2.9 add_select_fusion.2
  517.7 2.9 add_select_fusion.2
  520.6 2.9 add_select_fusion.2
  523.5 2.9 add_select_fusion.2
  526.4 2.9 add_select_fusion.2
  529.3 2.9 add_select_fusion.2
  532.2 2.9 add_select_fusion.2
  535.1 2.9 add_select_fusion.2
  538.0 4.3 add_bitcast_fusion
  (17 shorter events, 0.2 us)
Async XLA Ops:
  6.5 2.0 copy-start
  6.5 89.7 %all-gather.5.cloned.1.call-start = ((), (), s32[]{:S(2)}) async-start(), calls=%async_computation.1 | async-start | bytes 5898240 | tf_op jit(solution)/shard_map/all_gather | solution.py:51
  9.8 1.7 copy-start.2
  12.9 188.7 %all-gather.7.cloned.1.call-start = ((), (), s32[]{:S(2)}) async-start(), calls=%async_computation.2 | async-start | bytes 20889600 | tf_op jit(solution)/shard_map/all_gather | solution.py:48
  13.7 364.8 %reduce-scatter.2.cloned.1.call-start = ((), (), s32[]{:S(2)}) async-start(), calls=%async_computation.3 | async-start | bytes 11796480 | tf_op jit(solution)/shard_map/reduce_scatter | solution.py:66
  217.5 1.9 copy-start.4
  225.3 2.1 copy-start.3
  245.0 0.7 copy-start.5
  245.0 247.0 %all-gather.9.cloned.1.call-start = ((), (), s32[]{:S(2)}) async-start(), calls=%async_computation.4 | async-start | bytes 22282240 | tf_op jit(solution)/shard_map/all_gather | solution.py:11
  538.0 4.3 copy-start.1
Sparse Core Ops, SparseCore 0:
  13.1 83.1 all-gather.4
  97.9 103.7 all-gather.6
  245.1 133.3 reduce-scatter.1
  381.8 110.1 all-gather.8
where the time goes:
time: 550 us; the launch traced here: 549 us
  waiting for transfers between devices  431 us (78%)
  other arithmetic  58.3 us (11%)
  matrix products  33.5 us (6%)
  between operations  14 us (3%)
  local copies, waits for them, and re-layouts  11.6 us (2%)
    reduce_scatter x1, waiting for transfers between devices, on_device(): lax.psum_scatter(jnp.dot(attended, wo, preferred_element_type=jnp.float32...  132 us
    all_gather x1, waiting for transfers between devices, entering(): everything = lax.all_gather(array, axis)  110 us
    all_gather x1, waiting for transfers between devices, on_device(): own_weights = lax.all_gather(wqkv, 'tm', axis=1, tiled=True)  105 us
    all_gather x1, waiting for transfers between devices, on_device(): lax.all_gather(modded, 'seq', axis=0, tiled=True)  82.5 us
    select_n x16, other arithmetic, step(): return jnp.where(reached, new, before)  46 us
    dot_general x1, matrix products, on_device(): jnp.einsum('td,jdc->jtc', lax.all_gather(modded, 'seq', axis=0, tiled=Tru...  15.8 us
  transfers between devices with their start and end apart: 4, of which 4 were waited for; matrix products, arithmetic and copies ran while one was open for 0% of the time, Pallas kernels for 0%

commit v1 on v0

v1 whole, which is shorter than its diff:
```python
import jax
import jax.numpy as jnp
from jax import lax
from jax.sharding import Mesh, PartitionSpec as P

HEAD_DIM = 128
TM = ("xl", "y", "core")
SEQ = ("xh", "z")


def send(array, axis, shift):
    size = lax.axis_size(axis)
    return lax.ppermute(array, axis, [(i, (i + shift) % size) for i in range(size)])


def gather_tokens(modded):
    half = modded.shape[0] // 2
    rows = []
    for block in (modded, send(modded, "xh", 1)):
        above = send(block, "z", -1)
        below = send(block, "z", 1)
        far = jnp.concatenate(
            [send(above[:half], "z", -1), send(below[half:], "z", 1)], axis=0
        )
        rows.append([block, above, far, below])
    return rows


def normed(projected):
    per_head = projected.reshape(projected.shape[0], -1, HEAD_DIM)
    scaled = per_head * lax.rsqrt(
        jnp.mean(per_head * per_head, axis=-1, keepdims=True) + 1e-06
    )
    return scaled.astype(jnp.bfloat16)


def on_device(states, start, t_index, coef, mod_table, wqkv, wo):
    state = states[0]
    tokens, width = state.shape
    step = t_index[0]
    modulation = lax.dynamic_index_in_dim(mod_table, step, 0, keepdims=False)
    factor = lax.dynamic_index_in_dim(coef, step, 0, keepdims=False)
    shift_row, scale_row, gate_row = (modulation[0], modulation[1], modulation[2])
    weights_of = [lax.all_gather(wqkv[j], TM, axis=0, tiled=True) for j in range(3)]
    center = jnp.mean(state, axis=-1, keepdims=True)
    spread = jnp.mean((state - center) * (state - center), axis=-1, keepdims=True)
    modded = ((state - center) * lax.rsqrt(spread + 1e-06) * (1.0 + scale_row) + shift_row).astype(
        jnp.bfloat16
    )
    rows = gather_tokens(modded)
    features = jnp.concatenate([block for row in rows for block in row], axis=0)
    projected = [
        jnp.dot(features, w, preferred_element_type=jnp.float32) for w in weights_of
    ]
    query, keys = normed(projected[0]), normed(projected[1])
    values = projected[2].reshape(features.shape[0], -1, HEAD_DIM).astype(jnp.bfloat16)
    scores = jnp.einsum(
        "qhc,khc->hqk", query, keys, preferred_element_type=jnp.float32
    ) * HEAD_DIM ** (-0.5)
    expo = jnp.exp(scores)
    weights = (expo / jnp.sum(expo, axis=-1, keepdims=True)).astype(jnp.bfloat16)
    attended = jnp.einsum(
        "hqk,khc->qhc", weights, values, preferred_element_type=jnp.float32
    ).astype(jnp.bfloat16)
    attended = attended.reshape(attended.shape[0], -1)
    partial = jnp.dot(attended, wo, preferred_element_type=jnp.float32).astype(jnp.bfloat16)
    nx, nz = lax.axis_size("xh"), lax.axis_size("z")
    xh, z = lax.axis_index("xh"), lax.axis_index("z")
    partial = partial.reshape(nx * nz, tokens, width)
    place = [((a + xh) % nx) * nz + (b - z + nz) % nz for a in range(nx) for b in range(nz)]
    partial = jnp.stack([lax.dynamic_index_in_dim(partial, p, 0, keepdims=False) for p in place])
    arrived = lax.all_to_all(partial, SEQ, 0, 0, tiled=False)
    output = jnp.sum(arrived.astype(jnp.float32), axis=0)
    term = ((factor * gate_row) * output).astype(jnp.bfloat16)
    steps = lax.axis_size(TM)
    by_step = lax.all_to_all(term.reshape(steps, tokens // steps, width), TM, 0, 0)
    total = jnp.cumsum(by_step.astype(jnp.float32), axis=0).astype(jnp.bfloat16)
    total = lax.all_to_all(total, TM, 0, 0).reshape(tokens, width)
    return (start + total.astype(jnp.float32))[None]


def solution(mesh):
    wide = Mesh(mesh.devices.reshape(2, 4, 2, 2, 4), TM + SEQ)
    placed = (
        P(TM, SEQ, None),
        P(SEQ, None),
        P(TM),
        P(),
        P(),
        P(None, TM, SEQ),
        P(SEQ, None),
    )
    return jax.shard_map(
        on_device, mesh=wide, in_specs=placed, out_specs=P(TM, SEQ, None), check_vma=False
    )
```

time: 550 us -> 289 us (0.53)
  waiting for transfers between devices: 431 us -> 104 us
  blocking collectives: 0 us -> 100 us
  other arithmetic: 58.3 us -> 7.61 us
  starting transfers between devices: 0.12 us -> 17.1 us
    all_gather x3, waiting for transfers between devices: 298 us -> 65 us  [on_device(): lax.all_gather(wqkv[j], TM, axis=0, tiled=True)]
    reduce_scatter x1 -> x0, waiting for transfers between devices: 132 us -> none  [on_device(): lax.psum_scatter(jnp.dot(attended, wo, preferred_element_type=jnp.float32...]
    all_to_all x0 -> x3, blocking collectives: none -> 100 us  [the longest x1 67.1 us: on_device(): arrived = lax.all_to_all(partial, SEQ, 0, 0, tiled=False)]
    select_n x16 -> x0, other arithmetic: 46 us -> none  [step(): return jnp.where(reached, new, before)]
    ppermute x0 -> x9, waiting for transfers between devices: none -> 37.9 us  [send(): lax.ppermute(array, axis, [(i, (i + shift) % size) for i in range(size)])]
    ppermute x0 -> x9, starting transfers between devices: none -> 17 us  [send(): lax.ppermute(array, axis, [(i, (i + shift) % size) for i in range(size)])]
    dot_general x2 -> x3, matrix products: 17 us -> 25.7 us  [on_device(): jnp.dot(features, w, preferred_element_type=jnp.float32)]
  transfers between devices with their start and end apart: 4 -> 12, of which waited for: 4 -> 7; matrix products, arithmetic and copies ran while one was open for 0% -> 11% of each run, Pallas kernels for 0% -> 0%
where the time goes in v1:
time: 289 us
  waiting for transfers between devices  104 us (36%)
  blocking collectives  100 us (35%)
  matrix products  32.5 us (11%)
  starting transfers between devices  17.1 us (6%)
  between operations  14 us (5%)
  local copies, waits for them, and re-layouts  13.4 us (5%)
  other arithmetic  7.61 us (3%)
    all_to_all x1, blocking collectives, on_device(): arrived = lax.all_to_all(partial, SEQ, 0, 0, tiled=False)  67.1 us
    all_gather x3, waiting for transfers between devices, on_device(): lax.all_gather(wqkv[j], TM, axis=0, tiled=True)  65 us
    ppermute x9, waiting for transfers between devices, send(): lax.ppermute(array, axis, [(i, (i + shift) % size) for i in range(size)])  37.9 us
    dot_general x3, matrix products, on_device(): jnp.dot(features, w, preferred_element_type=jnp.float32)  25.7 us
    all_to_all x1, blocking collectives, on_device(): lax.all_to_all(term.reshape(steps, tokens // steps, width), TM, 0, 0)  18 us
    ppermute x9, starting transfers between devices, send(): lax.ppermute(array, axis, [(i, (i + shift) % size) for i in range(size)])  17 us
    all_to_all x1, blocking collectives, on_device(): total = lax.all_to_all(total, TM, 0, 0).reshape(tokens, width)  14.9 us
    unnamed x23, local copies, waits for them, and re-layouts  7.88 us
  transfers between devices with their start and end apart: 12, of which 7 were waited for; matrix products, arithmetic and copies ran while one was open for 11% of the time, Pallas kernels for 0%

profile of v1, /device:TPU:1, one launch (start us, length us, event | category | flops | bytes accessed | tf_op | source)
XLA Modules:
  0.0 288.8 jit_solution(3299350184460694517)
XLA Ops:
  6.5 2.5 fusion.17
  9.1 0.7 all-gather.11.cloned.1.call-update
  9.8 0.7 all-gather.9.cloned.1.call-update
  11.2 1.3 dynamic_slice.33
  12.4 1.5 reduce_sum.56
  13.9 0.3 multiply_reduce_fusion.2
  14.2 1.8 dynamic-slice_multiply_fusion
  16.0 1.2 constant_dynamic-update-slice_fusion.9
  17.2 4.6 %collective-permute-start = (bf16[64,5120]{1,0:T(8,128)(2,1)S(1)}, bf16[64,5120]{1,0:T(8,128)(2,1)S(1)}, u32[]{:S(2)}, u32[]{:S(2)}) collective-permute-start(bf16[64,5120]{1,0:T(8,128)(2,1)S(1)} %get-tuple-element.6), channel_id=1, source_target_pairs={{0,3},{1,0},{2,1},{3,2},{4,7},{5,4},{6,5},{7,6},{8,11},{9,8},{10,9... | collective-permute-start | bytes 1966088 | tf_op jit(solution)/shard_map/ppermute | solution.py:13
  21.8 2.7 collective-permute-start.4
  24.5 10.7 %collective-permute-done = bf16[64,5120]{1,0:T(8,128)(2,1)S(1)} collective-permute-done((bf16[64,5120]{1,0:T(8,128)(2,1)S(1)}, bf16[64,5120]{1,0:T(8,128)(2,1)S(1)}, u32[]{:S(2)}, u32[]{:S(2)}) %collective-permute-start) | collective-permute-done | bytes 655392 | tf_op jit(solution)/shard_map/ppermute | solution.py:13
  35.2 3.5 %collective-permute-start.1 = (bf16[32,5120]{1,0:T(8,128)(2,1)S(1)}, bf16[32,5120]{1,0:T(8,128)(2,1)S(1)}, u32[]{:S(2)}, u32[]{:S(2)}) collective-permute-start(bf16[32,5120]{1,0:T(8,128)(2,1)S(1)} %slice.43), channel_id=1, source_target_pairs={{0,3},{1,0},{2,1},{3,2},{4,7},{5,4},{6,5},{7,6},{8,11},{9,8},{10,9... | collective-permute-start | bytes 983048 | tf_op jit(solution)/shard_map/ppermute | solution.py:13
  38.8 14.3 %collective-permute-done.4 = bf16[64,5120]{1,0:T(8,128)(2,1)S(1)} collective-permute-done((bf16[64,5120]{1,0:T(8,128)(2,1)S(1)}, bf16[64,5120]{1,0:T(8,128)(2,1)S(1)}, u32[]{:S(2)}, u32[]{:S(2)}) %collective-permute-start.4) | collective-permute-done | bytes 655392 | tf_op jit(solution)/shard_map/ppermute | solution.py:13
  53.1 2.6 collective-permute-start.5
  55.7 0.9 constant_dynamic-update-slice_fusion.8
  56.5 0.7 constant_dynamic-update-slice_fusion.7
  57.3 0.8 constant_dynamic-update-slice_fusion.6
  58.1 0.9 constant_dynamic-update-slice_fusion.5
  58.9 0.9 constant_dynamic-update-slice_fusion.4
  59.8 7.4 %collective-permute-done.5 = bf16[64,5120]{1,0:T(8,128)(2,1)S(1)} collective-permute-done((bf16[64,5120]{1,0:T(8,128)(2,1)S(1)}, bf16[64,5120]{1,0:T(8,128)(2,1)S(1)}, u32[]{:S(2)}, u32[]{:S(2)}) %collective-permute-start.5) | collective-permute-done | bytes 655392 | tf_op jit(solution)/shard_map/ppermute | solution.py:13
  67.3 3.5 %collective-permute-start.6 = (bf16[32,5120]{1,0:T(8,128)(2,1)S(1)}, bf16[32,5120]{1,0:T(8,128)(2,1)S(1)}, u32[]{:S(2)}, u32[]{:S(2)}) collective-permute-start(bf16[32,5120]{1,0:T(8,128)(2,1)S(1)} %slice.45), channel_id=1, source_target_pairs={{0,3},{1,0},{2,1},{3,2},{4,7},{5,4},{6,5},{7,6},{8,11},{9,8},{10,9... | collective-permute-start | bytes 983048 | tf_op jit(solution)/shard_map/ppermute | solution.py:13
  70.9 0.9 constant_dynamic-update-slice_fusion.3
  71.8 3.0 %collective-permute-done.6 = bf16[32,5120]{1,0:T(8,128)(2,1)S(1)} collective-permute-done((bf16[32,5120]{1,0:T(8,128)(2,1)S(1)}, bf16[32,5120]{1,0:T(8,128)(2,1)S(1)}, u32[]{:S(2)}, u32[]{:S(2)}) %collective-permute-start.6) | collective-permute-done | bytes 327712 | tf_op jit(solution)/shard_map/ppermute | solution.py:13
  74.8 0.8 constant_dynamic-update-slice_fusion.2
  75.5 2.5 collective-permute-done.8
  78.0 0.8 constant_dynamic-update-slice_fusion.1
  78.7 0.9 constant_dynamic-update-slice_fusion
  79.6 8.9 %fusion.9 = bf16[512,640]{1,0:T(8,128)(2,1)S(1)} fusion(bf16[512,5120]{1,0:T(8,128)(2,1)} %constant_dynamic-update-slice_fusion, bf16[1,5120,640]{2,1,0:T(8,128)(2,1)} %all-gather.7.cloned.1.call-done), kind=kOutput, calls=%fused_computation.14 | convolution fusion | flops 3355770880 | bytes 12451840 | tf_op jit(solution)/shard_map/dot_general | solution.py:53
  88.5 0.3 copy.12
  88.8 27.4 %all-gather.11.cloned.1.call-done = bf16[1,5120,640]{2,1,0:T(8,128)(2,1)} async-done(((bf16[1,320,640]{2,1,0:T(8,128)(2,1)}), bf16[1,5120,640]{2,1,0:T(8,128)(2,1)}) %all-gather.11.cloned.1.call-update) | async-done | bytes 6553616 | tf_op jit(solution)/shard_map/all_gather | solution.py:44
  116.2 8.4 %fusion = f32[512,640]{0,1:T(8,128)S(1)} fusion(bf16[512,5120]{1,0:T(8,128)(2,1)} %constant_dynamic-update-slice_fusion, bf16[1,5120,640]{2,1,0:T(8,128)(2,1)} %all-gather.11.cloned.1.call-done), kind=kOutput, calls=%fused_computation.2 | convolution fusion | flops 3355443200 | bytes 13107200 | tf_op jit(solution)/shard_map/dot_general | solution.py:53
  124.6 0.2 multiply_reduce_fusion
  124.8 37.6 %all-gather.9.cloned.1.call-done = bf16[1,5120,640]{2,1,0:T(8,128)(2,1)} async-done(((bf16[1,320,640]{2,1,0:T(8,128)(2,1)}), bf16[1,5120,640]{2,1,0:T(8,128)(2,1)}) %all-gather.9.cloned.1.call-update) | async-done | bytes 6553616 | tf_op jit(solution)/shard_map/all_gather | solution.py:44
  162.4 8.4 %fusion.2 = f32[512,640]{0,1:T(8,128)S(1)} fusion(bf16[512,5120]{1,0:T(8,128)(2,1)} %constant_dynamic-update-slice_fusion, bf16[1,5120,640]{2,1,0:T(8,128)(2,1)} %all-gather.9.cloned.1.call-done), kind=kOutput, calls=%fused_computation.4 | convolution fusion | flops 3355443200 | bytes 13107200 | tf_op jit(solution)/shard_map/dot_general | solution.py:53
  170.8 0.2 multiply_reduce_fusion.1
  171.0 1.1 fusion.6
  172.1 1.1 fusion.8
  173.2 0.9 slice-done.1
  174.1 4.5 %convolution_convert_fusion = bf16[512,5120]{1,0:T(8,128)(2,1)S(1)} fusion(bf16[512,640]{0,1:T(8,128)(2,1)S(1)} %bitcast.59, bf16[640,5120]{1,0:T(8,128)(2,1)S(1)} %bitcast.58), kind=kOutput, calls=%fused_computation.1 | convolution fusion | flops 3358064640 | bytes 12451840 | tf_op jit(solution)/shard_map/dot_general | solution.py:66
  179.2 67.1 %all_to_all.15 = bf16[8,64,5120]{2,1,0:T(8,128)(2,1)S(1)} all-to-all(bf16[8,64,5120]{2,1,0:T(8,128)(2,1)S(1)} %dynamic-slice_dynamic-update-slice_fusion), channel_id=1, replica_groups=mesh['xl'=2,'y'=4,'core'=2,'xh'=2,'z'=4] {'xh','z'}, dimensions={0} | all-to-all | bytes 10485760 | tf_op jit(solution)/shard_map/all_to_all | solution.py:72
  246.2 0.9 convert_reduce_fusion
  247.1 0.4 reduce_sum.62
  247.5 0.2 multiply_convert_fusion
  247.8 18.0 %all_to_all.16 = bf16[16,4,5120]{2,1,0:T(4,128)(2,1)S(1)} all-to-all(bf16[16,4,5120]{2,1,0:T(4,128)(2,1)S(1)} %multiply_convert_fusion), channel_id=1, replica_groups=mesh['xl'=2,'y'=4,'core'=2,'xh'=2,'z'=4] {'xl','y','core'}, dimensions={0} | all-to-all | bytes 1310720 | tf_op jit(solution)/shard_map/all_to_all | solution.py:76
  265.8 0.3 reduce-window_convert_fusion
  266.1 14.9 %all_to_all.17 = bf16[16,4,5120]{2,1,0:T(4,128)(2,1)S(1)} all-to-all(bf16[16,4,5120]{2,1,0:T(4,128)(2,1)S(1)} %reduce-window_convert_fusion), channel_id=1, replica_groups=mesh['xl'=2,'y'=4,'core'=2,'xh'=2,'z'=4] {'xl','y','core'}, dimensions={0} | all-to-all | bytes 1310720 | tf_op jit(solution)/shard_map/all_to_all | solution.py:78
  281.0 0.1 reshape.77
  281.1 1.2 add_bitcast_fusion
  (37 shorter events, 0.8 us)
Async XLA Ops:
  6.5 7.4 %copy-start = (f32[1,64,5120]{2,1,0:T(8,128)S(1)}, f32[1,64,5120]{2,1,0:T(8,128)}, u32[]{:S(2)}) copy-start(f32[1,64,5120]{2,1,0:T(8,128)} %param.7) | copy-start | bytes 3932164
  6.5 73.1 %all-gather.7.cloned.1.call-start = ((), (), s32[]{:S(2)}) async-start(), calls=%async_computation.3 | async-start | bytes 6963200 | tf_op jit(solution)/shard_map/all_gather | solution.py:44
  9.0 107.2 %all-gather.11.cloned.1.call-start = ((), (), s32[]{:S(2)}) async-start(), calls=%async_computation.5 | async-start | bytes 6963200 | tf_op jit(solution)/shard_map/all_gather | solution.py:44
  9.8 152.6 %all-gather.9.cloned.1.call-start = ((), (), s32[]{:S(2)}) async-start(), calls=%async_computation.4 | async-start | bytes 6963200 | tf_op jit(solution)/shard_map/all_gather | solution.py:44
  17.2 18.0 %collective-permute-start = (bf16[64,5120]{1,0:T(8,128)(2,1)S(1)}, bf16[64,5120]{1,0:T(8,128)(2,1)S(1)}, u32[]{:S(2)}, u32[]{:S(2)}) collective-permute-start(bf16[64,5120]{1,0:T(8,128)(2,1)S(1)} %get-tuple-element.6), channel_id=1, source_target_pairs={{0,3},{1,0},{2,1},{3,2},{4,7},{5,4},{6,5},{7,6},{8,11},{9,8},{10,9... | collective-permute-start | bytes 1966088 | tf_op jit(solution)/shard_map/ppermute | solution.py:13
  21.8 16.9 %collective-permute-start.2 = (bf16[64,5120]{1,0:T(8,128)(2,1)S(1)}, bf16[64,5120]{1,0:T(8,128)(2,1)S(1)}, u32[]{:S(2)}, u32[]{:S(2)}) collective-permute-start(bf16[64,5120]{1,0:T(8,128)(2,1)S(1)} %get-tuple-element.6), channel_id=1, source_target_pairs={{0,1},{1,2},{2,3},{3,0},{4,5},{5,6},{6,7},{7,4},{8,9},{9,10},{10,1... | collective-permute-start | bytes 1966088 | tf_op jit(solution)/shard_map/ppermute | solution.py:13
  21.8 31.3 %collective-permute-start.4 = (bf16[64,5120]{1,0:T(8,128)(2,1)S(1)}, bf16[64,5120]{1,0:T(8,128)(2,1)S(1)}, u32[]{:S(2)}, u32[]{:S(2)}) collective-permute-start(bf16[64,5120]{1,0:T(8,128)(2,1)S(1)} %get-tuple-element.6), channel_id=1, source_target_pairs={{0,4},{4,0},{1,5},{5,1},{2,6},{6,2},{3,7},{7,3},{8,12},{12,8},{9,1... | collective-permute-start | bytes 1966088 | tf_op jit(solution)/shard_map/ppermute | solution.py:13
  35.2 21.4 %collective-permute-start.1 = (bf16[32,5120]{1,0:T(8,128)(2,1)S(1)}, bf16[32,5120]{1,0:T(8,128)(2,1)S(1)}, u32[]{:S(2)}, u32[]{:S(2)}) collective-permute-start(bf16[32,5120]{1,0:T(8,128)(2,1)S(1)} %slice.43), channel_id=1, source_target_pairs={{0,3},{1,0},{2,1},{3,2},{4,7},{5,4},{6,5},{7,6},{8,11},{9,8},{10,9... | collective-permute-start | bytes 983048 | tf_op jit(solution)/shard_map/ppermute | solution.py:13
  38.7 18.6 %collective-permute-start.3 = (bf16[32,5120]{1,0:T(8,128)(2,1)S(1)}, bf16[32,5120]{1,0:T(8,128)(2,1)S(1)}, u32[]{:S(2)}, u32[]{:S(2)}) collective-permute-start(bf16[32,5120]{1,0:T(8,128)(2,1)S(1)} %slice.44), channel_id=1, source_target_pairs={{0,1},{1,2},{2,3},{3,0},{4,5},{5,6},{6,7},{7,4},{8,9},{9,10},{10,1... | collective-permute-start | bytes 983048 | tf_op jit(solution)/shard_map/ppermute | solution.py:13
  53.1 14.2 %collective-permute-start.5 = (bf16[64,5120]{1,0:T(8,128)(2,1)S(1)}, bf16[64,5120]{1,0:T(8,128)(2,1)S(1)}, u32[]{:S(2)}, u32[]{:S(2)}) collective-permute-start(bf16[64,5120]{1,0:T(8,128)(2,1)S(1)} %collective-permute-done.4), channel_id=1, source_target_pairs={{0,3},{1,0},{2,1},{3,2},{4,7},{5,4},{6,5},{7,6},{8,11},{9,8},{10,9... | collective-permute-start | bytes 1966088 | tf_op jit(solution)/shard_map/ppermute | solution.py:13
  55.7 15.1 %collective-permute-start.7 = (bf16[64,5120]{1,0:T(8,128)(2,1)S(1)}, bf16[64,5120]{1,0:T(8,128)(2,1)S(1)}, u32[]{:S(2)}, u32[]{:S(2)}) collective-permute-start(bf16[64,5120]{1,0:T(8,128)(2,1)S(1)} %collective-permute-done.4), channel_id=1, source_target_pairs={{0,1},{1,2},{2,3},{3,0},{4,5},{5,6},{6,7},{7,4},{8,9},{9,10},{10,1... | collective-permute-start | bytes 1966088 | tf_op jit(solution)/shard_map/ppermute | solution.py:13
  67.3 7.5 %collective-permute-start.6 = (bf16[32,5120]{1,0:T(8,128)(2,1)S(1)}, bf16[32,5120]{1,0:T(8,128)(2,1)S(1)}, u32[]{:S(2)}, u32[]{:S(2)}) collective-permute-start(bf16[32,5120]{1,0:T(8,128)(2,1)S(1)} %slice.45), channel_id=1, source_target_pairs={{0,3},{1,0},{2,1},{3,2},{4,7},{5,4},{6,5},{7,6},{8,11},{9,8},{10,9... | collective-permute-start | bytes 983048 | tf_op jit(solution)/shard_map/ppermute | solution.py:13
  70.8 7.2 %collective-permute-start.8 = (bf16[32,5120]{1,0:T(8,128)(2,1)S(1)}, bf16[32,5120]{1,0:T(8,128)(2,1)S(1)}, u32[]{:S(2)}, u32[]{:S(2)}) collective-permute-start(bf16[32,5120]{1,0:T(8,128)(2,1)S(1)} %slice.46), channel_id=1, source_target_pairs={{0,1},{1,2},{2,3},{3,0},{4,5},{5,6},{6,7},{7,4},{8,9},{9,10},{10,1... | collective-permute-start | bytes 983048 | tf_op jit(solution)/shard_map/ppermute | solution.py:13
  171.0 2.2 slice-start
  172.1 2.1 slice-start.1
  247.5 33.6 %copy-start.1 = (f32[64,5120]{1,0:T(8,128)S(1)}, f32[64,5120]{1,0:T(8,128)}, u32[]{:S(2)}) copy-start(f32[64,5120]{1,0:T(8,128)} %param.8) | copy-start | bytes 3932164
Sparse Core Ops, SparseCore 0:
  9.2 61.0 all-gather.6
  71.9 44.2 all-gather.10
  117.9 44.4 all-gather.8

commit v2 on v1

v2 whole, which is shorter than its diff:
```python
import functools

import jax
import jax.numpy as jnp
from jax import lax
from jax.experimental import pallas as pl
from jax.experimental.pallas import tpu as pltpu
from jax.sharding import Mesh, PartitionSpec as P

HEAD_DIM = 128
TM = ("xl", "y", "core")
SEQ = ("xh", "z")
F32, BF16 = jnp.float32, jnp.bfloat16
VMEM_BYTES = 48 * 1024 * 1024
ROUND = [0, 1, 3, 2]
ORDER = [(0, 2), (1, 2), (1, 1), (1, 3), (0, 1), (0, 3), (1, 0), (0, 0)]


def send(array, axis, shift):
    size = lax.axis_size(axis)
    return lax.ppermute(array, axis, [(i, (i + shift) % size) for i in range(size)])


def after(array, *others):
    return lax.optimization_barrier((array,) + others)[0]


def add(a, b):
    return (a.astype(F32) + b.astype(F32)).astype(BF16)


def modulate_kernel(rows, t_ref, state_ref, mod_ref, coef_ref, mine_ref, other_ref, gate_ref, scratch):
    state = state_ref[0]
    line = pl.ds(lax.rem(t_ref[0], 8), 1)
    shift_row, scale_row = mod_ref[0, line, :], mod_ref[1, line, :]
    gate_ref[...] = mod_ref[2, line, :] * coef_ref[t_ref[0]]
    center = jnp.mean(state, axis=-1, keepdims=True)
    moved = state - center
    spread = jnp.mean(moved * moved, axis=-1, keepdims=True)
    scratch[...] = moved * lax.rsqrt(spread + 1e-06) * (1.0 + scale_row) + shift_row
    xl, y, core = (lax.axis_index(a) for a in TM)
    ny, wide = 4, 2 * rows
    low = core == 0
    for place, dy in enumerate(ROUND):
        mine, other = [], []
        for dxl in range(2):
            chip = lax.rem(xl + dxl, 2) * ny + lax.rem(y + dy, ny)
            block = scratch[:, pl.ds(pl.multiple_of(chip * wide, 128), wide)]
            first, second = block[:, :rows], block[:, rows:]
            mine.append(jnp.where(low, first, second))
            other.append(jnp.where(low, second, first))
        here = slice(place * wide, (place + 1) * wide)
        mine_ref[:, here] = jnp.concatenate(mine, axis=1).astype(BF16)
        other_ref[:, here] = jnp.concatenate(other, axis=1).astype(BF16)


def modulate(states, t_index, mod_table, coef, rows):
    _, tokens, width = states.shape
    half = jax.ShapeDtypeStruct((tokens, width // 2), BF16)
    return pl.pallas_call(
        functools.partial(modulate_kernel, rows),
        out_shape=(half, half, jax.ShapeDtypeStruct((1, width), F32)),
        grid_spec=pltpu.PrefetchScalarGridSpec(
            num_scalar_prefetch=1,
            grid=(1,),
            in_specs=[
                pl.BlockSpec((1, tokens, width), lambda i, t: (0, 0, 0)),
                pl.BlockSpec((3, 8, width), lambda i, t: (0, t[0] // 8, 0)),
                pl.BlockSpec(memory_space=pltpu.SMEM),
            ],
            out_specs=[
                pl.BlockSpec((tokens, width // 2), lambda i, t: (0, 0)),
                pl.BlockSpec((tokens, width // 2), lambda i, t: (0, 0)),
                pl.BlockSpec((1, width), lambda i, t: (0, 0)),
            ],
            scratch_shapes=[pltpu.VMEM((tokens, width), F32)],
        ),
        compiler_params=pltpu.CompilerParams(vmem_limit_bytes=VMEM_BYTES),
        cost_estimate=pl.CostEstimate(flops=1000, bytes_accessed=1000, transcendentals=0),
    )(t_index, states, jnp.transpose(mod_table, (1, 0, 2)), coef)


def attention_kernel(qa, qb, ka, kb, va, vb, out_ref):
    def whole(a, b):
        return a[...] + b[...].astype(F32)

    def normed(x):
        return (x * lax.rsqrt(jnp.mean(x * x, axis=-1, keepdims=True) + 1e-06)).astype(BF16)

    query, keys = normed(whole(qa, qb)), normed(whole(ka, kb))
    values = whole(va, vb).astype(BF16)
    scores = lax.dot_general(
        query, keys, (((1,), (1,)), ((), ())), preferred_element_type=F32
    ) * HEAD_DIM ** (-0.5)
    expo = jnp.exp(scores)
    weights = (expo * (1.0 / jnp.sum(expo, axis=-1, keepdims=True))).astype(BF16)
    out_ref[...] = jnp.dot(weights, values, preferred_element_type=F32).astype(BF16)


def attention(parts):
    count, width = parts[1].shape
    spec = pl.BlockSpec((count, HEAD_DIM), lambda h: (0, h))
    return pl.pallas_call(
        attention_kernel,
        out_shape=jax.ShapeDtypeStruct((count, width), BF16),
        grid=(width // HEAD_DIM,),
        in_specs=[spec] * 6,
        out_specs=spec,
        compiler_params=pltpu.CompilerParams(vmem_limit_bytes=VMEM_BYTES),
        cost_estimate=pl.CostEstimate(
            flops=4 * count * count * width, bytes_accessed=20 * count * width, transcendentals=0
        ),
    )(*parts)


def on_device(states, start, t_index, coef, mod_table, wqkv, wo):
    tokens, width = states.shape[1:]
    rows = wqkv.shape[1]
    half, short = rows // 2, tokens // 2

    own = wqkv
    a1, b1 = send(own, "y", -1), send(own, "y", 1)
    p = send(own[:2], "xl", 1)

    mine, other, gate_row = modulate(states, t_index, mod_table, coef, rows)
    pair = jnp.stack([mine, send(other, "core", 1)])

    za, zb = send(pair, "z", -1), send(pair, "z", 1)
    across = send(after(pair, p), "xh", 1)
    zfa = send(za[:, :short], "z", -1)
    zfb = send(zb[:, short:], "z", 1)

    pa = send(after(jnp.concatenate([p.reshape(2 * rows, -1), a1[2, :half]], axis=0), b1), "y", -1)
    pb = send(after(jnp.concatenate([p.reshape(2 * rows, -1), b1[2, half:]], axis=0), a1), "y", 1)
    farv = jnp.concatenate([pa[2 * rows :], pb[2 * rows :]], axis=0)
    pa, pb = pa[: 2 * rows].reshape(p.shape), pb[: 2 * rows].reshape(p.shape)
    xvo = send(after(own[2], across), "xl", 1)
    xvab = send(after(jnp.stack([a1[2], b1[2]]), xvo), "xl", 1)

    across = after(across, zfa, zfb)
    xa, xb = send(across, "z", -1), send(across, "z", 1)
    xfa = send(after(xa[:, :short], xvo), "z", -1)
    xfb = send(after(xb[:, short:], xvo), "z", 1)

    fa = send(jnp.concatenate([a1[:2, :half], pa[:, :half]], axis=0), "y", -1)
    fb = send(jnp.concatenate([b1[:2, half:], pb[:, half:]], axis=0), "y", 1)
    xvf = send(after(farv, xvab), "xl", 1)
    far = jnp.concatenate([fa, fb], axis=1)

    blocks = {
        (0, 0): pair, (0, 1): za, (0, 2): jnp.concatenate([zfa, zfb], axis=1), (0, 3): zb,
        (1, 0): across, (1, 1): xa, (1, 2): jnp.concatenate([xfa, xfb], axis=1), (1, 3): xb,
    }
    features = jnp.concatenate([blocks[k] for k in ORDER], axis=1)
    count = features.shape[1]
    features = features.reshape(2 * count, -1)
    early = 6 * rows
    parts = []
    begun = [
        jnp.dot(
            features[:, :early],
            jnp.concatenate([own[j], p[j], a1[j], pa[j], b1[j], pb[j]], axis=0),
            preferred_element_type=F32,
        )
        for j in range(2)
    ]
    begun = lax.optimization_barrier(begun)
    for j in range(3):
        if j < 2:
            here = begun[j] + jnp.dot(
                features[:, early:],
                jnp.concatenate([far[j], far[2 + j]], axis=0),
                preferred_element_type=F32,
            )
        else:
            here = jnp.dot(
                features,
                jnp.concatenate([own[2], xvo, a1[2], xvab[0], b1[2], xvab[1], farv, xvf], axis=0),
                preferred_element_type=F32,
            )
        parts += [here, send(here[count:].astype(BF16), "core", 1)]
    attended = attention(parts)

    cut = width // 2
    first = jnp.dot(attended[: 2 * tokens], wo, preferred_element_type=F32).astype(BF16)
    rest = jnp.dot(after(attended[2 * tokens :], first), wo, preferred_element_type=F32)
    part = {k: rest[i * tokens : (i + 1) * tokens] for i, k in enumerate(ORDER[2:])}
    first = first.reshape(2, tokens, width)
    up, down = send(first[:, :, :cut], "z", 1), send(first[:, :, cut:], "z", -1)

    def over_z(dx):
        raised = jnp.concatenate(
            [part[dx, 1][:, :cut] + up[dx].astype(F32), part[dx, 1][:, cut:]], axis=1
        ).astype(BF16)
        lowered = jnp.concatenate(
            [part[dx, 3][:, :cut], part[dx, 3][:, cut:] + down[dx].astype(F32)], axis=1
        ).astype(BF16)
        return (
            part[dx, 0] + send(raised, "z", 1).astype(F32) + send(lowered, "z", -1).astype(F32)
        )

    there = send(over_z(1).astype(BF16), "xh", 1)
    output = over_z(0) + there.astype(F32)
    term = (gate_row * output).astype(BF16)
    steps = lax.axis_size(TM)
    by_step = lax.all_to_all(term.reshape(steps, tokens // steps, width), TM, 0, 0)
    total = jnp.cumsum(by_step.astype(F32), axis=0).astype(BF16)
    total = lax.all_to_all(total, TM, 0, 0).reshape(tokens, width)
    return (start + total.astype(F32))[None]


def solution(mesh):
    wide = Mesh(mesh.devices.reshape(2, 4, 2, 2, 4), TM + SEQ)
    placed = (
        P(TM, SEQ, None),
        P(SEQ, None),
        P(TM),
        P(),
        P(),
        P(None, TM, SEQ),
        P(SEQ, None),
    )
    return jax.shard_map(
        on_device, mesh=wide, in_specs=placed, out_specs=P(TM, SEQ, None), check_vma=False
    )
```

time: 289 us -> 197 us (0.68)
  blocking collectives: 100 us -> 34.1 us
  starting transfers between devices: 17.1 us -> 46.8 us
  waiting for transfers between devices: 104 us -> 77.1 us
  matrix products: 32.5 us -> 18 us
  between operations: 14 us -> 1.26 us
  Pallas kernels: 0 us -> 7.32 us
  local copies, waits for them, and re-layouts: 13.4 us -> 8.74 us
  other arithmetic: 7.61 us -> 3.09 us
    all_to_all x1 -> x0, blocking collectives: 67.1 us -> none  [on_device(): arrived = lax.all_to_all(partial, SEQ, 0, 0, tiled=False)]
    all_gather x3 -> x0, waiting for transfers between devices: 65 us -> none  [on_device(): lax.all_gather(wqkv[j], TM, axis=0, tiled=True)]
    ppermute x9 -> x30, waiting for transfers between devices: 37.9 us -> 77.1 us  [send(): lax.ppermute(array, axis, [(i, (i + shift) % size) for i in range(size)])]
    ppermute x9 -> x30, starting transfers between devices: 17 us -> 46.8 us  [send(): lax.ppermute(array, axis, [(i, (i + shift) % size) for i in range(size)])]
    dot_general x6 -> x7, matrix products: 32.5 us -> 18 us  [the longest x2 6.69 us: on_device(): jnp.dot(features[:, :early], jnp.concatenate([own[j], p[j], a1[j], pa[j],...]
    pallas_call x0 -> x2, Pallas kernels: none -> 7.32 us  [the longest x1 5.86 us: attention(): pl.pallas_call(attention_kernel, out_shape=jax.ShapeDtypeStruct((count, w...]
    reduce_sum x5 -> x0, other arithmetic: 2.97 us -> none  [the longest x1 1.48 us: on_device(): center = jnp.mean(state, axis=-1, keepdims=True)]
    unnamed x23 -> x35, local copies, waits for them, and re-layouts: 7.88 us -> 6.74 us
  transfers between devices with their start and end apart: 12 -> 30, of which waited for: 7 -> 14; matrix products, arithmetic and copies ran while one was open for 11% -> 9% of each run, Pallas kernels for 0% -> 0%
where the time goes in v2:
time: 197 us
  waiting for transfers between devices  77.1 us (39%)
  starting transfers between devices  46.8 us (24%)
  blocking collectives  34.1 us (17%)
  matrix products  18 us (9%)
  local copies, waits for them, and re-layouts  8.74 us (4%)
  Pallas kernels  7.32 us (4%)
  other arithmetic  3.09 us (2%)
    ppermute x30, waiting for transfers between devices, send(): lax.ppermute(array, axis, [(i, (i + shift) % size) for i in range(size)])  77.1 us
    ppermute x30, starting transfers between devices, send(): lax.ppermute(array, axis, [(i, (i + shift) % size) for i in range(size)])  46.8 us
    all_to_all x1, blocking collectives, on_device(): lax.all_to_all(term.reshape(steps, tokens // steps, width), TM, 0, 0)  19 us
    all_to_all x1, blocking collectives, on_device(): total = lax.all_to_all(total, TM, 0, 0).reshape(tokens, width)  15.1 us
    unnamed x35, local copies, waits for them, and re-layouts  6.74 us
    dot_general x2, matrix products, on_device(): jnp.dot(features[:, :early], jnp.concatenate([own[j], p[j], a1[j], pa[j],...  6.69 us
    pallas_call x1, Pallas kernels, attention(): pl.pallas_call(attention_kernel, out_shape=jax.ShapeDtypeStruct((count, w...  5.86 us
    dot_general x1, matrix products, on_device(): jnp.dot(features, jnp.concatenate([own[2], xvo, a1[2], xvab[0], b1[2], xv...  4.21 us
  transfers between devices with their start and end apart: 30, of which 14 were waited for; matrix products, arithmetic and copies ran while one was open for 9% of the time, Pallas kernels for 0%

profile of v2, /device:TPU:1, one launch (start us, length us, event | category | flops | bytes accessed | tf_op | source)
XLA Modules:
  0.0 196.5 jit_solution(7008383423068903623)
XLA Ops:
  0.7 2.0 copy-done
  2.6 1.3 copy-done.1
  4.6 1.5 shard_map.73
  6.1 1.5 collective-permute-start
  7.6 1.4 collective-permute-start.13
  9.0 1.4 collective-permute-start.12
  10.5 1.3 collective-permute-start.5
  11.8 3.8 %collective-permute-start.1 = (bf16[2,64,2560]{2,1,0:T(8,128)(2,1)S(1)}, bf16[2,64,2560]{2,1,0:T(8,128)(2,1)S(1)}, u32[]{:S(2)}, u32[]{:S(2)}) collective-permute-start(bf16[2,64,2560]{2,1,0:T(8,128)(2,1)S(1)} %pad_maximum_fusion.5), channel_id=1, source_target_pairs={{0,3},{1,0},{2,1},{3,2},{4,7},{5,4},{6,5},{7,6},{8,11},{9,8},{10,9... | collective-permute-start | bytes 1966088 | tf_op jit(solution)/shard_map/ppermute | solution.py:21
  15.8 14.0 %collective-permute-done.5 = bf16[2,320,640]{2,1,0:T(8,128)(2,1)S(1)} collective-permute-done((bf16[2,320,640]{2,1,0:T(8,128)(2,1)S(1)}, bf16[2,320,640]{2,1,0:T(8,128)(2,1)S(1)}, u32[]{:S(2)}, u32[]{:S(2)}) %collective-permute-start.5) | collective-permute-done | bytes 819232 | tf_op jit(solution)/shard_map/ppermute | solution.py:21
  29.8 2.7 %collective-permute-start.6 = (bf16[2,64,2560]{2,1,0:T(8,128)(2,1)S(1)}, bf16[2,64,2560]{2,1,0:T(8,128)(2,1)S(1)}, u32[]{:S(2)}, u32[]{:S(2)}) collective-permute-start(bf16[2,64,2560]{2,1,0:T(8,128)(2,1)S(1)} %pad_maximum_fusion.5), channel_id=1, source_target_pairs={{0,4},{4,0},{1,5},{5,1},{2,6},{6,2},{3,7},{7,3},{8,12},{12,8},{9,1... | collective-permute-start | bytes 1966088 | tf_op jit(solution)/shard_map/ppermute | solution.py:21
  32.7 3.8 %collective-permute-start.2 = (bf16[2,32,2560]{2,1,0:T(8,128)(2,1)S(1)}, bf16[2,32,2560]{2,1,0:T(8,128)(2,1)S(1)}, u32[]{:S(2)}, u32[]{:S(2)}) collective-permute-start(bf16[2,32,2560]{2,1,0:T(8,128)(2,1)S(1)} %slice.268), channel_id=1, source_target_pairs={{0,3},{1,0},{2,1},{3,2},{4,7},{5,4},{6,5},{7,6},{8,11},{9,8},{10,9... | collective-permute-start | bytes 983048 | tf_op jit(solution)/shard_map/ppermute | solution.py:21
  36.6 1.0 collective-permute-done.13
  37.9 2.4 %collective-permute-start.14 = (bf16[800,640]{1,0:T(8,128)(2,1)S(1)}, bf16[800,640]{1,0:T(8,128)(2,1)S(1)}, u32[]{:S(2)}, u32[]{:S(2)}) collective-permute-start(bf16[800,640]{1,0:T(8,128)(2,1)S(1)} %get-tuple-element.28), channel_id=1, source_target_pairs={{0,48},{16,0},{32,16},{48,32},{1,49},{17,1},{33,17},{49,33},{2,50}... | collective-permute-start | bytes 3072008 | tf_op jit(solution)/shard_map/ppermute | solution.py:21
  40.5 5.7 %collective-permute-done.6 = bf16[2,64,2560]{2,1,0:T(8,128)(2,1)S(1)} collective-permute-done((bf16[2,64,2560]{2,1,0:T(8,128)(2,1)S(1)}, bf16[2,64,2560]{2,1,0:T(8,128)(2,1)S(1)}, u32[]{:S(2)}, u32[]{:S(2)}) %collective-permute-start.6) | collective-permute-done | bytes 655392 | tf_op jit(solution)/shard_map/ppermute | solution.py:21
  46.2 1.0 collective-permute-start.8
  47.3 3.8 %collective-permute-start.7 = (bf16[2,64,2560]{2,1,0:T(8,128)(2,1)S(1)}, bf16[2,64,2560]{2,1,0:T(8,128)(2,1)S(1)}, u32[]{:S(2)}, u32[]{:S(2)}) collective-permute-start(bf16[2,64,2560]{2,1,0:T(8,128)(2,1)S(1)} %collective-permute-done.6), channel_id=1, source_target_pairs={{0,3},{1,0},{2,1},{3,2},{4,7},{5,4},{6,5},{7,6},{8,11},{9,8},{10,9... | collective-permute-start | bytes 1966088 | tf_op jit(solution)/shard_map/ppermute | solution.py:21
  51.2 3.7 %collective-permute-done.8 = bf16[320,640]{1,0:T(8,128)(2,1)S(1)} collective-permute-done((bf16[320,640]{1,0:T(8,128)(2,1)S(1)}, bf16[320,640]{1,0:T(8,128)(2,1)S(1)}, u32[]{:S(2)}, u32[]{:S(2)}) %collective-permute-start.8) | collective-permute-done | bytes 409632 | tf_op jit(solution)/shard_map/ppermute | solution.py:21
  54.9 0.9 collective-permute-start.20
  56.1 6.4 %collective-permute-done.7 = bf16[2,64,2560]{2,1,0:T(8,128)(2,1)S(1)} collective-permute-done((bf16[2,64,2560]{2,1,0:T(8,128)(2,1)S(1)}, bf16[2,64,2560]{2,1,0:T(8,128)(2,1)S(1)}, u32[]{:S(2)}, u32[]{:S(2)}) %collective-permute-start.7) | collective-permute-done | bytes 655392 | tf_op jit(solution)/shard_map/ppermute | solution.py:21
  62.5 3.5 %collective-permute-start.9 = (bf16[2,32,2560]{2,1,0:T(8,128)(2,1)S(1)}, bf16[2,32,2560]{2,1,0:T(8,128)(2,1)S(1)}, u32[]{:S(2)}, u32[]{:S(2)}) collective-permute-start(bf16[2,32,2560]{2,1,0:T(8,128)(2,1)S(1)} %slice.270), channel_id=1, source_target_pairs={{0,3},{1,0},{2,1},{3,2},{4,7},{5,4},{6,5},{7,6},{8,11},{9,8},{10,9... | collective-permute-start | bytes 983048 | tf_op jit(solution)/shard_map/ppermute | solution.py:21
  66.4 1.4 collective-permute-start.16
  68.3 1.7 collective-permute-done.9
  70.1 3.2 %collective-permute-done.11 = bf16[2,32,2560]{2,1,0:T(8,128)(2,1)S(1)} collective-permute-done((bf16[2,32,2560]{2,1,0:T(8,128)(2,1)S(1)}, bf16[2,32,2560]{2,1,0:T(8,128)(2,1)S(1)}, u32[]{:S(2)}, u32[]{:S(2)}) %collective-permute-start.11) | collective-permute-done | bytes 327712 | tf_op jit(solution)/shard_map/ppermute | solution.py:21
  74.7 3.3 %fusion = f32[1024,640]{1,0:T(8,128)S(1)} fusion(bf16[1920,640]{1,0:T(8,128)(2,1)S(1)} %get-tuple-element.64, bf16[1024,2560]{1,0:T(8,128)(2,1)S(1)} %bitcast.104), kind=kOutput, calls=%fused_computation.2 | convolution fusion | flops 2516582400 | bytes 9011200 | tf_op jit(solution)/shard_map/dot_general | solution.py:160
  78.1 3.3 %fusion.2 = f32[1024,640]{1,0:T(8,128)S(1)} fusion(bf16[1920,640]{1,0:T(8,128)(2,1)S(1)} %get-tuple-element.65, bf16[1024,2560]{1,0:T(8,128)(2,1)S(1)} %bitcast.105), kind=kOutput, calls=%fused_computation.4 | convolution fusion | flops 2516582400 | bytes 9011200 | tf_op jit(solution)/shard_map/dot_general | solution.py:160
  81.4 0.9 collective-permute-done.16
  82.4 2.4 %collective-permute-done.17 = bf16[4,160,640]{2,1,0:T(8,128)(2,1)S(1)} collective-permute-done((bf16[4,160,640]{2,1,0:T(8,128)(2,1)S(1)}, bf16[4,160,640]{2,1,0:T(8,128)(2,1)S(1)}, u32[]{:S(2)}, u32[]{:S(2)}) %collective-permute-start.17) | collective-permute-done | bytes 819232 | tf_op jit(solution)/shard_map/ppermute | solution.py:21
  85.1 1.3 convolution_add_fusion.ka
  86.5 5.2 %collective-permute-start.19 = (bf16[512,640]{1,0:T(8,128)(2,1)S(1)}, bf16[512,640]{1,0:T(8,128)(2,1)S(1)}, u32[]{:S(2)}, u32[]{:S(2)}) collective-permute-start(bf16[512,640]{1,0:T(8,128)(2,1)S(1)} %slice.418), channel_id=1, source_target_pairs={{0,8},{8,0},{1,9},{9,1},{2,10},{10,2},{3,11},{11,3},{4,12},{12,4},... | collective-permute-start | bytes 1966088 | tf_op jit(solution)/shard_map/ppermute | solution.py:21
  91.7 1.3 convolution_add_fusion.1.qa
  93.3 4.2 %fusion.39.va = f32[1024,640]{1,0:T(8,128)S(1)} fusion(bf16[1024,2560]{1,0:T(8,128)(2,1)S(1)} %bitcast.108, bf16[2560,640]{1,0:T(8,128)(2,1)S(1)} %constant_dynamic-update-slice_fusion.12), kind=kOutput, calls=%fused_computation.108 | convolution fusion | flops 3355443200 | bytes 11141120 | tf_op jit(solution)/shard_map/dot_general | solution.py:176
  97.5 1.5 copy-done.5
  99.1 0.8 collective-permute-start.22
  99.9 1.7 collective-permute-done.22.vb
  101.6 5.9 %shard_map.74 = bf16[512,640]{1,0:T(8,128)(2,1)S(1)} custom-call(f32[1024,640]{1,0:T(8,128)S(1)} %convolution_add_fusion.1.qa, bf16[512,640]{1,0:T(8,128)(2,1)S(1)} %collective-permute-done.18.qb, f32[1024,640]{1,0:T(8,128)} %copy-done.3, bf16[512,640]{1,0:T(8,128)(2,1)S(1)} %collective-permute-done.19.kb, f32[1024,640]{1,0:T(8,128)} %copy-done.5, ...), custom_call_target="tpu_custom_call" | custom-call | flops 671088640 | bytes 6553600 | tf_op jit(solution)/shard_map/pallas_call | solution.py:103
  107.5 1.3 convolution_convert_fusion
  108.8 3.3 %fusion.38 = (bf16[384,5120]{1,0:T(8,128)(2,1)S(1)}, f32[384,5120]{1,0:T(8,128)S(1)}) fusion(bf16[384,640]{1,0:T(8,128)(2,1)S(1)} %slice.305, bf16[640,5120]{1,0:T(8,128)(2,1)S(1)} %bitcast.99), kind=kOutput, calls=%fused_computation.107 | convolution fusion | flops 2518548480 | bytes 18841600 | tf_op jit(solution)/shard_map/dot_general | solution.py:186
  112.3 2.7 %collective-permute-start.25 = (bf16[2,64,2560]{2,1,0:T(8,128)(2,1)S(1)}, bf16[2,64,2560]{2,1,0:T(8,128)(2,1)S(1)}, u32[]{:S(2)}, u32[]{:S(2)}) collective-permute-start(bf16[2,64,2560]{2,1,0:T(8,128)(2,1)S(1)} %get-tuple-element.50), channel_id=1, source_target_pairs={{0,3},{1,0},{2,1},{3,2},{4,7},{5,4},{6,5},{7,6},{8,11},{9,8},{10,9... | collective-permute-start | bytes 1966088 | tf_op jit(solution)/shard_map/ppermute | solution.py:21
  115.1 14.3 %collective-permute-done.23 = bf16[2,64,2560]{2,1,0:T(8,128)(2,1)S(1)} collective-permute-done((bf16[2,64,2560]{2,1,0:T(8,128)(2,1)S(1)}, bf16[2,64,2560]{2,1,0:T(8,128)(2,1)S(1)}, u32[]{:S(2)}, u32[]{:S(2)}) %collective-permute-start.23) | collective-permute-done | bytes 655392 | tf_op jit(solution)/shard_map/ppermute | solution.py:21
  129.8 0.9 collective-permute-start.27
  130.8 1.9 collective-permute-start.28
  132.9 2.7 %collective-permute-start.26 = (bf16[64,5120]{1,0:T(8,128)(2,1)S(1)}, bf16[64,5120]{1,0:T(8,128)(2,1)S(1)}, u32[]{:S(2)}, u32[]{:S(2)}) collective-permute-start(bf16[64,5120]{1,0:T(8,128)(2,1)S(1)} %pad_maximum_fusion.7), channel_id=1, source_target_pairs={{0,3},{1,0},{2,1},{3,2},{4,7},{5,4},{6,5},{7,6},{8,11},{9,8},{10,9... | collective-permute-start | bytes 1966088 | tf_op jit(solution)/shard_map/ppermute | solution.py:21
  135.6 10.5 %collective-permute-done.27 = bf16[64,5120]{1,0:T(8,128)(2,1)S(1)} collective-permute-done((bf16[64,5120]{1,0:T(8,128)(2,1)S(1)}, bf16[64,5120]{1,0:T(8,128)(2,1)S(1)}, u32[]{:S(2)}, u32[]{:S(2)}) %collective-permute-start.27) | collective-permute-done | bytes 655392 | tf_op jit(solution)/shard_map/ppermute | solution.py:21
  146.3 2.5 %collective-permute-start.29 = (bf16[64,5120]{1,0:T(8,128)(2,1)S(1)}, bf16[64,5120]{1,0:T(8,128)(2,1)S(1)}, u32[]{:S(2)}, u32[]{:S(2)}) collective-permute-start(bf16[64,5120]{1,0:T(8,128)(2,1)S(1)} %fusion.5), channel_id=1, source_target_pairs={{0,4},{4,0},{1,5},{5,1},{2,6},{6,2},{3,7},{7,3},{8,12},{12,8},{9,1... | collective-permute-start | bytes 1966088 | tf_op jit(solution)/shard_map/ppermute | solution.py:21
  148.9 11.3 %collective-permute-done.24 = bf16[64,5120]{1,0:T(8,128)(2,1)S(1)} collective-permute-done((bf16[64,5120]{1,0:T(8,128)(2,1)S(1)}, bf16[64,5120]{1,0:T(8,128)(2,1)S(1)}, u32[]{:S(2)}, u32[]{:S(2)}) %collective-permute-start.24) | collective-permute-done | bytes 655392 | tf_op jit(solution)/shard_map/ppermute | solution.py:21
  160.9 19.0 %all_to_all.10 = bf16[16,4,5120]{2,1,0:T(4,128)(2,1)S(1)} all-to-all(bf16[16,4,5120]{2,1,0:T(4,128)(2,1)S(1)} %reshape.43), channel_id=1, replica_groups=mesh['xl'=2,'y'=4,'core'=2,'xh'=2,'z'=4] {'xl','y','core'}, dimensions={0} | all-to-all | bytes 1310720 | tf_op jit(solution)/shard_map/all_to_all | solution.py:206
  180.2 15.1 %all_to_all.11 = bf16[16,4,5120]{2,1,0:T(4,128)(2,1)S(1)} all-to-all(bf16[16,4,5120]{2,1,0:T(4,128)(2,1)S(1)} %reduce-window_convert_fusion), channel_id=1, replica_groups=mesh['xl'=2,'y'=4,'core'=2,'xh'=2,'z'=4] {'xl','y','core'}, dimensions={0} | all-to-all | bytes 1310720 | tf_op jit(solution)/shard_map/all_to_all | solution.py:208
  195.3 1.2 add_bitcast_fusion
  (105 shorter events, 7.1 us)
Async XLA Ops:
  0.7 2.0 %copy-start = (f32[50,3,5120]{2,0,1:T(8,128)S(1)}, f32[50,3,5120]{2,0,1:T(8,128)}, u32[]{:S(2)}) copy-start(f32[50,3,5120]{2,0,1:T(8,128)} %param.11) | copy-start | bytes 9216004
  2.6 1.3 copy-start.1
  3.9 0.7 copy-start.2
  4.6 3.0 %copy-start.4 = (bf16[3,320,640]{2,1,0:T(8,128)(2,1)S(1)}, bf16[3,320,640]{2,1,0:T(8,128)(2,1)}, u32[]{:S(2)}) copy-start(bf16[3,320,640]{2,1,0:T(8,128)(2,1)} %param.12) | copy-start | bytes 3686404
  6.1 5.7 %collective-permute-start = (bf16[64,2560]{1,0:T(8,128)(2,1)S(1)}, bf16[64,2560]{1,0:T(8,128)(2,1)S(1)}, u32[]{:S(2)}, u32[]{:S(2)}) collective-permute-start(bf16[64,2560]{1,0:T(8,128)(2,1)S(1)} %get-tuple-element.22), channel_id=1, source_target_pairs={{0,8},{8,0},{1,9},{9,1},{2,10},{10,2},{3,11},{11,3},{4,12},{12,4},... | collective-permute-start | bytes 983048 | tf_op jit(solution)/shard_map/ppermute | solution.py:21
  7.6 30.1 %collective-permute-start.13 = (bf16[3,320,640]{2,1,0:T(8,128)(2,1)S(1)}, bf16[3,320,640]{2,1,0:T(8,128)(2,1)S(1)}, u32[]{:S(2)}, u32[]{:S(2)}) collective-permute-start(bf16[3,320,640]{2,1,0:T(8,128)(2,1)S(1)} %copy-done.4), channel_id=1, source_target_pairs={{0,16},{16,32},{32,48},{48,0},{1,17},{17,33},{33,49},{49,1},{2,18}... | collective-permute-start | bytes 3686408 | tf_op jit(solution)/shard_map/ppermute | solution.py:21
  9.0 28.7 %collective-permute-start.12 = (bf16[3,320,640]{2,1,0:T(8,128)(2,1)S(1)}, bf16[3,320,640]{2,1,0:T(8,128)(2,1)S(1)}, u32[]{:S(2)}, u32[]{:S(2)}) collective-permute-start(bf16[3,320,640]{2,1,0:T(8,128)(2,1)S(1)} %copy-done.4), channel_id=1, source_target_pairs={{0,48},{16,0},{32,16},{48,32},{1,49},{17,1},{33,17},{49,33},{2,50}... | collective-permute-start | bytes 3686408 | tf_op jit(solution)/shard_map/ppermute | solution.py:21
  10.5 19.4 %collective-permute-start.5 = (bf16[2,320,640]{2,1,0:T(8,128)(2,1)S(1)}, bf16[2,320,640]{2,1,0:T(8,128)(2,1)S(1)}, u32[]{:S(2)}, u32[]{:S(2)}) collective-permute-start(bf16[2,320,640]{2,1,0:T(8,128)(2,1)S(1)} %slice.211), channel_id=1, source_target_pairs={{0,64},{64,0},{1,65},{65,1},{2,66},{66,2},{3,67},{67,3},{4,68},{68... | collective-permute-start | bytes 2457608 | tf_op jit(solution)/shard_map/ppermute | solution.py:21
  11.8 20.8 %collective-permute-start.1 = (bf16[2,64,2560]{2,1,0:T(8,128)(2,1)S(1)}, bf16[2,64,2560]{2,1,0:T(8,128)(2,1)S(1)}, u32[]{:S(2)}, u32[]{:S(2)}) collective-permute-start(bf16[2,64,2560]{2,1,0:T(8,128)(2,1)S(1)} %pad_maximum_fusion.5), channel_id=1, source_target_pairs={{0,3},{1,0},{2,1},{3,2},{4,7},{5,4},{6,5},{7,6},{8,11},{9,8},{10,9... | collective-permute-start | bytes 1966088 | tf_op jit(solution)/shard_map/ppermute | solution.py:21
  15.7 20.8 %collective-permute-start.3 = (bf16[2,64,2560]{2,1,0:T(8,128)(2,1)S(1)}, bf16[2,64,2560]{2,1,0:T(8,128)(2,1)S(1)}, u32[]{:S(2)}, u32[]{:S(2)}) collective-permute-start(bf16[2,64,2560]{2,1,0:T(8,128)(2,1)S(1)} %pad_maximum_fusion.5), channel_id=1, source_target_pairs={{0,1},{1,2},{2,3},{3,0},{4,5},{5,6},{6,7},{7,4},{8,9},{9,10},{10,1... | collective-permute-start | bytes 1966088 | tf_op jit(solution)/shard_map/ppermute | solution.py:21
  29.8 16.4 %collective-permute-start.6 = (bf16[2,64,2560]{2,1,0:T(8,128)(2,1)S(1)}, bf16[2,64,2560]{2,1,0:T(8,128)(2,1)S(1)}, u32[]{:S(2)}, u32[]{:S(2)}) collective-permute-start(bf16[2,64,2560]{2,1,0:T(8,128)(2,1)S(1)} %pad_maximum_fusion.5), channel_id=1, source_target_pairs={{0,4},{4,0},{1,5},{5,1},{2,6},{6,2},{3,7},{7,3},{8,12},{12,8},{9,1... | collective-permute-start | bytes 1966088 | tf_op jit(solution)/shard_map/ppermute | solution.py:21
  32.7 14.6 %collective-permute-start.2 = (bf16[2,32,2560]{2,1,0:T(8,128)(2,1)S(1)}, bf16[2,32,2560]{2,1,0:T(8,128)(2,1)S(1)}, u32[]{:S(2)}, u32[]{:S(2)}) collective-permute-start(bf16[2,32,2560]{2,1,0:T(8,128)(2,1)S(1)} %slice.268), channel_id=1, source_target_pairs={{0,3},{1,0},{2,1},{3,2},{4,7},{5,4},{6,5},{7,6},{8,11},{9,8},{10,9... | collective-permute-start | bytes 983048 | tf_op jit(solution)/shard_map/ppermute | solution.py:21
  36.5 10.8 %collective-permute-start.4 = (bf16[2,32,2560]{2,1,0:T(8,128)(2,1)S(1)}, bf16[2,32,2560]{2,1,0:T(8,128)(2,1)S(1)}, u32[]{:S(2)}, u32[]{:S(2)}) collective-permute-start(bf16[2,32,2560]{2,1,0:T(8,128)(2,1)S(1)} %slice.269), channel_id=1, source_target_pairs={{0,1},{1,2},{2,3},{3,0},{4,5},{5,6},{6,7},{7,4},{8,9},{9,10},{10,1... | collective-permute-start | bytes 983048 | tf_op jit(solution)/shard_map/ppermute | solution.py:21
  37.9 28.2 %collective-permute-start.14 = (bf16[800,640]{1,0:T(8,128)(2,1)S(1)}, bf16[800,640]{1,0:T(8,128)(2,1)S(1)}, u32[]{:S(2)}, u32[]{:S(2)}) collective-permute-start(bf16[800,640]{1,0:T(8,128)(2,1)S(1)} %get-tuple-element.28), channel_id=1, source_target_pairs={{0,48},{16,0},{32,16},{48,32},{1,49},{17,1},{33,17},{49,33},{2,50}... | collective-permute-start | bytes 3072008 | tf_op jit(solution)/shard_map/ppermute | solution.py:21
  40.3 27.5 %collective-permute-start.15 = (bf16[800,640]{1,0:T(8,128)(2,1)S(1)}, bf16[800,640]{1,0:T(8,128)(2,1)S(1)}, u32[]{:S(2)}, u32[]{:S(2)}) collective-permute-start(bf16[800,640]{1,0:T(8,128)(2,1)S(1)} %get-tuple-element.29), channel_id=1, source_target_pairs={{0,16},{16,32},{32,48},{48,0},{1,17},{17,33},{33,49},{49,1},{2,18}... | collective-permute-start | bytes 3072008 | tf_op jit(solution)/shard_map/ppermute | solution.py:21
  46.2 8.7 %collective-permute-start.8 = (bf16[320,640]{1,0:T(8,128)(2,1)S(1)}, bf16[320,640]{1,0:T(8,128)(2,1)S(1)}, u32[]{:S(2)}, u32[]{:S(2)}) collective-permute-start(bf16[320,640]{1,0:T(8,128)(2,1)S(1)} %slice_bitcast_fusion.12), channel_id=1, source_target_pairs={{0,64},{64,0},{1,65},{65,1},{2,66},{66,2},{3,67},{67,3},{4,68},{68... | collective-permute-start | bytes 1228808 | tf_op jit(solution)/shard_map/ppermute | solution.py:21
  47.3 15.2 %collective-permute-start.7 = (bf16[2,64,2560]{2,1,0:T(8,128)(2,1)S(1)}, bf16[2,64,2560]{2,1,0:T(8,128)(2,1)S(1)}, u32[]{:S(2)}, u32[]{:S(2)}) collective-permute-start(bf16[2,64,2560]{2,1,0:T(8,128)(2,1)S(1)} %collective-permute-done.6), channel_id=1, source_target_pairs={{0,3},{1,0},{2,1},{3,2},{4,7},{5,4},{6,5},{7,6},{8,11},{9,8},{10,9... | collective-permute-start | bytes 1966088 | tf_op jit(solution)/shard_map/ppermute | solution.py:21
  51.1 14.9 %collective-permute-start.10 = (bf16[2,64,2560]{2,1,0:T(8,128)(2,1)S(1)}, bf16[2,64,2560]{2,1,0:T(8,128)(2,1)S(1)}, u32[]{:S(2)}, u32[]{:S(2)}) collective-permute-start(bf16[2,64,2560]{2,1,0:T(8,128)(2,1)S(1)} %collective-permute-done.6), channel_id=1, source_target_pairs={{0,1},{1,2},{2,3},{3,0},{4,5},{5,6},{6,7},{7,4},{8,9},{9,10},{10,1... | collective-permute-start | bytes 1966088 | tf_op jit(solution)/shard_map/ppermute | solution.py:21
  54.9 18.7 %collective-permute-start.20 = (bf16[2,320,640]{2,1,0:T(8,128)(2,1)S(1)}, bf16[2,320,640]{2,1,0:T(8,128)(2,1)S(1)}, u32[]{:S(2)}, u32[]{:S(2)}) collective-permute-start(bf16[2,320,640]{2,1,0:T(8,128)(2,1)S(1)} %pad_maximum_fusion.4), channel_id=1, source_target_pairs={{0,64},{64,0},{1,65},{65,1},{2,66},{66,2},{3,67},{67,3},{4,68},{68... | collective-permute-start | bytes 2457608 | tf_op jit(solution)/shard_map/ppermute | solution.py:21
  62.5 7.5 %collective-permute-start.9 = (bf16[2,32,2560]{2,1,0:T(8,128)(2,1)S(1)}, bf16[2,32,2560]{2,1,0:T(8,128)(2,1)S(1)}, u32[]{:S(2)}, u32[]{:S(2)}) collective-permute-start(bf16[2,32,2560]{2,1,0:T(8,128)(2,1)S(1)} %slice.270), channel_id=1, source_target_pairs={{0,3},{1,0},{2,1},{3,2},{4,7},{5,4},{6,5},{7,6},{8,11},{9,8},{10,9... | collective-permute-start | bytes 983048 | tf_op jit(solution)/shard_map/ppermute | solution.py:21
  66.0 7.2 %collective-permute-start.11 = (bf16[2,32,2560]{2,1,0:T(8,128)(2,1)S(1)}, bf16[2,32,2560]{2,1,0:T(8,128)(2,1)S(1)}, u32[]{:S(2)}, u32[]{:S(2)}) collective-permute-start(bf16[2,32,2560]{2,1,0:T(8,128)(2,1)S(1)} %slice.271), channel_id=1, source_target_pairs={{0,1},{1,2},{2,3},{3,0},{4,5},{5,6},{6,7},{7,4},{8,9},{9,10},{10,1... | collective-permute-start | bytes 983048 | tf_op jit(solution)/shard_map/ppermute | solution.py:21
  66.4 16.0 %collective-permute-start.16 = (bf16[4,160,640]{2,1,0:T(8,128)(2,1)S(1)}, bf16[4,160,640]{2,1,0:T(8,128)(2,1)S(1)}, u32[]{:S(2)}, u32[]{:S(2)}) collective-permute-start(bf16[4,160,640]{2,1,0:T(8,128)(2,1)S(1)} %pad_maximum_fusion.2), channel_id=1, source_target_pairs={{0,48},{16,0},{32,16},{48,32},{1,49},{17,1},{33,17},{49,33},{2,50}... | collective-permute-start | bytes 2457608 | tf_op jit(solution)/shard_map/ppermute | solution.py:21
  68.0 16.8 %collective-permute-start.17 = (bf16[4,160,640]{2,1,0:T(8,128)(2,1)S(1)}, bf16[4,160,640]{2,1,0:T(8,128)(2,1)S(1)}, u32[]{:S(2)}, u32[]{:S(2)}) collective-permute-start(bf16[4,160,640]{2,1,0:T(8,128)(2,1)S(1)} %pad_maximum_fusion.3), channel_id=1, source_target_pairs={{0,16},{16,32},{32,48},{48,0},{1,17},{17,33},{33,49},{49,1},{2,18}... | collective-permute-start | bytes 2457608 | tf_op jit(solution)/shard_map/ppermute | solution.py:21
  74.2 18.9 %collective-permute-start.21 = (bf16[320,640]{1,0:T(8,128)(2,1)S(1)}, bf16[320,640]{1,0:T(8,128)(2,1)S(1)}, u32[]{:S(2)}, u32[]{:S(2)}) collective-permute-start(bf16[320,640]{1,0:T(8,128)(2,1)S(1)} %pad_maximum_fusion.10), channel_id=1, source_target_pairs={{0,64},{64,0},{1,65},{65,1},{2,66},{66,2},{3,67},{67,3},{4,68},{68... | collective-permute-start | bytes 1228808 | tf_op jit(solution)/shard_map/ppermute | solution.py:21
  86.4 6.6 %copy-start.3 = (f32[1024,640]{1,0:T(8,128)}, f32[1024,640]{1,0:T(8,128)S(1)}, u32[]{:S(2)}) copy-start(f32[1024,640]{1,0:T(8,128)S(1)} %convolution_add_fusion.ka) | copy-start | bytes 7864324
  86.5 13.4 %collective-permute-start.19 = (bf16[512,640]{1,0:T(8,128)(2,1)S(1)}, bf16[512,640]{1,0:T(8,128)(2,1)S(1)}, u32[]{:S(2)}, u32[]{:S(2)}) collective-permute-start(bf16[512,640]{1,0:T(8,128)(2,1)S(1)} %slice.418), channel_id=1, source_target_pairs={{0,8},{8,0},{1,9},{9,1},{2,10},{10,2},{3,11},{11,3},{4,12},{12,4},... | collective-permute-start | bytes 1966088 | tf_op jit(solution)/shard_map/ppermute | solution.py:21
  93.0 14.5 %slice-start = ((s8[6553600]{0:T(1024)(128)(4,1)}), s8[4194304]{0:T(1024)(128)(4,1)S(1)}, s32[]{:S(2)}) async-start(s8[6553600]{0:T(1024)(128)(4,1)} %bitcast.98), calls=%async_computation.2 | async-start | bytes 8388608
  93.1 6.8 %collective-permute-start.18 = (bf16[512,640]{1,0:T(8,128)(2,1)S(1)}, bf16[512,640]{1,0:T(8,128)(2,1)S(1)}, u32[]{:S(2)}, u32[]{:S(2)}) collective-permute-start(bf16[512,640]{1,0:T(8,128)(2,1)S(1)} %slice.419), channel_id=1, source_target_pairs={{0,8},{8,0},{1,9},{9,1},{2,10},{10,2},{3,11},{11,3},{4,12},{12,4},... | collective-permute-start | bytes 1966088 | tf_op jit(solution)/shard_map/ppermute | solution.py:21
  93.2 14.3 %slice-start.1 = ((s8[6553600]{0:T(1024)(128)(4,1)}), s8[2359296]{0:T(1024)(128)(4,1)S(1)}, s32[]{:S(2)}) async-start(s8[6553600]{0:T(1024)(128)(4,1)} %bitcast.98), calls=%async_computation.3 | async-start | bytes 4718592
  97.5 1.5 copy-start.5
  99.1 2.5 %collective-permute-start.22 = (bf16[512,640]{1,0:T(8,128)(2,1)S(1)}, bf16[512,640]{1,0:T(8,128)(2,1)S(1)}, u32[]{:S(2)}, u32[]{:S(2)}) collective-permute-start(bf16[512,640]{1,0:T(8,128)(2,1)S(1)} %slice.417), channel_id=1, source_target_pairs={{0,8},{8,0},{1,9},{9,1},{2,10},{10,2},{3,11},{11,3},{4,12},{12,4},... | collective-permute-start | bytes 1966088 | tf_op jit(solution)/shard_map/ppermute | solution.py:21
  112.2 17.2 %collective-permute-start.23 = (bf16[2,64,2560]{2,1,0:T(8,128)(2,1)S(1)}, bf16[2,64,2560]{2,1,0:T(8,128)(2,1)S(1)}, u32[]{:S(2)}, u32[]{:S(2)}) collective-permute-start(bf16[2,64,2560]{2,1,0:T(8,128)(2,1)S(1)} %get-tuple-element.49), channel_id=1, source_target_pairs={{0,1},{1,2},{2,3},{3,0},{4,5},{5,6},{6,7},{7,4},{8,9},{9,10},{10,1... | collective-permute-start | bytes 1966088 | tf_op jit(solution)/shard_map/ppermute | solution.py:21
  112.3 17.1 %collective-permute-start.25 = (bf16[2,64,2560]{2,1,0:T(8,128)(2,1)S(1)}, bf16[2,64,2560]{2,1,0:T(8,128)(2,1)S(1)}, u32[]{:S(2)}, u32[]{:S(2)}) collective-permute-start(bf16[2,64,2560]{2,1,0:T(8,128)(2,1)S(1)} %get-tuple-element.50), channel_id=1, source_target_pairs={{0,3},{1,0},{2,1},{3,2},{4,7},{5,4},{6,5},{7,6},{8,11},{9,8},{10,9... | collective-permute-start | bytes 1966088 | tf_op jit(solution)/shard_map/ppermute | solution.py:21
  129.8 16.3 %collective-permute-start.27 = (bf16[64,5120]{1,0:T(8,128)(2,1)S(1)}, bf16[64,5120]{1,0:T(8,128)(2,1)S(1)}, u32[]{:S(2)}, u32[]{:S(2)}) collective-permute-start(bf16[64,5120]{1,0:T(8,128)(2,1)S(1)} %pad_maximum_fusion.8), channel_id=1, source_target_pairs={{0,1},{1,2},{2,3},{3,0},{4,5},{5,6},{6,7},{7,4},{8,9},{9,10},{10,1... | collective-permute-start | bytes 1966088 | tf_op jit(solution)/shard_map/ppermute | solution.py:21
  130.8 15.4 %collective-permute-start.28 = (bf16[64,5120]{1,0:T(8,128)(2,1)S(1)}, bf16[64,5120]{1,0:T(8,128)(2,1)S(1)}, u32[]{:S(2)}, u32[]{:S(2)}) collective-permute-start(bf16[64,5120]{1,0:T(8,128)(2,1)S(1)} %pad_maximum_fusion.9), channel_id=1, source_target_pairs={{0,3},{1,0},{2,1},{3,2},{4,7},{5,4},{6,5},{7,6},{8,11},{9,8},{10,9... | collective-permute-start | bytes 1966088 | tf_op jit(solution)/shard_map/ppermute | solution.py:21
  132.7 27.4 %collective-permute-start.24 = (bf16[64,5120]{1,0:T(8,128)(2,1)S(1)}, bf16[64,5120]{1,0:T(8,128)(2,1)S(1)}, u32[]{:S(2)}, u32[]{:S(2)}) collective-permute-start(bf16[64,5120]{1,0:T(8,128)(2,1)S(1)} %pad_maximum_fusion.6), channel_id=1, source_target_pairs={{0,1},{1,2},{2,3},{3,0},{4,5},{5,6},{6,7},{7,4},{8,9},{9,10},{10,1... | collective-permute-start | bytes 1966088 | tf_op jit(solution)/shard_map/ppermute | solution.py:21
  132.9 27.3 %collective-permute-start.26 = (bf16[64,5120]{1,0:T(8,128)(2,1)S(1)}, bf16[64,5120]{1,0:T(8,128)(2,1)S(1)}, u32[]{:S(2)}, u32[]{:S(2)}) collective-permute-start(bf16[64,5120]{1,0:T(8,128)(2,1)S(1)} %pad_maximum_fusion.7), channel_id=1, source_target_pairs={{0,3},{1,0},{2,1},{3,2},{4,7},{5,4},{6,5},{7,6},{8,11},{9,8},{10,9... | collective-permute-start | bytes 1966088 | tf_op jit(solution)/shard_map/ppermute | solution.py:21
  146.3 14.0 %collective-permute-start.29 = (bf16[64,5120]{1,0:T(8,128)(2,1)S(1)}, bf16[64,5120]{1,0:T(8,128)(2,1)S(1)}, u32[]{:S(2)}, u32[]{:S(2)}) collective-permute-start(bf16[64,5120]{1,0:T(8,128)(2,1)S(1)} %fusion.5), channel_id=1, source_target_pairs={{0,4},{4,0},{1,5},{5,1},{2,6},{6,2},{3,7},{7,3},{8,12},{12,8},{9,1... | collective-permute-start | bytes 1966088 | tf_op jit(solution)/shard_map/ppermute | solution.py:21
  179.9 15.4 %copy-start.6 = (f32[64,5120]{1,0:T(8,128)S(1)}, f32[64,5120]{1,0:T(8,128)}, u32[]{:S(2)}) copy-start(f32[64,5120]{1,0:T(8,128)} %param.8) | copy-start | bytes 3932164

commit v3 on v2

v3 whole, which is shorter than its diff:
```python
import functools

import jax
import jax.numpy as jnp
from jax import lax
from jax.experimental import pallas as pl
from jax.experimental.pallas import tpu as pltpu
from jax.sharding import Mesh, PartitionSpec as P

HEAD_DIM = 128
TM = ("xl", "y", "core")
SEQ = ("xh", "z")
F32, BF16 = jnp.float32, jnp.bfloat16
VMEM_BYTES = 60 * 1024 * 1024
ROUND = [0, 1, 3, 2]
BLOCKS = [2, 1, 3, 0]


def send(array, axis, shift):
    size = lax.axis_size(axis)
    return lax.ppermute(array, axis, [(i, (i + shift) % size) for i in range(size)])


def after(array, *others):
    return lax.optimization_barrier((array,) + others)[0]


def add(a, b):
    return (a.astype(F32) + b.astype(F32)).astype(BF16)


def modulate_kernel(rows, t_ref, state_ref, mod_ref, coef_ref, mine_ref, other_ref, gate_ref, scratch):
    state = state_ref[0]
    line = pl.ds(lax.rem(t_ref[0], 8), 1)
    shift_row, scale_row = mod_ref[0, line, :], mod_ref[1, line, :]
    gate_ref[...] = mod_ref[2, line, :] * coef_ref[t_ref[0]]
    center = jnp.mean(state, axis=-1, keepdims=True)
    moved = state - center
    spread = jnp.mean(moved * moved, axis=-1, keepdims=True)
    scratch[...] = moved * lax.rsqrt(spread + 1e-06) * (1.0 + scale_row) + shift_row
    xl, y, core = (lax.axis_index(a) for a in TM)
    ny, wide = 4, 2 * rows
    low = core == 0
    for dxl in range(2):
        for pair in range(ny // 2):
            mine, other = [], []
            for dy in ROUND[2 * pair : 2 * pair + 2]:
                chip = lax.rem(xl + dxl, 2) * ny + lax.rem(y + dy, ny)
                block = scratch[:, pl.ds(pl.multiple_of(chip * wide, 128), wide)]
                first, second = block[:, :rows], block[:, rows:]
                mine.append(jnp.where(low, first, second))
                other.append(jnp.where(low, second, first))
            place = dxl * ny // 2 + pair
            here = slice(place * wide, (place + 1) * wide)
            mine_ref[:, here] = jnp.concatenate(mine, axis=1).astype(BF16)
            other_ref[:, here] = jnp.concatenate(other, axis=1).astype(BF16)


def modulate(states, t_index, mod_table, coef, rows):
    _, tokens, width = states.shape
    half = jax.ShapeDtypeStruct((tokens, width // 2), BF16)
    return pl.pallas_call(
        functools.partial(modulate_kernel, rows),
        out_shape=(half, half, jax.ShapeDtypeStruct((1, width), F32)),
        grid_spec=pltpu.PrefetchScalarGridSpec(
            num_scalar_prefetch=1,
            grid=(1,),
            in_specs=[
                pl.BlockSpec((1, tokens, width), lambda i, t: (0, 0, 0)),
                pl.BlockSpec((3, 8, width), lambda i, t: (0, t[0] // 8, 0)),
                pl.BlockSpec(memory_space=pltpu.SMEM),
            ],
            out_specs=[
                pl.BlockSpec((tokens, width // 2), lambda i, t: (0, 0)),
                pl.BlockSpec((tokens, width // 2), lambda i, t: (0, 0)),
                pl.BlockSpec((1, width), lambda i, t: (0, 0)),
            ],
            scratch_shapes=[pltpu.VMEM((tokens, width), F32)],
        ),
        compiler_params=pltpu.CompilerParams(vmem_limit_bytes=VMEM_BYTES),
        cost_estimate=pl.CostEstimate(flops=1000, bytes_accessed=1000, transcendentals=0),
    )(t_index, states, jnp.transpose(mod_table, (1, 0, 2)), coef)


def normed(x):
    return (x * lax.rsqrt(jnp.mean(x * x, axis=-1, keepdims=True) + 1e-06)).astype(BF16)


def attend(query, keys, values):
    scores = lax.dot_general(query, keys, (((1,), (1,)), ((), ())), preferred_element_type=F32)
    expo = jnp.exp(scores * HEAD_DIM ** (-0.5))
    total = jnp.sum(expo, axis=-1, keepdims=True)
    return (
        jnp.dot(expo.astype(BF16), values, preferred_element_type=F32) * (1.0 / total)
    ).astype(BF16)


def first_kernel(head, q0, q1, qb, k0, k1, kb, v0, v1, vb, query_ref, keys_ref, values_ref, out_ref):
    half = q0.shape[0]
    for dx, (q, k, v) in enumerate(((q0, k0, v0), (q1, k1, v1))):
        rows = slice(dx * half, (dx + 1) * half)
        query_ref[rows] = normed(q[...] + qb[rows].astype(F32))
        keys_ref[rows] = normed(k[...] + kb[rows].astype(F32))
        values_ref[rows] = (v[...] + vb[rows].astype(F32)).astype(BF16)
    out_ref[...] = attend(query_ref[half : half + head], keys_ref[...], values_ref[...])


def second_kernel(head, query_ref, keys_ref, values_ref, out_ref):
    half = query_ref.shape[0] // 2
    query = jnp.concatenate([query_ref[:half], query_ref[half + head :]], axis=0)
    out_ref[...] = attend(query, keys_ref[...], values_ref[...])


def attention_call(kernel, operands, heights, shapes):
    count, width = operands[-1].shape

    def spec(rows):
        return pl.BlockSpec((rows, HEAD_DIM), lambda h: (0, h))

    return pl.pallas_call(
        kernel,
        out_shape=[jax.ShapeDtypeStruct((rows, width), BF16) for rows in shapes],
        grid=(width // HEAD_DIM,),
        in_specs=[spec(rows) for rows in heights],
        out_specs=[spec(rows) for rows in shapes],
        compiler_params=pltpu.CompilerParams(vmem_limit_bytes=16 * 1024 * 1024),
        cost_estimate=pl.CostEstimate(
            flops=4 * shapes[-1] * count * width, bytes_accessed=8 * count * width, transcendentals=0
        ),
    )(*operands)


def on_device(states, start, t_index, coef, mod_table, wqkv, wo):
    tokens, width = states.shape[1:]
    rows = wqkv.shape[1]
    half, short = rows // 2, tokens // 2

    own = wqkv
    a1, b1 = send(own, "y", -1), send(own, "y", 1)
    p = send(own[:2], "xl", 1)

    mine, other, gate_row = modulate(states, t_index, mod_table, coef, rows)
    pair = jnp.stack([mine, send(other, "core", 1)])

    za, zb = send(pair, "z", -1), send(pair, "z", 1)
    across = send(after(pair, p), "xh", 1)
    zfa = send(after(za[:, :short], zb), "z", -1)
    zfb = send(after(zb[:, short:], za), "z", 1)

    xv = send(after(jnp.stack([own[2], a1[2], b1[2]]), across), "xl", 1)
    fa = send(after(a1[:, :half], b1), "y", -1)
    fb = send(after(b1[:, half:], a1), "y", 1)
    far = jnp.concatenate([fa, fb], axis=1)

    distant = after(across, zfa, zfb)
    xa, xb = send(distant, "z", -1), send(distant, "z", 1)
    xfa = send(after(xa[:, :short], xb), "z", -1)
    xfb = send(after(xb[:, short:], xa), "z", 1)

    near = after(p, fa, fb)
    pa, pb = send(near, "y", -1), send(near, "y", 1)
    xvf = send(after(far[2], xv), "xl", 1)
    pfa = send(after(pa[:, :half], pb), "y", -1)
    pfb = send(after(pb[:, half:], pa), "y", 1)
    pfar = jnp.concatenate([pfa, pfb], axis=1)

    features = []
    for near, above, below, ends in ((pair, za, zb, (zfa, zfb)), (across, xa, xb, (xfa, xfb))):
        rowed = jnp.concatenate([*ends, above, below, near], axis=1)
        features.append(rowed.reshape(2 * rowed.shape[1], -1))
    count = features[0].shape[0]

    def product(begin, weights):
        stop = begin + weights[0].shape[0]
        return [
            [jnp.dot(f[:, begin:stop], w, preferred_element_type=F32) for w in weights]
            for f in features
        ]

    def plus(sofar, more):
        return [[a + b for a, b in zip(x, y)] for x, y in zip(sofar, more)]

    stacked = [
        [jnp.concatenate(blocks, axis=0) for blocks in stage]
        for stage in (
            [[own[j], a1[j], b1[j], far[j]] for j in range(3)],
            [[p[0], pa[0]], [p[1], pa[1]], [xv[0], xv[1]]],
            [[pb[0], pfar[0]], [pb[1], pfar[1]], [xv[2], xvf]],
        )
    ]
    features[1] = after(features[1], pa, pb)
    stacked[1] = [after(w, xv) for w in stacked[1]]
    begun = [lax.optimization_barrier(x) for x in product(0, stacked[0])]
    begun = [lax.optimization_barrier(x) for x in plus(begun, product(4 * rows, stacked[1]))]
    begun = plus(begun, product(6 * rows, stacked[2]))
    parts = []
    for j in range(3):
        mates = jnp.concatenate([x[j][count // 2 :] for x in begun], axis=0).astype(BF16)
        parts += [begun[0][j], begun[1][j], send(mates, "core", 1)]

    cut, half, head = width // 2, count // 2, 3 * tokens
    query, keys, values, attended = attention_call(
        functools.partial(first_kernel, head), parts, (half, half, count) * 3,
        (count, count, count, head),
    )
    first = jnp.dot(attended, wo, preferred_element_type=F32).astype(BF16)
    far1, above1, below1 = (first[i * tokens : (i + 1) * tokens] for i in range(3))
    joins = [send(far1[:, :cut], "xh", 1), send(far1[:, cut:], "xh", 1)]
    up1, down1 = send(above1, "z", 1), send(below1, "z", -1)
    (attended,) = attention_call(
        functools.partial(second_kernel, head), (after(query, joins[0]), keys, values),
        (count,) * 3, (count - head,),
    )
    rest = jnp.dot(attended, wo, preferred_element_type=F32)
    far0, above0, below0, near0, near1 = (rest[i * tokens : (i + 1) * tokens] for i in range(5))
    free = send(above0[:, cut:].astype(BF16), "z", 1), send(below0[:, :cut].astype(BF16), "z", -1)
    up = send((far0[:, :cut] + joins[0].astype(F32)).astype(BF16), "z", 1)
    down = send((far0[:, cut:] + joins[1].astype(F32)).astype(BF16), "z", -1)
    there = send((near1 + up1.astype(F32) + down1.astype(F32)).astype(BF16), "xh", 1)
    bound = (
        send((above0[:, :cut] + up.astype(F32)).astype(BF16), "z", 1),
        send((below0[:, cut:] + down.astype(F32)).astype(BF16), "z", -1),
    )
    output = (
        near0
        + jnp.concatenate([bound[0], free[0]], axis=1).astype(F32)
        + jnp.concatenate([free[1], bound[1]], axis=1).astype(F32)
        + there.astype(F32)
    )
    term = (gate_row * output).astype(BF16)
    steps = lax.axis_size(TM)
    by_step = lax.all_to_all(term.reshape(steps, tokens // steps, width), TM, 0, 0)
    total = jnp.cumsum(by_step.astype(F32), axis=0).astype(BF16)
    total = lax.all_to_all(total, TM, 0, 0).reshape(tokens, width)
    return (start + total.astype(F32))[None]


def solution(mesh):
    wide = Mesh(mesh.devices.reshape(2, 4, 2, 2, 4), TM + SEQ)
    placed = (
        P(TM, SEQ, None),
        P(SEQ, None),
        P(TM),
        P(),
        P(),
        P(None, TM, SEQ),
        P(SEQ, None),
    )
    return jax.shard_map(
        on_device, mesh=wide, in_specs=placed, out_specs=P(TM, SEQ, None), check_vma=False
    )
```

time: 197 us -> 184 us (0.934)
  waiting for transfers between devices: 77.1 us -> 56.2 us
  starting transfers between devices: 46.8 us -> 57.2 us
  local copies, waits for them, and re-layouts: 8.74 us -> 2.54 us
  matrix products: 18 us -> 20.5 us
  Pallas kernels: 7.32 us -> 9.65 us
    ppermute x30 -> x35, waiting for transfers between devices: 77.1 us -> 56.2 us  [send(): lax.ppermute(array, axis, [(i, (i + shift) % size) for i in range(size)])]
    ppermute x30 -> x35, starting transfers between devices: 46.8 us -> 57.2 us  [send(): lax.ppermute(array, axis, [(i, (i + shift) % size) for i in range(size)])]
    unnamed x35 -> x22, local copies, waits for them, and re-layouts: 6.74 us -> 0.39 us
    dot_general x7 -> x20, matrix products: 18 us -> 20.5 us  [the longest x18 16 us: product(): jnp.dot(f[:, begin:stop], w, preferred_element_type=F32)]
    pallas_call x1 -> x2, Pallas kernels: 5.86 us -> 6.36 us  [attention_call(): pl.pallas_call(kernel, out_shape=[jax.ShapeDtypeStruct((rows, width), BF1...]
  transfers between devices with their start and end apart: 30 -> 35, of which waited for: 14 -> 17; matrix products, arithmetic and copies ran while one was open for 9% -> 12% of each run, Pallas kernels for 0% -> 1%
where the time goes in v3:
time: 184 us
  starting transfers between devices  57.2 us (31%)
  waiting for transfers between devices  56.2 us (31%)
  blocking collectives  33.3 us (18%)
  matrix products  20.5 us (11%)
  Pallas kernels  9.65 us (5%)
  other arithmetic  2.95 us (2%)
  local copies, waits for them, and re-layouts  2.54 us (1%)
    ppermute x35, starting transfers between devices, send(): lax.ppermute(array, axis, [(i, (i + shift) % size) for i in range(size)])  57.2 us
    ppermute x35, waiting for transfers between devices, send(): lax.ppermute(array, axis, [(i, (i + shift) % size) for i in range(size)])  56.2 us
    all_to_all x1, blocking collectives, on_device(): lax.all_to_all(term.reshape(steps, tokens // steps, width), TM, 0, 0)  18.2 us
    dot_general x18, matrix products, product(): jnp.dot(f[:, begin:stop], w, preferred_element_type=F32)  16 us
    all_to_all x1, blocking collectives, on_device(): total = lax.all_to_all(total, TM, 0, 0).reshape(tokens, width)  15.1 us
    pallas_call x2, Pallas kernels, attention_call(): pl.pallas_call(kernel, out_shape=[jax.ShapeDtypeStruct((rows, width), BF1...  6.36 us
  transfers between devices with their start and end apart: 35, of which 17 were waited for; matrix products, arithmetic and copies ran while one was open for 12% of the time, Pallas kernels for 1%

profile of v3, /device:TPU:1, one launch (start us, length us, event | category | flops | bytes accessed | tf_op | source)
XLA Modules:
  0.0 183.6 jit_solution(2485609218060427536)
XLA Ops:
  0.7 3.3 %shard_map.73 = (bf16[64,2560]{1,0:T(8,128)(2,1)}, bf16[64,2560]{1,0:T(8,128)(2,1)}, f32[1,5120]{1,0:T(1,128)}) custom-call(s32[1]{0:T(128)S(6)} %copy.18.t_ref, f32[1,64,5120]{2,1,0:T(8,128)} %state_ref.1, f32[3,50,5120]{2,1,0:T(8,128)} %bitcast.84, f32[50]{0:T(128)} %coef_ref.1), custom_call_target="tpu_custom_call" | custom-call | flops 1000 | bytes 1000 | tf_op jit(solution)/shard_map/pallas_call | solution.py:62
  4.0 1.4 collective-permute-start
  5.4 2.8 %collective-permute-start.5 = (bf16[3,320,640]{2,1,0:T(8,128)(2,1)S(1)}, bf16[3,320,640]{2,1,0:T(8,128)(2,1)S(1)}, u32[]{:S(2)}, u32[]{:S(2)}) collective-permute-start(bf16[3,320,640]{2,1,0:T(8,128)(2,1)S(1)} %copy-done), channel_id=1, source_target_pairs={{0,48},{16,0},{32,16},{48,32},{1,49},{17,1},{33,17},{49,33},{2,50}... | collective-permute-start | bytes 3686408 | tf_op jit(solution)/shard_map/ppermute | solution.py:21
  8.3 1.3 collective-permute-start.9
  9.7 1.7 collective-permute-start.2
  11.4 2.2 %collective-permute-start.1 = (bf16[2,64,2560]{2,1,0:T(8,128)(2,1)S(1)}, bf16[2,64,2560]{2,1,0:T(8,128)(2,1)S(1)}, u32[]{:S(2)}, u32[]{:S(2)}) collective-permute-start(bf16[2,64,2560]{2,1,0:T(8,128)(2,1)S(1)} %pad_maximum_fusion.10), channel_id=1, source_target_pairs={{0,3},{1,0},{2,1},{3,2},{4,7},{5,4},{6,5},{7,6},{8,11},{9,8},{10,9... | collective-permute-start | bytes 1966088 | tf_op jit(solution)/shard_map/ppermute | solution.py:21
  13.7 14.2 %collective-permute-done.9 = bf16[2,320,640]{2,1,0:T(8,128)(2,1)S(1)} collective-permute-done((bf16[2,320,640]{2,1,0:T(8,128)(2,1)S(1)}, bf16[2,320,640]{2,1,0:T(8,128)(2,1)S(1)}, u32[]{:S(2)}, u32[]{:S(2)}) %collective-permute-start.9) | collective-permute-done | bytes 819232 | tf_op jit(solution)/shard_map/ppermute | solution.py:21
  27.9 2.7 %collective-permute-start.11 = (bf16[2,64,2560]{2,1,0:T(8,128)(2,1)S(1)}, bf16[2,64,2560]{2,1,0:T(8,128)(2,1)S(1)}, u32[]{:S(2)}, u32[]{:S(2)}) collective-permute-start(bf16[2,64,2560]{2,1,0:T(8,128)(2,1)S(1)} %pad_maximum_fusion.10), channel_id=1, source_target_pairs={{0,4},{4,0},{1,5},{5,1},{2,6},{6,2},{3,7},{7,3},{8,12},{12,8},{9,1... | collective-permute-start | bytes 1966088 | tf_op jit(solution)/shard_map/ppermute | solution.py:21
  30.8 3.8 %collective-permute-start.3 = (bf16[2,32,2560]{2,1,0:T(8,128)(2,1)S(1)}, bf16[2,32,2560]{2,1,0:T(8,128)(2,1)S(1)}, u32[]{:S(2)}, u32[]{:S(2)}) collective-permute-start(bf16[2,32,2560]{2,1,0:T(8,128)(2,1)S(1)} %slice.260), channel_id=1, source_target_pairs={{0,3},{1,0},{2,1},{3,2},{4,7},{5,4},{6,5},{7,6},{8,11},{9,8},{10,9... | collective-permute-start | bytes 983048 | tf_op jit(solution)/shard_map/ppermute | solution.py:21
  34.6 3.0 %collective-permute-done.6 = bf16[3,320,640]{2,1,0:T(8,128)(2,1)S(1)} collective-permute-done((bf16[3,320,640]{2,1,0:T(8,128)(2,1)S(1)}, bf16[3,320,640]{2,1,0:T(8,128)(2,1)S(1)}, u32[]{:S(2)}, u32[]{:S(2)}) %collective-permute-start.6) | collective-permute-done | bytes 1228832 | tf_op jit(solution)/shard_map/ppermute | solution.py:21
  37.8 2.7 %collective-permute-start.7 = (bf16[3,160,640]{2,1,0:T(8,128)(2,1)S(1)}, bf16[3,160,640]{2,1,0:T(8,128)(2,1)S(1)}, u32[]{:S(2)}, u32[]{:S(2)}) collective-permute-start(bf16[3,160,640]{2,1,0:T(8,128)(2,1)S(1)} %slice.265), channel_id=1, source_target_pairs={{0,48},{16,0},{32,16},{48,32},{1,49},{17,1},{33,17},{49,33},{2,50}... | collective-permute-start | bytes 1843208 | tf_op jit(solution)/shard_map/ppermute | solution.py:21
  41.0 2.3 %collective-permute-done.4 = bf16[2,32,2560]{2,1,0:T(8,128)(2,1)S(1)} collective-permute-done((bf16[2,32,2560]{2,1,0:T(8,128)(2,1)S(1)}, bf16[2,32,2560]{2,1,0:T(8,128)(2,1)S(1)}, u32[]{:S(2)}, u32[]{:S(2)}) %collective-permute-start.4) | collective-permute-done | bytes 327712 | tf_op jit(solution)/shard_map/ppermute | solution.py:21
  44.4 1.6 collective-permute-start.17
  46.0 2.1 %collective-permute-start.16 = (bf16[2,64,2560]{2,1,0:T(8,128)(2,1)S(1)}, bf16[2,64,2560]{2,1,0:T(8,128)(2,1)S(1)}, u32[]{:S(2)}, u32[]{:S(2)}) collective-permute-start(bf16[2,64,2560]{2,1,0:T(8,128)(2,1)S(1)} %collective-permute-done.11), channel_id=1, source_target_pairs={{0,3},{1,0},{2,1},{3,2},{4,7},{5,4},{6,5},{7,6},{8,11},{9,8},{10,9... | collective-permute-start | bytes 1966088 | tf_op jit(solution)/shard_map/ppermute | solution.py:21
  48.2 1.2 collective-permute-start.12
  49.4 3.8 %collective-permute-done.8 = bf16[3,160,640]{2,1,0:T(8,128)(2,1)S(1)} collective-permute-done((bf16[3,160,640]{2,1,0:T(8,128)(2,1)S(1)}, bf16[3,160,640]{2,1,0:T(8,128)(2,1)S(1)}, u32[]{:S(2)}, u32[]{:S(2)}) %collective-permute-start.8) | collective-permute-done | bytes 614432 | tf_op jit(solution)/shard_map/ppermute | solution.py:21
  53.2 2.7 %collective-permute-start.10 = (bf16[2,320,640]{2,1,0:T(8,128)(2,1)S(1)}, bf16[2,320,640]{2,1,0:T(8,128)(2,1)S(1)}, u32[]{:S(2)}, u32[]{:S(2)}) collective-permute-start(bf16[2,320,640]{2,1,0:T(8,128)(2,1)S(1)} %collective-permute-done.9), channel_id=1, source_target_pairs={{0,48},{16,0},{32,16},{48,32},{1,49},{17,1},{33,17},{49,33},{2,50}... | collective-permute-start | bytes 2457608 | tf_op jit(solution)/shard_map/ppermute | solution.py:21
  58.5 1.7 collective-permute-done.16
  61.1 2.5 %collective-permute-start.18 = (bf16[2,32,2560]{2,1,0:T(8,128)(2,1)S(1)}, bf16[2,32,2560]{2,1,0:T(8,128)(2,1)S(1)}, u32[]{:S(2)}, u32[]{:S(2)}) collective-permute-start(bf16[2,32,2560]{2,1,0:T(8,128)(2,1)S(1)} %slice.286), channel_id=1, source_target_pairs={{0,3},{1,0},{2,1},{3,2},{4,7},{5,4},{6,5},{7,6},{8,11},{9,8},{10,9... | collective-permute-start | bytes 983048 | tf_op jit(solution)/shard_map/ppermute | solution.py:21
  65.1 2.5 %collective-permute-done.18 = bf16[2,32,2560]{2,1,0:T(8,128)(2,1)S(1)} collective-permute-done((bf16[2,32,2560]{2,1,0:T(8,128)(2,1)S(1)}, bf16[2,32,2560]{2,1,0:T(8,128)(2,1)S(1)}, u32[]{:S(2)}, u32[]{:S(2)}) %collective-permute-start.18) | collective-permute-done | bytes 327712 | tf_op jit(solution)/shard_map/ppermute | solution.py:21
  67.7 4.9 %collective-permute-done.19 = bf16[2,32,2560]{2,1,0:T(8,128)(2,1)S(1)} collective-permute-done((bf16[2,32,2560]{2,1,0:T(8,128)(2,1)S(1)}, bf16[2,32,2560]{2,1,0:T(8,128)(2,1)S(1)}, u32[]{:S(2)}, u32[]{:S(2)}) %collective-permute-start.19) | collective-permute-done | bytes 327712 | tf_op jit(solution)/shard_map/ppermute | solution.py:21
  72.7 1.2 fusion.15
  73.9 1.2 fusion.13
  75.2 1.8 collective-permute-start.14
  78.5 1.3 collective-permute-start.22
  88.4 6.0 %collective-permute-start.21 = (bf16[512,640]{1,0:T(8,128)(2,1)S(1)}, bf16[512,640]{1,0:T(8,128)(2,1)S(1)}, u32[]{:S(2)}, u32[]{:S(2)}) collective-permute-start(bf16[512,640]{1,0:T(8,128)(2,1)S(1)} %pad_maximum_fusion.12), channel_id=1, source_target_pairs={{0,8},{8,0},{1,9},{9,1},{2,10},{10,2},{3,11},{11,3},{4,12},{12,4},... | collective-permute-start | bytes 1966088 | tf_op jit(solution)/shard_map/ppermute | solution.py:21
  97.0 1.7 collective-permute-done.23.vb
  98.7 3.7 %shard_map.74 = (bf16[512,640]{1,0:T(8,128)(2,1)S(1)}, bf16[512,640]{1,0:T(8,128)(2,1)S(1)}, bf16[512,640]{1,0:T(8,128)(2,1)S(1)}, bf16[192,640]{1,0:T(8,128)(2,1)S(1)}) custom-call(f32[512,640]{1,0:T(8,128)S(1)} %convolution_add_fusion.8.q0, f32[512,640]{1,0:T(8,128)S(1)} %convolution_add_fusion.4.q1, bf16[512,640]{1,0:T(8,128)(2,1)S(1)} %collective-permute-done.20.qb, ...), custom_call_target="tpu_custom_call" | custom-call | flops 251658240 | bytes 2621440 | tf_op jit(solution)/shard_map/pallas_call | solution.py:120
  102.4 1.7 convolution_convert_fusion
  104.2 2.8 %collective-permute-start.24 = (bf16[64,2560]{1,0:T(8,128)(2,1)S(1)}, bf16[64,2560]{1,0:T(8,128)(2,1)S(1)}, u32[]{:S(2)}, u32[]{:S(2)}) collective-permute-start(bf16[64,2560]{1,0:T(8,128)(2,1)S(1)} %get-tuple-element.84), channel_id=1, source_target_pairs={{0,4},{4,0},{1,5},{5,1},{2,6},{6,2},{3,7},{7,3},{8,12},{12,8},{9,1... | collective-permute-start | bytes 983048 | tf_op jit(solution)/shard_map/ppermute | solution.py:21
  108.2 2.1 %collective-permute-start.33 = (bf16[64,5120]{1,0:T(8,128)(2,1)S(1)}, bf16[64,5120]{1,0:T(8,128)(2,1)S(1)}, u32[]{:S(2)}, u32[]{:S(2)}) collective-permute-start(bf16[64,5120]{1,0:T(8,128)(2,1)S(1)} %get-tuple-element.86), channel_id=1, source_target_pairs={{0,3},{1,0},{2,1},{3,2},{4,7},{5,4},{6,5},{7,6},{8,11},{9,8},{10,9... | collective-permute-start | bytes 1966088 | tf_op jit(solution)/shard_map/ppermute | solution.py:21
  110.4 4.3 %collective-permute-done.24 = bf16[64,2560]{1,0:T(8,128)(2,1)S(1)} collective-permute-done((bf16[64,2560]{1,0:T(8,128)(2,1)S(1)}, bf16[64,2560]{1,0:T(8,128)(2,1)S(1)}, u32[]{:S(2)}, u32[]{:S(2)}) %collective-permute-start.24) | collective-permute-done | bytes 327712 | tf_op jit(solution)/shard_map/ppermute | solution.py:21
  114.7 2.7 %shard_map.75 = bf16[320,640]{1,0:T(8,128)(2,1)S(1)} custom-call(bf16[512,640]{1,0:T(8,128)(2,1)S(1)} %get-tuple-element.76.query_ref, bf16[512,640]{1,0:T(8,128)(2,1)S(1)} %get-tuple-element.77.keys_ref, bf16[512,640]{1,0:T(8,128)(2,1)S(1)} %get-tuple-element.78.values_ref), custom_call_target="tpu_custom_call" | custom-call | flops 419430400 | bytes 2621440 | tf_op jit(solution)/shard_map/pallas_call | solution.py:120
  117.4 2.7 %fusion.53 = (bf16[320,5120]{1,0:T(8,128)(2,1)S(1)}, f32[320,5120]{1,0:T(8,128)S(1)}) fusion(bf16[320,640]{1,0:T(8,128)(2,1)S(1)} %shard_map.75, bf16[640,5120]{1,0:T(8,128)(2,1)S(1)} %bitcast.65), kind=kOutput, calls=%fused_computation.131 | convolution fusion | flops 2098790400 | bytes 16793600 | tf_op jit(solution)/shard_map/dot_general | solution.py:214
  120.1 1.6 collective-permute-done.29
  121.8 3.0 %collective-permute-start.30 = (bf16[64,2560]{1,0:T(8,128)(2,1)S(1)}, bf16[64,2560]{1,0:T(8,128)(2,1)S(1)}, u32[]{:S(2)}, u32[]{:S(2)}) collective-permute-start(bf16[64,2560]{1,0:T(8,128)(2,1)S(1)} %fusion.19), channel_id=1, source_target_pairs={{0,3},{1,0},{2,1},{3,2},{4,7},{5,4},{6,5},{7,6},{8,11},{9,8},{10,9... | collective-permute-start | bytes 983048 | tf_op jit(solution)/shard_map/ppermute | solution.py:21
  125.0 1.3 collective-permute-start.27
  126.4 4.7 %collective-permute-done.30 = bf16[64,2560]{1,0:T(8,128)(2,1)S(1)} collective-permute-done((bf16[64,2560]{1,0:T(8,128)(2,1)S(1)}, bf16[64,2560]{1,0:T(8,128)(2,1)S(1)}, u32[]{:S(2)}, u32[]{:S(2)}) %collective-permute-start.30) | collective-permute-done | bytes 327712 | tf_op jit(solution)/shard_map/ppermute | solution.py:21
  131.2 1.6 collective-permute-start.25
  133.1 2.8 %collective-permute-start.34 = (bf16[64,5120]{1,0:T(8,128)(2,1)S(1)}, bf16[64,5120]{1,0:T(8,128)(2,1)S(1)}, u32[]{:S(2)}, u32[]{:S(2)}) collective-permute-start(bf16[64,5120]{1,0:T(8,128)(2,1)S(1)} %fusion.1), channel_id=1, source_target_pairs={{0,4},{4,0},{1,5},{5,1},{2,6},{6,2},{3,7},{7,3},{8,12},{12,8},{9,1... | collective-permute-start | bytes 1966088 | tf_op jit(solution)/shard_map/ppermute | solution.py:21
  135.9 1.4 collective-permute-start.31
  137.3 1.9 %collective-permute-done.25 = bf16[64,2560]{1,0:T(8,128)(2,1)S(1)} collective-permute-done((bf16[64,2560]{1,0:T(8,128)(2,1)S(1)}, bf16[64,2560]{1,0:T(8,128)(2,1)S(1)}, u32[]{:S(2)}, u32[]{:S(2)}) %collective-permute-start.25) | collective-permute-done | bytes 327712 | tf_op jit(solution)/shard_map/ppermute | solution.py:21
  139.3 1.6 collective-permute-start.26
  140.9 2.5 %collective-permute-done.31 = bf16[64,2560]{1,0:T(8,128)(2,1)S(1)} collective-permute-done((bf16[64,2560]{1,0:T(8,128)(2,1)S(1)}, bf16[64,2560]{1,0:T(8,128)(2,1)S(1)}, u32[]{:S(2)}, u32[]{:S(2)}) %collective-permute-start.31) | collective-permute-done | bytes 327712 | tf_op jit(solution)/shard_map/ppermute | solution.py:21
  143.4 4.8 %collective-permute-done.34 = bf16[64,5120]{1,0:T(8,128)(2,1)S(1)} collective-permute-done((bf16[64,5120]{1,0:T(8,128)(2,1)S(1)}, bf16[64,5120]{1,0:T(8,128)(2,1)S(1)}, u32[]{:S(2)}, u32[]{:S(2)}) %collective-permute-start.34) | collective-permute-done | bytes 655392 | tf_op jit(solution)/shard_map/ppermute | solution.py:21
  148.8 18.2 %all_to_all.10 = bf16[16,4,5120]{2,1,0:T(4,128)(2,1)S(1)} all-to-all(bf16[16,4,5120]{2,1,0:T(4,128)(2,1)S(1)} %reshape.14), channel_id=1, replica_groups=mesh['xl'=2,'y'=4,'core'=2,'xh'=2,'z'=4] {'xl','y','core'}, dimensions={0} | all-to-all | bytes 1310720 | tf_op jit(solution)/shard_map/all_to_all | solution.py:232
  167.3 15.1 %all_to_all.11 = bf16[16,4,5120]{2,1,0:T(4,128)(2,1)S(1)} all-to-all(bf16[16,4,5120]{2,1,0:T(4,128)(2,1)S(1)} %reduce-window_convert_fusion), channel_id=1, replica_groups=mesh['xl'=2,'y'=4,'core'=2,'xh'=2,'z'=4] {'xl','y','core'}, dimensions={0} | all-to-all | bytes 1310720 | tf_op jit(solution)/shard_map/all_to_all | solution.py:234
  182.4 1.2 add_bitcast_fusion
  (117 shorter events, 22.8 us)
Async XLA Ops:
  0.7 4.7 %copy-start = (bf16[3,320,640]{2,1,0:T(8,128)(2,1)S(1)}, bf16[3,320,640]{2,1,0:T(8,128)(2,1)}, u32[]{:S(2)}) copy-start(bf16[3,320,640]{2,1,0:T(8,128)(2,1)} %param.12) | copy-start | bytes 3686404
  4.0 5.6 %copy-start.1 = (bf16[64,2560]{1,0:T(8,128)(2,1)S(1)}, bf16[64,2560]{1,0:T(8,128)(2,1)}, u32[]{:S(2)}) copy-start(bf16[64,2560]{1,0:T(8,128)(2,1)} %get-tuple-element.43) | copy-start | bytes 983044
  4.0 5.6 %collective-permute-start = (bf16[64,2560]{1,0:T(8,128)(2,1)}, bf16[64,2560]{1,0:T(8,128)(2,1)S(1)}, u32[]{:S(2)}, u32[]{:S(2)}) collective-permute-start(bf16[64,2560]{1,0:T(8,128)(2,1)} %get-tuple-element.44), channel_id=1, source_target_pairs={{0,8},{8,0},{1,9},{9,1},{2,10},{10,2},{3,11},{11,3},{4,12},{12,4},... | collective-permute-start | bytes 983048 | tf_op jit(solution)/shard_map/ppermute | solution.py:21
  5.4 29.2 %collective-permute-start.5 = (bf16[3,320,640]{2,1,0:T(8,128)(2,1)S(1)}, bf16[3,320,640]{2,1,0:T(8,128)(2,1)S(1)}, u32[]{:S(2)}, u32[]{:S(2)}) collective-permute-start(bf16[3,320,640]{2,1,0:T(8,128)(2,1)S(1)} %copy-done), channel_id=1, source_target_pairs={{0,48},{16,0},{32,16},{48,32},{1,49},{17,1},{33,17},{49,33},{2,50}... | collective-permute-start | bytes 3686408 | tf_op jit(solution)/shard_map/ppermute | solution.py:21
  8.2 29.5 %collective-permute-start.6 = (bf16[3,320,640]{2,1,0:T(8,128)(2,1)S(1)}, bf16[3,320,640]{2,1,0:T(8,128)(2,1)S(1)}, u32[]{:S(2)}, u32[]{:S(2)}) collective-permute-start(bf16[3,320,640]{2,1,0:T(8,128)(2,1)S(1)} %copy-done), channel_id=1, source_target_pairs={{0,16},{16,32},{32,48},{48,0},{1,17},{17,33},{33,49},{49,1},{2,18}... | collective-permute-start | bytes 3686408 | tf_op jit(solution)/shard_map/ppermute | solution.py:21
  8.3 19.6 %collective-permute-start.9 = (bf16[2,320,640]{2,1,0:T(8,128)(2,1)S(1)}, bf16[2,320,640]{2,1,0:T(8,128)(2,1)S(1)}, u32[]{:S(2)}, u32[]{:S(2)}) collective-permute-start(bf16[2,320,640]{2,1,0:T(8,128)(2,1)S(1)} %slice.222), channel_id=1, source_target_pairs={{0,64},{64,0},{1,65},{65,1},{2,66},{66,2},{3,67},{67,3},{4,68},{68... | collective-permute-start | bytes 2457608 | tf_op jit(solution)/shard_map/ppermute | solution.py:21
  9.7 21.0 %collective-permute-start.2 = (bf16[2,64,2560]{2,1,0:T(8,128)(2,1)S(1)}, bf16[2,64,2560]{2,1,0:T(8,128)(2,1)S(1)}, u32[]{:S(2)}, u32[]{:S(2)}) collective-permute-start(bf16[2,64,2560]{2,1,0:T(8,128)(2,1)S(1)} %pad_maximum_fusion.10), channel_id=1, source_target_pairs={{0,1},{1,2},{2,3},{3,0},{4,5},{5,6},{6,7},{7,4},{8,9},{9,10},{10,1... | collective-permute-start | bytes 1966088 | tf_op jit(solution)/shard_map/ppermute | solution.py:21
  11.4 19.3 %collective-permute-start.1 = (bf16[2,64,2560]{2,1,0:T(8,128)(2,1)S(1)}, bf16[2,64,2560]{2,1,0:T(8,128)(2,1)S(1)}, u32[]{:S(2)}, u32[]{:S(2)}) collective-permute-start(bf16[2,64,2560]{2,1,0:T(8,128)(2,1)S(1)} %pad_maximum_fusion.10), channel_id=1, source_target_pairs={{0,3},{1,0},{2,1},{3,2},{4,7},{5,4},{6,5},{7,6},{8,11},{9,8},{10,9... | collective-permute-start | bytes 1966088 | tf_op jit(solution)/shard_map/ppermute | solution.py:21
  27.9 16.6 %collective-permute-start.11 = (bf16[2,64,2560]{2,1,0:T(8,128)(2,1)S(1)}, bf16[2,64,2560]{2,1,0:T(8,128)(2,1)S(1)}, u32[]{:S(2)}, u32[]{:S(2)}) collective-permute-start(bf16[2,64,2560]{2,1,0:T(8,128)(2,1)S(1)} %pad_maximum_fusion.10), channel_id=1, source_target_pairs={{0,4},{4,0},{1,5},{5,1},{2,6},{6,2},{3,7},{7,3},{8,12},{12,8},{9,1... | collective-permute-start | bytes 1966088 | tf_op jit(solution)/shard_map/ppermute | solution.py:21
  30.8 10.2 %collective-permute-start.3 = (bf16[2,32,2560]{2,1,0:T(8,128)(2,1)S(1)}, bf16[2,32,2560]{2,1,0:T(8,128)(2,1)S(1)}, u32[]{:S(2)}, u32[]{:S(2)}) collective-permute-start(bf16[2,32,2560]{2,1,0:T(8,128)(2,1)S(1)} %slice.260), channel_id=1, source_target_pairs={{0,3},{1,0},{2,1},{3,2},{4,7},{5,4},{6,5},{7,6},{8,11},{9,8},{10,9... | collective-permute-start | bytes 983048 | tf_op jit(solution)/shard_map/ppermute | solution.py:21
  34.6 8.7 %collective-permute-start.4 = (bf16[2,32,2560]{2,1,0:T(8,128)(2,1)S(1)}, bf16[2,32,2560]{2,1,0:T(8,128)(2,1)S(1)}, u32[]{:S(2)}, u32[]{:S(2)}) collective-permute-start(bf16[2,32,2560]{2,1,0:T(8,128)(2,1)S(1)} %slice.261), channel_id=1, source_target_pairs={{0,1},{1,2},{2,3},{3,0},{4,5},{5,6},{6,7},{7,4},{8,9},{9,10},{10,1... | collective-permute-start | bytes 983048 | tf_op jit(solution)/shard_map/ppermute | solution.py:21
  37.7 15.4 %collective-permute-start.8 = (bf16[3,160,640]{2,1,0:T(8,128)(2,1)S(1)}, bf16[3,160,640]{2,1,0:T(8,128)(2,1)S(1)}, u32[]{:S(2)}, u32[]{:S(2)}) collective-permute-start(bf16[3,160,640]{2,1,0:T(8,128)(2,1)S(1)} %slice.266), channel_id=1, source_target_pairs={{0,16},{16,32},{32,48},{48,0},{1,17},{17,33},{33,49},{49,1},{2,18}... | collective-permute-start | bytes 1843208 | tf_op jit(solution)/shard_map/ppermute | solution.py:21
  37.8 15.4 %collective-permute-start.7 = (bf16[3,160,640]{2,1,0:T(8,128)(2,1)S(1)}, bf16[3,160,640]{2,1,0:T(8,128)(2,1)S(1)}, u32[]{:S(2)}, u32[]{:S(2)}) collective-permute-start(bf16[3,160,640]{2,1,0:T(8,128)(2,1)S(1)} %slice.265), channel_id=1, source_target_pairs={{0,48},{16,0},{32,16},{48,32},{1,49},{17,1},{33,17},{49,33},{2,50}... | collective-permute-start | bytes 1843208 | tf_op jit(solution)/shard_map/ppermute | solution.py:21
  44.4 16.7 %collective-permute-start.17 = (bf16[2,64,2560]{2,1,0:T(8,128)(2,1)S(1)}, bf16[2,64,2560]{2,1,0:T(8,128)(2,1)S(1)}, u32[]{:S(2)}, u32[]{:S(2)}) collective-permute-start(bf16[2,64,2560]{2,1,0:T(8,128)(2,1)S(1)} %collective-permute-done.11), channel_id=1, source_target_pairs={{0,1},{1,2},{2,3},{3,0},{4,5},{5,6},{6,7},{7,4},{8,9},{9,10},{10,1... | collective-permute-start | bytes 1966088 | tf_op jit(solution)/shard_map/ppermute | solution.py:21
  46.0 14.2 %collective-permute-start.16 = (bf16[2,64,2560]{2,1,0:T(8,128)(2,1)S(1)}, bf16[2,64,2560]{2,1,0:T(8,128)(2,1)S(1)}, u32[]{:S(2)}, u32[]{:S(2)}) collective-permute-start(bf16[2,64,2560]{2,1,0:T(8,128)(2,1)S(1)} %collective-permute-done.11), channel_id=1, source_target_pairs={{0,3},{1,0},{2,1},{3,2},{4,7},{5,4},{6,5},{7,6},{8,11},{9,8},{10,9... | collective-permute-start | bytes 1966088 | tf_op jit(solution)/shard_map/ppermute | solution.py:21
  48.2 30.3 %collective-permute-start.12 = (bf16[3,320,640]{2,1,0:T(8,128)(2,1)S(1)}, bf16[3,320,640]{2,1,0:T(8,128)(2,1)S(1)}, u32[]{:S(2)}, u32[]{:S(2)}) collective-permute-start(bf16[3,320,640]{2,1,0:T(8,128)(2,1)S(1)} %pad_maximum_fusion.3), channel_id=1, source_target_pairs={{0,64},{64,0},{1,65},{65,1},{2,66},{66,2},{3,67},{67,3},{4,68},{68... | collective-permute-start | bytes 3686408 | tf_op jit(solution)/shard_map/ppermute | solution.py:21
  53.2 19.5 %collective-permute-start.13 = (bf16[2,320,640]{2,1,0:T(8,128)(2,1)S(1)}, bf16[2,320,640]{2,1,0:T(8,128)(2,1)S(1)}, u32[]{:S(2)}, u32[]{:S(2)}) collective-permute-start(bf16[2,320,640]{2,1,0:T(8,128)(2,1)S(1)} %collective-permute-done.9), channel_id=1, source_target_pairs={{0,16},{16,32},{32,48},{48,0},{1,17},{17,33},{33,49},{49,1},{2,18}... | collective-permute-start | bytes 2457608 | tf_op jit(solution)/shard_map/ppermute | solution.py:21
  53.2 19.5 %collective-permute-start.10 = (bf16[2,320,640]{2,1,0:T(8,128)(2,1)S(1)}, bf16[2,320,640]{2,1,0:T(8,128)(2,1)S(1)}, u32[]{:S(2)}, u32[]{:S(2)}) collective-permute-start(bf16[2,320,640]{2,1,0:T(8,128)(2,1)S(1)} %collective-permute-done.9), channel_id=1, source_target_pairs={{0,48},{16,0},{32,16},{48,32},{1,49},{17,1},{33,17},{49,33},{2,50}... | collective-permute-start | bytes 2457608 | tf_op jit(solution)/shard_map/ppermute | solution.py:21
  61.1 6.5 %collective-permute-start.18 = (bf16[2,32,2560]{2,1,0:T(8,128)(2,1)S(1)}, bf16[2,32,2560]{2,1,0:T(8,128)(2,1)S(1)}, u32[]{:S(2)}, u32[]{:S(2)}) collective-permute-start(bf16[2,32,2560]{2,1,0:T(8,128)(2,1)S(1)} %slice.286), channel_id=1, source_target_pairs={{0,3},{1,0},{2,1},{3,2},{4,7},{5,4},{6,5},{7,6},{8,11},{9,8},{10,9... | collective-permute-start | bytes 983048 | tf_op jit(solution)/shard_map/ppermute | solution.py:21
  64.8 7.7 %collective-permute-start.19 = (bf16[2,32,2560]{2,1,0:T(8,128)(2,1)S(1)}, bf16[2,32,2560]{2,1,0:T(8,128)(2,1)S(1)}, u32[]{:S(2)}, u32[]{:S(2)}) collective-permute-start(bf16[2,32,2560]{2,1,0:T(8,128)(2,1)S(1)} %slice.287), channel_id=1, source_target_pairs={{0,1},{1,2},{2,3},{3,0},{4,5},{5,6},{6,7},{7,4},{8,9},{9,10},{10,1... | collective-permute-start | bytes 983048 | tf_op jit(solution)/shard_map/ppermute | solution.py:21
  75.2 9.4 %collective-permute-start.14 = (bf16[2,160,640]{2,1,0:T(8,128)(2,1)S(1)}, bf16[2,160,640]{2,1,0:T(8,128)(2,1)S(1)}, u32[]{:S(2)}, u32[]{:S(2)}) collective-permute-start(bf16[2,160,640]{2,1,0:T(8,128)(2,1)S(1)} %slice.283), channel_id=1, source_target_pairs={{0,48},{16,0},{32,16},{48,32},{1,49},{17,1},{33,17},{49,33},{2,50}... | collective-permute-start | bytes 1228808 | tf_op jit(solution)/shard_map/ppermute | solution.py:21
  77.0 8.0 %collective-permute-start.15 = (bf16[2,160,640]{2,1,0:T(8,128)(2,1)S(1)}, bf16[2,160,640]{2,1,0:T(8,128)(2,1)S(1)}, u32[]{:S(2)}, u32[]{:S(2)}) collective-permute-start(bf16[2,160,640]{2,1,0:T(8,128)(2,1)S(1)} %slice.284), channel_id=1, source_target_pairs={{0,16},{16,32},{32,48},{48,0},{1,17},{17,33},{33,49},{49,1},{2,18}... | collective-permute-start | bytes 1228808 | tf_op jit(solution)/shard_map/ppermute | solution.py:21
  78.5 16.2 %collective-permute-start.22 = (bf16[320,640]{1,0:T(8,128)(2,1)S(1)}, bf16[320,640]{1,0:T(8,128)(2,1)S(1)}, u32[]{:S(2)}, u32[]{:S(2)}) collective-permute-start(bf16[320,640]{1,0:T(8,128)(2,1)S(1)} %get-tuple-element.72), channel_id=1, source_target_pairs={{0,64},{64,0},{1,65},{65,1},{2,66},{66,2},{3,67},{67,3},{4,68},{68... | collective-permute-start | bytes 1228808 | tf_op jit(solution)/shard_map/ppermute | solution.py:21
  88.4 8.6 %collective-permute-start.21 = (bf16[512,640]{1,0:T(8,128)(2,1)S(1)}, bf16[512,640]{1,0:T(8,128)(2,1)S(1)}, u32[]{:S(2)}, u32[]{:S(2)}) collective-permute-start(bf16[512,640]{1,0:T(8,128)(2,1)S(1)} %pad_maximum_fusion.12), channel_id=1, source_target_pairs={{0,8},{8,0},{1,9},{9,1},{2,10},{10,2},{3,11},{11,3},{4,12},{12,4},... | collective-permute-start | bytes 1966088 | tf_op jit(solution)/shard_map/ppermute | solution.py:21
  94.4 2.6 %collective-permute-start.20 = (bf16[512,640]{1,0:T(8,128)(2,1)S(1)}, bf16[512,640]{1,0:T(8,128)(2,1)S(1)}, u32[]{:S(2)}, u32[]{:S(2)}) collective-permute-start(bf16[512,640]{1,0:T(8,128)(2,1)S(1)} %pad_maximum_fusion.11), channel_id=1, source_target_pairs={{0,8},{8,0},{1,9},{9,1},{2,10},{10,2},{3,11},{11,3},{4,12},{12,4},... | collective-permute-start | bytes 1966088 | tf_op jit(solution)/shard_map/ppermute | solution.py:21
  96.3 6.1 %slice-start = ((s8[6553600]{0:T(1024)(128)(4,1)}), s8[4194304]{0:T(1024)(128)(4,1)S(1)}, s32[]{:S(2)}) async-start(s8[6553600]{0:T(1024)(128)(4,1)} %bitcast.64), calls=%async_computation.2 | async-start | bytes 8388608
  96.4 6.0 %slice-start.1 = ((s8[6553600]{0:T(1024)(128)(4,1)}), s8[2359296]{0:T(1024)(128)(4,1)S(1)}, s32[]{:S(2)}) async-start(s8[6553600]{0:T(1024)(128)(4,1)} %bitcast.64), calls=%async_computation.3 | async-start | bytes 4718592
  96.4 2.3 %collective-permute-start.23 = (bf16[512,640]{1,0:T(8,128)(2,1)S(1)}, bf16[512,640]{1,0:T(8,128)(2,1)S(1)}, u32[]{:S(2)}, u32[]{:S(2)}) collective-permute-start(bf16[512,640]{1,0:T(8,128)(2,1)S(1)} %pad_maximum_fusion.13), channel_id=1, source_target_pairs={{0,8},{8,0},{1,9},{9,1},{2,10},{10,2},{3,11},{11,3},{4,12},{12,4},... | collective-permute-start | bytes 1966088 | tf_op jit(solution)/shard_map/ppermute | solution.py:21
  104.2 10.5 %collective-permute-start.24 = (bf16[64,2560]{1,0:T(8,128)(2,1)S(1)}, bf16[64,2560]{1,0:T(8,128)(2,1)S(1)}, u32[]{:S(2)}, u32[]{:S(2)}) collective-permute-start(bf16[64,2560]{1,0:T(8,128)(2,1)S(1)} %get-tuple-element.84), channel_id=1, source_target_pairs={{0,4},{4,0},{1,5},{5,1},{2,6},{6,2},{3,7},{7,3},{8,12},{12,8},{9,1... | collective-permute-start | bytes 983048 | tf_op jit(solution)/shard_map/ppermute | solution.py:21
  107.1 14.6 %collective-permute-start.29 = (bf16[64,2560]{1,0:T(8,128)(2,1)S(1)}, bf16[64,2560]{1,0:T(8,128)(2,1)S(1)}, u32[]{:S(2)}, u32[]{:S(2)}) collective-permute-start(bf16[64,2560]{1,0:T(8,128)(2,1)S(1)} %get-tuple-element.83), channel_id=1, source_target_pairs={{0,4},{4,0},{1,5},{5,1},{2,6},{6,2},{3,7},{7,3},{8,12},{12,8},{9,1... | collective-permute-start | bytes 983048 | tf_op jit(solution)/shard_map/ppermute | solution.py:21
  107.4 25.4 %collective-permute-start.32 = (bf16[64,5120]{1,0:T(8,128)(2,1)S(1)}, bf16[64,5120]{1,0:T(8,128)(2,1)S(1)}, u32[]{:S(2)}, u32[]{:S(2)}) collective-permute-start(bf16[64,5120]{1,0:T(8,128)(2,1)S(1)} %get-tuple-element.85), channel_id=1, source_target_pairs={{0,1},{1,2},{2,3},{3,0},{4,5},{5,6},{6,7},{7,4},{8,9},{9,10},{10,1... | collective-permute-start | bytes 1966088 | tf_op jit(solution)/shard_map/ppermute | solution.py:21
  108.2 24.6 %collective-permute-start.33 = (bf16[64,5120]{1,0:T(8,128)(2,1)S(1)}, bf16[64,5120]{1,0:T(8,128)(2,1)S(1)}, u32[]{:S(2)}, u32[]{:S(2)}) collective-permute-start(bf16[64,5120]{1,0:T(8,128)(2,1)S(1)} %get-tuple-element.86), channel_id=1, source_target_pairs={{0,3},{1,0},{2,1},{3,2},{4,7},{5,4},{6,5},{7,6},{8,11},{9,8},{10,9... | collective-permute-start | bytes 1966088 | tf_op jit(solution)/shard_map/ppermute | solution.py:21
  121.8 9.3 %collective-permute-start.30 = (bf16[64,2560]{1,0:T(8,128)(2,1)S(1)}, bf16[64,2560]{1,0:T(8,128)(2,1)S(1)}, u32[]{:S(2)}, u32[]{:S(2)}) collective-permute-start(bf16[64,2560]{1,0:T(8,128)(2,1)S(1)} %fusion.19), channel_id=1, source_target_pairs={{0,3},{1,0},{2,1},{3,2},{4,7},{5,4},{6,5},{7,6},{8,11},{9,8},{10,9... | collective-permute-start | bytes 983048 | tf_op jit(solution)/shard_map/ppermute | solution.py:21
  124.8 16.1 %collective-permute-start.28 = (bf16[64,2560]{1,0:T(8,128)(2,1)S(1)}, bf16[64,2560]{1,0:T(8,128)(2,1)S(1)}, u32[]{:S(2)}, u32[]{:S(2)}) collective-permute-start(bf16[64,2560]{1,0:T(8,128)(2,1)S(1)} %get-tuple-element.81), channel_id=1, source_target_pairs={{0,3},{1,0},{2,1},{3,2},{4,7},{5,4},{6,5},{7,6},{8,11},{9,8},{10,9... | collective-permute-start | bytes 983048 | tf_op jit(solution)/shard_map/ppermute | solution.py:21
  125.0 15.9 %collective-permute-start.27 = (bf16[64,2560]{1,0:T(8,128)(2,1)S(1)}, bf16[64,2560]{1,0:T(8,128)(2,1)S(1)}, u32[]{:S(2)}, u32[]{:S(2)}) collective-permute-start(bf16[64,2560]{1,0:T(8,128)(2,1)S(1)} %get-tuple-element.82), channel_id=1, source_target_pairs={{0,1},{1,2},{2,3},{3,0},{4,5},{5,6},{6,7},{7,4},{8,9},{9,10},{10,1... | collective-permute-start | bytes 983048 | tf_op jit(solution)/shard_map/ppermute | solution.py:21
  131.2 17.0 %copy-start.3 = (f32[1,5120]{1,0:T(1,128)S(1)}, f32[1,5120]{1,0:T(1,128)}, u32[]{:S(2)}) copy-start(f32[1,5120]{1,0:T(1,128)} %get-tuple-element.42) | copy-start | bytes 61444
  131.2 8.0 %collective-permute-start.25 = (bf16[64,2560]{1,0:T(8,128)(2,1)S(1)}, bf16[64,2560]{1,0:T(8,128)(2,1)S(1)}, u32[]{:S(2)}, u32[]{:S(2)}) collective-permute-start(bf16[64,2560]{1,0:T(8,128)(2,1)S(1)} %get-tuple-element.80), channel_id=1, source_target_pairs={{0,1},{1,2},{2,3},{3,0},{4,5},{5,6},{6,7},{7,4},{8,9},{9,10},{10,1... | collective-permute-start | bytes 983048 | tf_op jit(solution)/shard_map/ppermute | solution.py:21
  133.1 15.1 %collective-permute-start.34 = (bf16[64,5120]{1,0:T(8,128)(2,1)S(1)}, bf16[64,5120]{1,0:T(8,128)(2,1)S(1)}, u32[]{:S(2)}, u32[]{:S(2)}) collective-permute-start(bf16[64,5120]{1,0:T(8,128)(2,1)S(1)} %fusion.1), channel_id=1, source_target_pairs={{0,4},{4,0},{1,5},{5,1},{2,6},{6,2},{3,7},{7,3},{8,12},{12,8},{9,1... | collective-permute-start | bytes 1966088 | tf_op jit(solution)/shard_map/ppermute | solution.py:21
  135.9 7.5 %collective-permute-start.31 = (bf16[64,2560]{1,0:T(8,128)(2,1)S(1)}, bf16[64,2560]{1,0:T(8,128)(2,1)S(1)}, u32[]{:S(2)}, u32[]{:S(2)}) collective-permute-start(bf16[64,2560]{1,0:T(8,128)(2,1)S(1)} %get-tuple-element.79), channel_id=1, source_target_pairs={{0,3},{1,0},{2,1},{3,2},{4,7},{5,4},{6,5},{7,6},{8,11},{9,8},{10,9... | collective-permute-start | bytes 983048 | tf_op jit(solution)/shard_map/ppermute | solution.py:21
  139.3 8.9 %collective-permute-start.26 = (bf16[64,2560]{1,0:T(8,128)(2,1)S(1)}, bf16[64,2560]{1,0:T(8,128)(2,1)S(1)}, u32[]{:S(2)}, u32[]{:S(2)}) collective-permute-start(bf16[64,2560]{1,0:T(8,128)(2,1)S(1)} %fusion.22), channel_id=1, source_target_pairs={{0,1},{1,2},{2,3},{3,0},{4,5},{5,6},{6,7},{7,4},{8,9},{9,10},{10,1... | collective-permute-start | bytes 983048 | tf_op jit(solution)/shard_map/ppermute | solution.py:21
  167.3 15.2 %copy-start.2 = (f32[64,5120]{1,0:T(8,128)S(1)}, f32[64,5120]{1,0:T(8,128)}, u32[]{:S(2)}) copy-start(f32[64,5120]{1,0:T(8,128)} %param.8) | copy-start | bytes 3932164

commit v4 on v3

--- a/solution.py
+++ b/solution.py
@@ -12,7 +12,7 @@
 SEQ = ("xh", "z")
 F32, BF16 = jnp.float32, jnp.bfloat16
 VMEM_BYTES = 60 * 1024 * 1024
-ROUND = [0, 1, 3, 2]
+COLUMNS = [(0, 0), (1, 0), (0, 1), (1, 1), (3, 0), (3, 1), (2, 0), (2, 1)]
 BLOCKS = [2, 1, 3, 0]
 
 
@@ -41,19 +41,17 @@
     xl, y, core = (lax.axis_index(a) for a in TM)
     ny, wide = 4, 2 * rows
     low = core == 0
-    for dxl in range(2):
-        for pair in range(ny // 2):
-            mine, other = [], []
-            for dy in ROUND[2 * pair : 2 * pair + 2]:
-                chip = lax.rem(xl + dxl, 2) * ny + lax.rem(y + dy, ny)
-                block = scratch[:, pl.ds(pl.multiple_of(chip * wide, 128), wide)]
-                first, second = block[:, :rows], block[:, rows:]
-                mine.append(jnp.where(low, first, second))
-                other.append(jnp.where(low, second, first))
-            place = dxl * ny // 2 + pair
-            here = slice(place * wide, (place + 1) * wide)
-            mine_ref[:, here] = jnp.concatenate(mine, axis=1).astype(BF16)
-            other_ref[:, here] = jnp.concatenate(other, axis=1).astype(BF16)
+    for place in range(0, len(COLUMNS), 2):
+        mine, other = [], []
+        for dy, dxl in COLUMNS[place : place + 2]:
+            chip = lax.rem(xl + dxl, 2) * ny + lax.rem(y + dy, ny)
+            block = scratch[:, pl.ds(pl.multiple_of(chip * wide, 128), wide)]
+            first, second = block[:, :rows], block[:, rows:]
+            mine.append(jnp.where(low, first, second))
+            other.append(jnp.where(low, second, first))
+        here = slice(place * rows, (place + 2) * rows)
+        mine_ref[:, here] = jnp.concatenate(mine, axis=1).astype(BF16)
+        other_ref[:, here] = jnp.concatenate(other, axis=1).astype(BF16)
 
 
 def modulate(states, t_index, mod_table, coef, rows):
@@ -144,25 +142,23 @@
 
     za, zb = send(pair, "z", -1), send(pair, "z", 1)
     across = send(after(pair, p), "xh", 1)
-    zfa = send(after(za[:, :short], zb), "z", -1)
-    zfb = send(after(zb[:, short:], za), "z", 1)
+    near = after(p, za, zb)
+    pa, pb = send(near, "y", -1), send(near, "y", 1)
+    zfa = send(after(za[:, :short], a1, b1), "z", -1)
+    zfb = send(after(zb[:, short:], a1, b1), "z", 1)
 
     xv = send(after(jnp.stack([own[2], a1[2], b1[2]]), across), "xl", 1)
-    fa = send(after(a1[:, :half], b1), "y", -1)
-    fb = send(after(b1[:, half:], a1), "y", 1)
-    far = jnp.concatenate([fa, fb], axis=1)
-
     distant = after(across, zfa, zfb)
     xa, xb = send(distant, "z", -1), send(distant, "z", 1)
+
+    fa = send(jnp.concatenate([a1[:, :half], pa[:, :half]], axis=0), "y", -1)
+    fb = send(jnp.concatenate([b1[:, half:], pb[:, half:]], axis=0), "y", 1)
     xfa = send(after(xa[:, :short], xb), "z", -1)
     xfb = send(after(xb[:, short:], xa), "z", 1)
-
-    near = after(p, fa, fb)
-    pa, pb = send(near, "y", -1), send(near, "y", 1)
-    xvf = send(after(far[2], xv), "xl", 1)
-    pfa = send(after(pa[:, :half], pb), "y", -1)
-    pfb = send(after(pb[:, half:], pa), "y", 1)
-    pfar = jnp.concatenate([pfa, pfb], axis=1)
+    vfa = send(after(xv[1, :half], xfa, xfb), "y", -1)
+    vfb = send(after(xv[2, half:], xfa, xfb), "y", 1)
+    far = jnp.concatenate([fa, fb], axis=1)
+    vfar = jnp.concatenate([vfa, vfb], axis=0)
 
     features = []
     for near, above, below, ends in ((pair, za, zb, (zfa, zfb)), (across, xa, xb, (xfa, xfb))):
@@ -170,33 +166,24 @@
         features.append(rowed.reshape(2 * rowed.shape[1], -1))
     count = features[0].shape[0]
 
-    def product(begin, weights):
-        stop = begin + weights[0].shape[0]
-        return [
-            [jnp.dot(f[:, begin:stop], w, preferred_element_type=F32) for w in weights]
-            for f in features
-        ]
+    def product(begin, blocks):
+        stop = begin + len(blocks) * rows
+        weight = jnp.concatenate(blocks, axis=0)
+        return [jnp.dot(f[:, begin:stop], weight, preferred_element_type=F32) for f in features]
 
     def plus(sofar, more):
-        return [[a + b for a, b in zip(x, y)] for x, y in zip(sofar, more)]
-
-    stacked = [
-        [jnp.concatenate(blocks, axis=0) for blocks in stage]
-        for stage in (
-            [[own[j], a1[j], b1[j], far[j]] for j in range(3)],
-            [[p[0], pa[0]], [p[1], pa[1]], [xv[0], xv[1]]],
-            [[pb[0], pfar[0]], [pb[1], pfar[1]], [xv[2], xvf]],
-        )
-    ]
-    features[1] = after(features[1], pa, pb)
-    stacked[1] = [after(w, xv) for w in stacked[1]]
-    begun = [lax.optimization_barrier(x) for x in product(0, stacked[0])]
-    begun = [lax.optimization_barrier(x) for x in plus(begun, product(4 * rows, stacked[1]))]
-    begun = plus(begun, product(6 * rows, stacked[2]))
+        return [a + b for a, b in zip(sofar, more)]
+
+    held = lax.optimization_barrier
+    begun = [[held(x) for x in product(0, [own[j], a1[j], p[j], pa[j], b1[j], pb[j]])] for j in range(2)]
+    begun.append([held(x) for x in product(0, [own[2], a1[2]])])
+    begun[2] = [held(x) for x in plus(begun[2], product(2 * rows, [xv[0], xv[1], b1[2], xv[2]]))]
+    last = [[far[0], far[3]], [far[1], far[4]], [far[2], vfar]]
+    begun = [plus(x, product(6 * rows, blocks)) for x, blocks in zip(begun, last)]
     parts = []
     for j in range(3):
-        mates = jnp.concatenate([x[j][count // 2 :] for x in begun], axis=0).astype(BF16)
-        parts += [begun[0][j], begun[1][j], send(mates, "core", 1)]
+        mates = jnp.concatenate([x[count // 2 :] for x in begun[j]], axis=0).astype(BF16)
+        parts += [*begun[j], send(mates, "core", 1)]
 
     cut, half, head = width // 2, count // 2, 3 * tokens
     query, keys, values, attended = attention_call(
@@ -205,17 +192,22 @@
     )
     first = jnp.dot(attended, wo, preferred_element_type=F32).astype(BF16)
     far1, above1, below1 = (first[i * tokens : (i + 1) * tokens] for i in range(3))
-    joins = [send(far1[:, :cut], "xh", 1), send(far1[:, cut:], "xh", 1)]
     up1, down1 = send(above1, "z", 1), send(below1, "z", -1)
+    quarter = cut // 2
+    joins = [send(far1[:, :quarter], "xh", 1), send(far1[:, quarter:], "xh", 1)]
     (attended,) = attention_call(
         functools.partial(second_kernel, head), (after(query, joins[0]), keys, values),
         (count,) * 3, (count - head,),
     )
     rest = jnp.dot(attended, wo, preferred_element_type=F32)
     far0, above0, below0, near0, near1 = (rest[i * tokens : (i + 1) * tokens] for i in range(5))
-    free = send(above0[:, cut:].astype(BF16), "z", 1), send(below0[:, :cut].astype(BF16), "z", -1)
-    up = send((far0[:, :cut] + joins[0].astype(F32)).astype(BF16), "z", 1)
-    down = send((far0[:, cut:] + joins[1].astype(F32)).astype(BF16), "z", -1)
+    far0 = (far0 + jnp.concatenate(joins, axis=1).astype(F32)).astype(BF16)
+    up, down = send(far0[:, :cut], "z", 1), send(far0[:, cut:], "z", -1)
+    free = (
+        send(after(above0[:, cut:].astype(BF16), up1, down1), "z", 1),
+        send(after(below0[:, :cut].astype(BF16), up1, down1), "z", -1),
+    )
+    near1 = after(near1, far0)
     there = send((near1 + up1.astype(F32) + down1.astype(F32)).astype(BF16), "xh", 1)
     bound = (
         send((above0[:, :cut] + up.astype(F32)).astype(BF16), "z", 1),

time: 184 us -> 179 us (0.973)
  starting transfers between devices: 57.2 us -> 47.4 us
  waiting for transfers between devices: 56.2 us -> 61 us
  other arithmetic: 2.95 us -> 4.84 us
    ppermute x35 -> x34, starting transfers between devices: 57.2 us -> 47.4 us  [send(): lax.ppermute(array, axis, [(i, (i + shift) % size) for i in range(size)])]
    ppermute x35 -> x34, waiting for transfers between devices: 56.2 us -> 61 us  [send(): lax.ppermute(array, axis, [(i, (i + shift) % size) for i in range(size)])]
    dot_general x18 -> x14, matrix products: 16 us -> 15.4 us  [product(): jnp.dot(f[:, begin:stop], weight, preferred_element_type=F32)]
  transfers between devices with their start and end apart: 35 -> 34, of which waited for: 17 -> 19; matrix products, arithmetic and copies ran while one was open for 12% -> 13% of each run, Pallas kernels for 1% -> 2%
where the time goes in v4:
time: 179 us
  waiting for transfers between devices  61 us (34%)
  starting transfers between devices  47.4 us (26%)
  blocking collectives  32 us (18%)
  matrix products  19.8 us (11%)
  Pallas kernels  9.66 us (5%)
  other arithmetic  4.84 us (3%)
  local copies, waits for them, and re-layouts  3.08 us (2%)
    ppermute x34, waiting for transfers between devices, send(): lax.ppermute(array, axis, [(i, (i + shift) % size) for i in range(size)])  61 us
    ppermute x34, starting transfers between devices, send(): lax.ppermute(array, axis, [(i, (i + shift) % size) for i in range(size)])  47.4 us
    all_to_all x1, blocking collectives, on_device(): lax.all_to_all(term.reshape(steps, tokens // steps, width), TM, 0, 0)  17 us
    dot_general x14, matrix products, product(): jnp.dot(f[:, begin:stop], weight, preferred_element_type=F32)  15.4 us
    all_to_all x1, blocking collectives, on_device(): total = lax.all_to_all(total, TM, 0, 0).reshape(tokens, width)  15.1 us
    pallas_call x2, Pallas kernels, attention_call(): pl.pallas_call(kernel, out_shape=[jax.ShapeDtypeStruct((rows, width), BF1...  6.36 us
  transfers between devices with their start and end apart: 34, of which 19 were waited for; matrix products, arithmetic and copies ran while one was open for 13% of the time, Pallas kernels for 2%

profile of v4, /device:TPU:1, one launch (start us, length us, event | category | flops | bytes accessed | tf_op | source)
XLA Modules:
  0.0 179.1 jit_solution(16904469277265121061)
XLA Ops:
  0.7 3.3 %shard_map.73 = (bf16[64,2560]{1,0:T(8,128)(2,1)}, bf16[64,2560]{1,0:T(8,128)(2,1)}, f32[1,5120]{1,0:T(1,128)}) custom-call(s32[1]{0:T(128)S(6)} %copy.27.t_ref, f32[1,64,5120]{2,1,0:T(8,128)} %state_ref.1, f32[3,50,5120]{2,1,0:T(8,128)} %bitcast.88, f32[50]{0:T(128)} %coef_ref.1), custom_call_target="tpu_custom_call" | custom-call | flops 1000 | bytes 1000 | tf_op jit(solution)/shard_map/pallas_call | solution.py:60
  4.0 1.4 collective-permute-start
  5.4 2.8 %collective-permute-start.2 = (bf16[3,320,640]{2,1,0:T(8,128)(2,1)S(1)}, bf16[3,320,640]{2,1,0:T(8,128)(2,1)S(1)}, u32[]{:S(2)}, u32[]{:S(2)}) collective-permute-start(bf16[3,320,640]{2,1,0:T(8,128)(2,1)S(1)} %copy-done), channel_id=1, source_target_pairs={{0,48},{16,0},{32,16},{48,32},{1,49},{17,1},{33,17},{49,33},{2,50}... | collective-permute-start | bytes 3686408 | tf_op jit(solution)/shard_map/ppermute | solution.py:21
  8.3 1.3 collective-permute-start.7
  9.6 1.0 pad_maximum_fusion.8
  10.6 3.8 %collective-permute-start.1 = (bf16[2,64,2560]{2,1,0:T(8,128)(2,1)S(1)}, bf16[2,64,2560]{2,1,0:T(8,128)(2,1)S(1)}, u32[]{:S(2)}, u32[]{:S(2)}) collective-permute-start(bf16[2,64,2560]{2,1,0:T(8,128)(2,1)S(1)} %pad_maximum_fusion.8), channel_id=1, source_target_pairs={{0,3},{1,0},{2,1},{3,2},{4,7},{5,4},{6,5},{7,6},{8,11},{9,8},{10,9... | collective-permute-start | bytes 1966088 | tf_op jit(solution)/shard_map/ppermute | solution.py:21
  14.6 13.2 %collective-permute-done.7 = bf16[2,320,640]{2,1,0:T(8,128)(2,1)S(1)} collective-permute-done((bf16[2,320,640]{2,1,0:T(8,128)(2,1)S(1)}, bf16[2,320,640]{2,1,0:T(8,128)(2,1)S(1)}, u32[]{:S(2)}, u32[]{:S(2)}) %collective-permute-start.7) | collective-permute-done | bytes 819232 | tf_op jit(solution)/shard_map/ppermute | solution.py:21
  27.8 2.7 %collective-permute-start.12 = (bf16[2,64,2560]{2,1,0:T(8,128)(2,1)S(1)}, bf16[2,64,2560]{2,1,0:T(8,128)(2,1)S(1)}, u32[]{:S(2)}, u32[]{:S(2)}) collective-permute-start(bf16[2,64,2560]{2,1,0:T(8,128)(2,1)S(1)} %pad_maximum_fusion.8), channel_id=1, source_target_pairs={{0,4},{4,0},{1,5},{5,1},{2,6},{6,2},{3,7},{7,3},{8,12},{12,8},{9,1... | collective-permute-start | bytes 1966088 | tf_op jit(solution)/shard_map/ppermute | solution.py:21
  31.0 2.4 %collective-permute-start.8 = (bf16[2,320,640]{2,1,0:T(8,128)(2,1)S(1)}, bf16[2,320,640]{2,1,0:T(8,128)(2,1)S(1)}, u32[]{:S(2)}, u32[]{:S(2)}) collective-permute-start(bf16[2,320,640]{2,1,0:T(8,128)(2,1)S(1)} %collective-permute-done.7), channel_id=1, source_target_pairs={{0,48},{16,0},{32,16},{48,32},{1,49},{17,1},{33,17},{49,33},{2,50}... | collective-permute-start | bytes 2457608 | tf_op jit(solution)/shard_map/ppermute | solution.py:21
  33.4 1.2 collective-permute-done.2
  34.6 3.1 %collective-permute-done.3 = bf16[3,320,640]{2,1,0:T(8,128)(2,1)S(1)} collective-permute-done((bf16[3,320,640]{2,1,0:T(8,128)(2,1)S(1)}, bf16[3,320,640]{2,1,0:T(8,128)(2,1)S(1)}, u32[]{:S(2)}, u32[]{:S(2)}) %collective-permute-start.3) | collective-permute-done | bytes 1228832 | tf_op jit(solution)/shard_map/ppermute | solution.py:21
  37.7 3.8 %collective-permute-start.4 = (bf16[2,32,2560]{2,1,0:T(8,128)(2,1)S(1)}, bf16[2,32,2560]{2,1,0:T(8,128)(2,1)S(1)}, u32[]{:S(2)}, u32[]{:S(2)}) collective-permute-start(bf16[2,32,2560]{2,1,0:T(8,128)(2,1)S(1)} %slice.270), channel_id=1, source_target_pairs={{0,3},{1,0},{2,1},{3,2},{4,7},{5,4},{6,5},{7,6},{8,11},{9,8},{10,9... | collective-permute-start | bytes 983048 | tf_op jit(solution)/shard_map/ppermute | solution.py:21
  42.0 2.3 %collective-permute-done.12 = bf16[2,64,2560]{2,1,0:T(8,128)(2,1)S(1)} collective-permute-done((bf16[2,64,2560]{2,1,0:T(8,128)(2,1)S(1)}, bf16[2,64,2560]{2,1,0:T(8,128)(2,1)S(1)}, u32[]{:S(2)}, u32[]{:S(2)}) %collective-permute-start.12) | collective-permute-done | bytes 655392 | tf_op jit(solution)/shard_map/ppermute | solution.py:21
  44.4 1.2 collective-permute-start.19
  46.5 3.1 %collective-permute-done.6 = bf16[2,32,2560]{2,1,0:T(8,128)(2,1)S(1)} collective-permute-done((bf16[2,32,2560]{2,1,0:T(8,128)(2,1)S(1)}, bf16[2,32,2560]{2,1,0:T(8,128)(2,1)S(1)}, u32[]{:S(2)}, u32[]{:S(2)}) %collective-permute-start.6) | collective-permute-done | bytes 327712 | tf_op jit(solution)/shard_map/ppermute | solution.py:21
  49.9 1.2 collective-permute-start.14
  52.3 1.9 %collective-permute-done.9 = bf16[2,320,640]{2,1,0:T(8,128)(2,1)S(1)} collective-permute-done((bf16[2,320,640]{2,1,0:T(8,128)(2,1)S(1)}, bf16[2,320,640]{2,1,0:T(8,128)(2,1)S(1)}, u32[]{:S(2)}, u32[]{:S(2)}) %collective-permute-start.9) | collective-permute-done | bytes 819232 | tf_op jit(solution)/shard_map/ppermute | solution.py:21
  54.4 1.8 fusion.6
  58.1 4.5 %collective-permute-done.13 = bf16[2,64,2560]{2,1,0:T(8,128)(2,1)S(1)} collective-permute-done((bf16[2,64,2560]{2,1,0:T(8,128)(2,1)S(1)}, bf16[2,64,2560]{2,1,0:T(8,128)(2,1)S(1)}, u32[]{:S(2)}, u32[]{:S(2)}) %collective-permute-start.13) | collective-permute-done | bytes 655392 | tf_op jit(solution)/shard_map/ppermute | solution.py:21
  62.7 1.5 collective-permute-done.14
  64.7 1.8 fusion.4
  67.5 2.9 %collective-permute-done.15 = bf16[2,32,2560]{2,1,0:T(8,128)(2,1)S(1)} collective-permute-done((bf16[2,32,2560]{2,1,0:T(8,128)(2,1)S(1)}, bf16[2,32,2560]{2,1,0:T(8,128)(2,1)S(1)}, u32[]{:S(2)}, u32[]{:S(2)}) %collective-permute-start.15) | collective-permute-done | bytes 327712 | tf_op jit(solution)/shard_map/ppermute | solution.py:21
  70.4 3.6 %collective-permute-done.16 = bf16[2,32,2560]{2,1,0:T(8,128)(2,1)S(1)} collective-permute-done((bf16[2,32,2560]{2,1,0:T(8,128)(2,1)S(1)}, bf16[2,32,2560]{2,1,0:T(8,128)(2,1)S(1)}, u32[]{:S(2)}, u32[]{:S(2)}) %collective-permute-start.16) | collective-permute-done | bytes 327712 | tf_op jit(solution)/shard_map/ppermute | solution.py:21
  74.2 1.8 fusion.2
  76.0 1.8 fusion
  78.6 1.2 convolution_add_fusion.2
  80.0 2.6 %collective-permute-start.20 = (bf16[160,640]{1,0:T(8,128)(2,1)S(1)}, bf16[160,640]{1,0:T(8,128)(2,1)S(1)}, u32[]{:S(2)}, u32[]{:S(2)}) collective-permute-start(bf16[160,640]{1,0:T(8,128)(2,1)S(1)} %get-tuple-element.37), channel_id=1, source_target_pairs={{0,48},{16,0},{32,16},{48,32},{1,49},{17,1},{33,17},{49,33},{2,50}... | collective-permute-start | bytes 614408 | tf_op jit(solution)/shard_map/ppermute | solution.py:21
  82.6 1.2 fusion.13
  87.9 5.6 %collective-permute-start.17 = (bf16[512,640]{1,0:T(8,128)(2,1)S(1)}, bf16[512,640]{1,0:T(8,128)(2,1)S(1)}, u32[]{:S(2)}, u32[]{:S(2)}) collective-permute-start(bf16[512,640]{1,0:T(8,128)(2,1)S(1)} %pad_maximum_fusion.9), channel_id=1, source_target_pairs={{0,8},{8,0},{1,9},{9,1},{2,10},{10,2},{3,11},{11,3},{4,12},{12,4},... | collective-permute-start | bytes 1966088 | tf_op jit(solution)/shard_map/ppermute | solution.py:21
  96.6 1.7 collective-permute-done.22.vb
  98.3 3.7 %shard_map.74 = (bf16[512,640]{1,0:T(8,128)(2,1)S(1)}, bf16[512,640]{1,0:T(8,128)(2,1)S(1)}, bf16[512,640]{1,0:T(8,128)(2,1)S(1)}, bf16[192,640]{1,0:T(8,128)(2,1)S(1)}) custom-call(f32[512,640]{1,0:T(8,128)S(1)} %add.51.q0, f32[512,640]{1,0:T(8,128)S(1)} %add.52.q1, bf16[512,640]{1,0:T(8,128)(2,1)S(1)} %collective-permute-done.17.qb, ...), custom_call_target="tpu_custom_call" | custom-call | flops 251658240 | bytes 2621440 | tf_op jit(solution)/shard_map/pallas_call | solution.py:118
  102.0 1.7 convolution_convert_fusion
  103.8 2.8 %collective-permute-start.23 = (bf16[64,1280]{1,0:T(8,128)(2,1)S(1)}, bf16[64,1280]{1,0:T(8,128)(2,1)S(1)}, u32[]{:S(2)}, u32[]{:S(2)}) collective-permute-start(bf16[64,1280]{1,0:T(8,128)(2,1)S(1)} %slice.314), channel_id=1, source_target_pairs={{0,4},{4,0},{1,5},{5,1},{2,6},{6,2},{3,7},{7,3},{8,12},{12,8},{9,1... | collective-permute-start | bytes 491528 | tf_op jit(solution)/shard_map/ppermute | solution.py:21
  108.5 2.3 %collective-permute-done.23 = bf16[64,1280]{1,0:T(8,128)(2,1)S(1)} collective-permute-done((bf16[64,1280]{1,0:T(8,128)(2,1)S(1)}, bf16[64,1280]{1,0:T(8,128)(2,1)S(1)}, u32[]{:S(2)}, u32[]{:S(2)}) %collective-permute-start.23) | collective-permute-done | bytes 163872 | tf_op jit(solution)/shard_map/ppermute | solution.py:21
  110.8 2.7 %shard_map.75 = bf16[320,640]{1,0:T(8,128)(2,1)S(1)} custom-call(bf16[512,640]{1,0:T(8,128)(2,1)S(1)} %get-tuple-element.41.query_ref, bf16[512,640]{1,0:T(8,128)(2,1)S(1)} %get-tuple-element.42.keys_ref, bf16[512,640]{1,0:T(8,128)(2,1)S(1)} %get-tuple-element.43.values_ref), custom_call_target="tpu_custom_call" | custom-call | flops 419430400 | bytes 2621440 | tf_op jit(solution)/shard_map/pallas_call | solution.py:118
  113.5 2.7 %fusion.58 = (bf16[320,5120]{1,0:T(8,128)(2,1)S(1)}, f32[320,5120]{1,0:T(8,128)S(1)}) fusion(bf16[320,640]{1,0:T(8,128)(2,1)S(1)} %shard_map.75, bf16[640,5120]{1,0:T(8,128)(2,1)S(1)} %bitcast.87), kind=kOutput, calls=%fused_computation.124 | convolution fusion | flops 2098790400 | bytes 16793600 | tf_op jit(solution)/shard_map/dot_general | solution.py:202
  116.2 4.4 %collective-permute-done.24 = bf16[64,3840]{1,0:T(8,128)(2,1)S(1)} collective-permute-done((bf16[64,3840]{1,0:T(8,128)(2,1)S(1)}, bf16[64,3840]{1,0:T(8,128)(2,1)S(1)}, u32[]{:S(2)}, u32[]{:S(2)}) %collective-permute-start.24) | collective-permute-done | bytes 491552 | tf_op jit(solution)/shard_map/ppermute | solution.py:21
  120.9 1.1 collective-permute-start.31
  122.5 1.4 collective-permute-done.27
  124.1 2.8 %collective-permute-start.33 = (bf16[64,5120]{1,0:T(8,128)(2,1)S(1)}, bf16[64,5120]{1,0:T(8,128)(2,1)S(1)}, u32[]{:S(2)}, u32[]{:S(2)}) collective-permute-start(bf16[64,5120]{1,0:T(8,128)(2,1)S(1)} %add_convert_fusion), channel_id=1, source_target_pairs={{0,4},{4,0},{1,5},{5,1},{2,6},{6,2},{3,7},{7,3},{8,12},{12,8},{9,1... | collective-permute-start | bytes 1966088 | tf_op jit(solution)/shard_map/ppermute | solution.py:21
  126.9 2.7 %collective-permute-start.30 = (bf16[64,2560]{1,0:T(8,128)(2,1)S(1)}, bf16[64,2560]{1,0:T(8,128)(2,1)S(1)}, u32[]{:S(2)}, u32[]{:S(2)}) collective-permute-start(bf16[64,2560]{1,0:T(8,128)(2,1)S(1)} %get-tuple-element.45), channel_id=1, source_target_pairs={{0,3},{1,0},{2,1},{3,2},{4,7},{5,4},{6,5},{7,6},{8,11},{9,8},{10,9... | collective-permute-start | bytes 983048 | tf_op jit(solution)/shard_map/ppermute | solution.py:21
  129.6 1.1 collective-permute-done.25
  130.9 2.7 %collective-permute-start.32 = (bf16[64,2560]{1,0:T(8,128)(2,1)S(1)}, bf16[64,2560]{1,0:T(8,128)(2,1)S(1)}, u32[]{:S(2)}, u32[]{:S(2)}) collective-permute-start(bf16[64,2560]{1,0:T(8,128)(2,1)S(1)} %get-tuple-element.47), channel_id=1, source_target_pairs={{0,3},{1,0},{2,1},{3,2},{4,7},{5,4},{6,5},{7,6},{8,11},{9,8},{10,9... | collective-permute-start | bytes 983048 | tf_op jit(solution)/shard_map/ppermute | solution.py:21
  133.6 4.3 %collective-permute-done.29 = bf16[64,2560]{1,0:T(8,128)(2,1)S(1)} collective-permute-done((bf16[64,2560]{1,0:T(8,128)(2,1)S(1)}, bf16[64,2560]{1,0:T(8,128)(2,1)S(1)}, u32[]{:S(2)}, u32[]{:S(2)}) %collective-permute-start.29) | collective-permute-done | bytes 327712 | tf_op jit(solution)/shard_map/ppermute | solution.py:21
  137.9 7.0 %collective-permute-done.26 = bf16[64,2560]{1,0:T(8,128)(2,1)S(1)} collective-permute-done((bf16[64,2560]{1,0:T(8,128)(2,1)S(1)}, bf16[64,2560]{1,0:T(8,128)(2,1)S(1)}, u32[]{:S(2)}, u32[]{:S(2)}) %collective-permute-start.26) | collective-permute-done | bytes 327712 | tf_op jit(solution)/shard_map/ppermute | solution.py:21
  145.5 17.0 %all_to_all.10 = bf16[16,4,5120]{2,1,0:T(4,128)(2,1)S(1)} all-to-all(bf16[16,4,5120]{2,1,0:T(4,128)(2,1)S(1)} %reshape.14), channel_id=1, replica_groups=mesh['xl'=2,'y'=4,'core'=2,'xh'=2,'z'=4] {'xl','y','core'}, dimensions={0} | all-to-all | bytes 1310720 | tf_op jit(solution)/shard_map/all_to_all | solution.py:224
  162.8 15.1 %all_to_all.11 = bf16[16,4,5120]{2,1,0:T(4,128)(2,1)S(1)} all-to-all(bf16[16,4,5120]{2,1,0:T(4,128)(2,1)S(1)} %reduce-window_convert_fusion), channel_id=1, replica_groups=mesh['xl'=2,'y'=4,'core'=2,'xh'=2,'z'=4] {'xl','y','core'}, dimensions={0} | all-to-all | bytes 1310720 | tf_op jit(solution)/shard_map/all_to_all | solution.py:226
  177.9 1.2 add_bitcast_fusion
  (124 shorter events, 19.5 us)
Async XLA Ops:
  0.7 4.7 %copy-start = (bf16[3,320,640]{2,1,0:T(8,128)(2,1)S(1)}, bf16[3,320,640]{2,1,0:T(8,128)(2,1)}, u32[]{:S(2)}) copy-start(bf16[3,320,640]{2,1,0:T(8,128)(2,1)} %param.12) | copy-start | bytes 3686404
  4.0 5.6 %collective-permute-start = (bf16[64,2560]{1,0:T(8,128)(2,1)}, bf16[64,2560]{1,0:T(8,128)(2,1)S(1)}, u32[]{:S(2)}, u32[]{:S(2)}) collective-permute-start(bf16[64,2560]{1,0:T(8,128)(2,1)} %get-tuple-element.28), channel_id=1, source_target_pairs={{0,8},{8,0},{1,9},{9,1},{2,10},{10,2},{3,11},{11,3},{4,12},{12,4},... | collective-permute-start | bytes 983048 | tf_op jit(solution)/shard_map/ppermute | solution.py:21
  5.4 29.2 %collective-permute-start.2 = (bf16[3,320,640]{2,1,0:T(8,128)(2,1)S(1)}, bf16[3,320,640]{2,1,0:T(8,128)(2,1)S(1)}, u32[]{:S(2)}, u32[]{:S(2)}) collective-permute-start(bf16[3,320,640]{2,1,0:T(8,128)(2,1)S(1)} %copy-done), channel_id=1, source_target_pairs={{0,48},{16,0},{32,16},{48,32},{1,49},{17,1},{33,17},{49,33},{2,50}... | collective-permute-start | bytes 3686408 | tf_op jit(solution)/shard_map/ppermute | solution.py:21
  8.2 29.5 %collective-permute-start.3 = (bf16[3,320,640]{2,1,0:T(8,128)(2,1)S(1)}, bf16[3,320,640]{2,1,0:T(8,128)(2,1)S(1)}, u32[]{:S(2)}, u32[]{:S(2)}) collective-permute-start(bf16[3,320,640]{2,1,0:T(8,128)(2,1)S(1)} %copy-done), channel_id=1, source_target_pairs={{0,16},{16,32},{32,48},{48,0},{1,17},{17,33},{33,49},{49,1},{2,18}... | collective-permute-start | bytes 3686408 | tf_op jit(solution)/shard_map/ppermute | solution.py:21
  8.3 19.6 %collective-permute-start.7 = (bf16[2,320,640]{2,1,0:T(8,128)(2,1)S(1)}, bf16[2,320,640]{2,1,0:T(8,128)(2,1)S(1)}, u32[]{:S(2)}, u32[]{:S(2)}) collective-permute-start(bf16[2,320,640]{2,1,0:T(8,128)(2,1)S(1)} %slice.214), channel_id=1, source_target_pairs={{0,64},{64,0},{1,65},{65,1},{2,66},{66,2},{3,67},{67,3},{4,68},{68... | collective-permute-start | bytes 2457608 | tf_op jit(solution)/shard_map/ppermute | solution.py:21
  10.6 20.0 %collective-permute-start.1 = (bf16[2,64,2560]{2,1,0:T(8,128)(2,1)S(1)}, bf16[2,64,2560]{2,1,0:T(8,128)(2,1)S(1)}, u32[]{:S(2)}, u32[]{:S(2)}) collective-permute-start(bf16[2,64,2560]{2,1,0:T(8,128)(2,1)S(1)} %pad_maximum_fusion.8), channel_id=1, source_target_pairs={{0,3},{1,0},{2,1},{3,2},{4,7},{5,4},{6,5},{7,6},{8,11},{9,8},{10,9... | collective-permute-start | bytes 1966088 | tf_op jit(solution)/shard_map/ppermute | solution.py:21
  14.4 16.5 %collective-permute-start.5 = (bf16[2,64,2560]{2,1,0:T(8,128)(2,1)S(1)}, bf16[2,64,2560]{2,1,0:T(8,128)(2,1)S(1)}, u32[]{:S(2)}, u32[]{:S(2)}) collective-permute-start(bf16[2,64,2560]{2,1,0:T(8,128)(2,1)S(1)} %pad_maximum_fusion.8), channel_id=1, source_target_pairs={{0,1},{1,2},{2,3},{3,0},{4,5},{5,6},{6,7},{7,4},{8,9},{9,10},{10,1... | collective-permute-start | bytes 1966088 | tf_op jit(solution)/shard_map/ppermute | solution.py:21
  27.8 16.5 %collective-permute-start.12 = (bf16[2,64,2560]{2,1,0:T(8,128)(2,1)S(1)}, bf16[2,64,2560]{2,1,0:T(8,128)(2,1)S(1)}, u32[]{:S(2)}, u32[]{:S(2)}) collective-permute-start(bf16[2,64,2560]{2,1,0:T(8,128)(2,1)S(1)} %pad_maximum_fusion.8), channel_id=1, source_target_pairs={{0,4},{4,0},{1,5},{5,1},{2,6},{6,2},{3,7},{7,3},{8,12},{12,8},{9,1... | collective-permute-start | bytes 1966088 | tf_op jit(solution)/shard_map/ppermute | solution.py:21
  31.0 21.1 %collective-permute-start.8 = (bf16[2,320,640]{2,1,0:T(8,128)(2,1)S(1)}, bf16[2,320,640]{2,1,0:T(8,128)(2,1)S(1)}, u32[]{:S(2)}, u32[]{:S(2)}) collective-permute-start(bf16[2,320,640]{2,1,0:T(8,128)(2,1)S(1)} %collective-permute-done.7), channel_id=1, source_target_pairs={{0,48},{16,0},{32,16},{48,32},{1,49},{17,1},{33,17},{49,33},{2,50}... | collective-permute-start | bytes 2457608 | tf_op jit(solution)/shard_map/ppermute | solution.py:21
  33.4 20.9 %collective-permute-start.9 = (bf16[2,320,640]{2,1,0:T(8,128)(2,1)S(1)}, bf16[2,320,640]{2,1,0:T(8,128)(2,1)S(1)}, u32[]{:S(2)}, u32[]{:S(2)}) collective-permute-start(bf16[2,320,640]{2,1,0:T(8,128)(2,1)S(1)} %collective-permute-done.7), channel_id=1, source_target_pairs={{0,16},{16,32},{32,48},{48,0},{1,17},{17,33},{33,49},{49,1},{2,18}... | collective-permute-start | bytes 2457608 | tf_op jit(solution)/shard_map/ppermute | solution.py:21
  34.6 7.0 %copy-start.2 = (bf16[3,320,640]{2,1,0:T(8,128)(2,1)}, bf16[3,320,640]{2,1,0:T(8,128)(2,1)S(1)}, u32[]{:S(2)}) copy-start(bf16[3,320,640]{2,1,0:T(8,128)(2,1)S(1)} %collective-permute-done.2) | copy-start | bytes 3686404
  37.7 14.5 %copy-start.1 = (bf16[3,320,640]{2,1,0:T(8,128)(2,1)}, bf16[3,320,640]{2,1,0:T(8,128)(2,1)S(1)}, u32[]{:S(2)}) copy-start(bf16[3,320,640]{2,1,0:T(8,128)(2,1)S(1)} %collective-permute-done.3) | copy-start | bytes 3686404
  37.7 8.8 %collective-permute-start.4 = (bf16[2,32,2560]{2,1,0:T(8,128)(2,1)S(1)}, bf16[2,32,2560]{2,1,0:T(8,128)(2,1)S(1)}, u32[]{:S(2)}, u32[]{:S(2)}) collective-permute-start(bf16[2,32,2560]{2,1,0:T(8,128)(2,1)S(1)} %slice.270), channel_id=1, source_target_pairs={{0,3},{1,0},{2,1},{3,2},{4,7},{5,4},{6,5},{7,6},{8,11},{9,8},{10,9... | collective-permute-start | bytes 983048 | tf_op jit(solution)/shard_map/ppermute | solution.py:21
  41.4 8.2 %collective-permute-start.6 = (bf16[2,32,2560]{2,1,0:T(8,128)(2,1)S(1)}, bf16[2,32,2560]{2,1,0:T(8,128)(2,1)S(1)}, u32[]{:S(2)}, u32[]{:S(2)}) collective-permute-start(bf16[2,32,2560]{2,1,0:T(8,128)(2,1)S(1)} %slice.271), channel_id=1, source_target_pairs={{0,1},{1,2},{2,3},{3,0},{4,5},{5,6},{6,7},{7,4},{8,9},{9,10},{10,1... | collective-permute-start | bytes 983048 | tf_op jit(solution)/shard_map/ppermute | solution.py:21
  42.0 9.2 %copy-start.3 = (bf16[64,2560]{1,0:T(8,128)(2,1)S(1)}, bf16[64,2560]{1,0:T(8,128)(2,1)}, u32[]{:S(2)}) copy-start(bf16[64,2560]{1,0:T(8,128)(2,1)} %get-tuple-element.27) | copy-start | bytes 983044
  44.4 34.1 %collective-permute-start.19 = (bf16[3,320,640]{2,1,0:T(8,128)(2,1)S(1)}, bf16[3,320,640]{2,1,0:T(8,128)(2,1)S(1)}, u32[]{:S(2)}, u32[]{:S(2)}) collective-permute-start(bf16[3,320,640]{2,1,0:T(8,128)(2,1)S(1)} %pad_maximum_fusion.1), channel_id=1, source_target_pairs={{0,64},{64,0},{1,65},{65,1},{2,66},{66,2},{3,67},{67,3},{4,68},{68... | collective-permute-start | bytes 3686408 | tf_op jit(solution)/shard_map/ppermute | solution.py:21
  49.6 13.1 %collective-permute-start.13 = (bf16[2,64,2560]{2,1,0:T(8,128)(2,1)S(1)}, bf16[2,64,2560]{2,1,0:T(8,128)(2,1)S(1)}, u32[]{:S(2)}, u32[]{:S(2)}) collective-permute-start(bf16[2,64,2560]{2,1,0:T(8,128)(2,1)S(1)} %collective-permute-done.12), channel_id=1, source_target_pairs={{0,3},{1,0},{2,1},{3,2},{4,7},{5,4},{6,5},{7,6},{8,11},{9,8},{10,9... | collective-permute-start | bytes 1966088 | tf_op jit(solution)/shard_map/ppermute | solution.py:21
  49.9 14.3 %collective-permute-start.14 = (bf16[2,64,2560]{2,1,0:T(8,128)(2,1)S(1)}, bf16[2,64,2560]{2,1,0:T(8,128)(2,1)S(1)}, u32[]{:S(2)}, u32[]{:S(2)}) collective-permute-start(bf16[2,64,2560]{2,1,0:T(8,128)(2,1)S(1)} %collective-permute-done.12), channel_id=1, source_target_pairs={{0,1},{1,2},{2,3},{3,0},{4,5},{5,6},{6,7},{7,4},{8,9},{9,10},{10,1... | collective-permute-start | bytes 1966088 | tf_op jit(solution)/shard_map/ppermute | solution.py:21
  54.4 1.8 %slice-start.3 = ((bf16[3,320,640]{2,1,0:T(8,128)(2,1)}), bf16[3,160,640]{2,1,0:T(8,128)(2,1)S(1)}, s32[]{:S(2)}) async-start(bf16[3,320,640]{2,1,0:T(8,128)(2,1)} %copy-done.2), calls=%async_computation.5 | async-start | bytes 1228800 | tf_op jit(solution)/shard_map/slice | solution.py:154
  56.2 1.1 slice-start.2
  56.4 27.5 %collective-permute-start.10 = (bf16[5,160,640]{2,1,0:T(8,128)(2,1)S(1)}, bf16[5,160,640]{2,1,0:T(8,128)(2,1)S(1)}, u32[]{:S(2)}, u32[]{:S(2)}) collective-permute-start(bf16[5,160,640]{2,1,0:T(8,128)(2,1)S(1)} %pad_maximum_fusion.2), channel_id=1, source_target_pairs={{0,48},{16,0},{32,16},{48,32},{1,49},{17,1},{33,17},{49,33},{2,50}... | collective-permute-start | bytes 3072008 | tf_op jit(solution)/shard_map/ppermute | solution.py:21
  57.4 26.6 %collective-permute-start.11 = (bf16[5,160,640]{2,1,0:T(8,128)(2,1)S(1)}, bf16[5,160,640]{2,1,0:T(8,128)(2,1)S(1)}, u32[]{:S(2)}, u32[]{:S(2)}) collective-permute-start(bf16[5,160,640]{2,1,0:T(8,128)(2,1)S(1)} %pad_maximum_fusion.3), channel_id=1, source_target_pairs={{0,16},{16,32},{32,48},{48,0},{1,17},{17,33},{33,49},{49,1},{2,18}... | collective-permute-start | bytes 3072008 | tf_op jit(solution)/shard_map/ppermute | solution.py:21
  64.2 6.2 %collective-permute-start.15 = (bf16[2,32,2560]{2,1,0:T(8,128)(2,1)S(1)}, bf16[2,32,2560]{2,1,0:T(8,128)(2,1)S(1)}, u32[]{:S(2)}, u32[]{:S(2)}) collective-permute-start(bf16[2,32,2560]{2,1,0:T(8,128)(2,1)S(1)} %slice.285), channel_id=1, source_target_pairs={{0,3},{1,0},{2,1},{3,2},{4,7},{5,4},{6,5},{7,6},{8,11},{9,8},{10,9... | collective-permute-start | bytes 983048 | tf_op jit(solution)/shard_map/ppermute | solution.py:21
  66.5 7.5 %collective-permute-start.16 = (bf16[2,32,2560]{2,1,0:T(8,128)(2,1)S(1)}, bf16[2,32,2560]{2,1,0:T(8,128)(2,1)S(1)}, u32[]{:S(2)}, u32[]{:S(2)}) collective-permute-start(bf16[2,32,2560]{2,1,0:T(8,128)(2,1)S(1)} %slice.286), channel_id=1, source_target_pairs={{0,1},{1,2},{2,3},{3,0},{4,5},{5,6},{6,7},{7,4},{8,9},{9,10},{10,1... | collective-permute-start | bytes 983048 | tf_op jit(solution)/shard_map/ppermute | solution.py:21
  79.8 14.5 %collective-permute-start.21 = (bf16[160,640]{1,0:T(8,128)(2,1)S(1)}, bf16[160,640]{1,0:T(8,128)(2,1)S(1)}, u32[]{:S(2)}, u32[]{:S(2)}) collective-permute-start(bf16[160,640]{1,0:T(8,128)(2,1)S(1)} %get-tuple-element.38), channel_id=1, source_target_pairs={{0,16},{16,32},{32,48},{48,0},{1,17},{17,33},{33,49},{49,1},{2,18}... | collective-permute-start | bytes 614408 | tf_op jit(solution)/shard_map/ppermute | solution.py:21
  80.0 14.4 %collective-permute-start.20 = (bf16[160,640]{1,0:T(8,128)(2,1)S(1)}, bf16[160,640]{1,0:T(8,128)(2,1)S(1)}, u32[]{:S(2)}, u32[]{:S(2)}) collective-permute-start(bf16[160,640]{1,0:T(8,128)(2,1)S(1)} %get-tuple-element.37), channel_id=1, source_target_pairs={{0,48},{16,0},{32,16},{48,32},{1,49},{17,1},{33,17},{49,33},{2,50}... | collective-permute-start | bytes 614408 | tf_op jit(solution)/shard_map/ppermute | solution.py:21
  87.9 8.7 %collective-permute-start.17 = (bf16[512,640]{1,0:T(8,128)(2,1)S(1)}, bf16[512,640]{1,0:T(8,128)(2,1)S(1)}, u32[]{:S(2)}, u32[]{:S(2)}) collective-permute-start(bf16[512,640]{1,0:T(8,128)(2,1)S(1)} %pad_maximum_fusion.9), channel_id=1, source_target_pairs={{0,8},{8,0},{1,9},{9,1},{2,10},{10,2},{3,11},{11,3},{4,12},{12,4},... | collective-permute-start | bytes 1966088 | tf_op jit(solution)/shard_map/ppermute | solution.py:21
  94.0 2.6 %collective-permute-start.18 = (bf16[512,640]{1,0:T(8,128)(2,1)S(1)}, bf16[512,640]{1,0:T(8,128)(2,1)S(1)}, u32[]{:S(2)}, u32[]{:S(2)}) collective-permute-start(bf16[512,640]{1,0:T(8,128)(2,1)S(1)} %pad_maximum_fusion.10), channel_id=1, source_target_pairs={{0,8},{8,0},{1,9},{9,1},{2,10},{10,2},{3,11},{11,3},{4,12},{12,4},... | collective-permute-start | bytes 1966088 | tf_op jit(solution)/shard_map/ppermute | solution.py:21
  95.9 6.1 %slice-start = ((s8[6553600]{0:T(1024)(128)(4,1)}), s8[4194304]{0:T(1024)(128)(4,1)S(1)}, s32[]{:S(2)}) async-start(s8[6553600]{0:T(1024)(128)(4,1)} %bitcast.86), calls=%async_computation.2 | async-start | bytes 8388608
  96.0 6.0 %slice-start.1 = ((s8[6553600]{0:T(1024)(128)(4,1)}), s8[2359296]{0:T(1024)(128)(4,1)S(1)}, s32[]{:S(2)}) async-start(s8[6553600]{0:T(1024)(128)(4,1)} %bitcast.86), calls=%async_computation.3 | async-start | bytes 4718592
  96.0 2.3 %collective-permute-start.22 = (bf16[512,640]{1,0:T(8,128)(2,1)S(1)}, bf16[512,640]{1,0:T(8,128)(2,1)S(1)}, u32[]{:S(2)}, u32[]{:S(2)}) collective-permute-start(bf16[512,640]{1,0:T(8,128)(2,1)S(1)} %pad_maximum_fusion.11), channel_id=1, source_target_pairs={{0,8},{8,0},{1,9},{9,1},{2,10},{10,2},{3,11},{11,3},{4,12},{12,4},... | collective-permute-start | bytes 1966088 | tf_op jit(solution)/shard_map/ppermute | solution.py:21
  103.8 7.0 %collective-permute-start.23 = (bf16[64,1280]{1,0:T(8,128)(2,1)S(1)}, bf16[64,1280]{1,0:T(8,128)(2,1)S(1)}, u32[]{:S(2)}, u32[]{:S(2)}) collective-permute-start(bf16[64,1280]{1,0:T(8,128)(2,1)S(1)} %slice.314), channel_id=1, source_target_pairs={{0,4},{4,0},{1,5},{5,1},{2,6},{6,2},{3,7},{7,3},{8,12},{12,8},{9,1... | collective-permute-start | bytes 491528 | tf_op jit(solution)/shard_map/ppermute | solution.py:21
  106.7 15.7 %collective-permute-start.28 = (bf16[64,5120]{1,0:T(8,128)(2,1)S(1)}, bf16[64,5120]{1,0:T(8,128)(2,1)S(1)}, u32[]{:S(2)}, u32[]{:S(2)}) collective-permute-start(bf16[64,5120]{1,0:T(8,128)(2,1)S(1)} %get-tuple-element.59), channel_id=1, source_target_pairs={{0,3},{1,0},{2,1},{3,2},{4,7},{5,4},{6,5},{7,6},{8,11},{9,8},{10,9... | collective-permute-start | bytes 1966088 | tf_op jit(solution)/shard_map/ppermute | solution.py:21
  107.4 13.3 %collective-permute-start.24 = (bf16[64,3840]{1,0:T(8,128)(2,1)S(1)}, bf16[64,3840]{1,0:T(8,128)(2,1)S(1)}, u32[]{:S(2)}, u32[]{:S(2)}) collective-permute-start(bf16[64,3840]{1,0:T(8,128)(2,1)S(1)} %slice.318), channel_id=1, source_target_pairs={{0,4},{4,0},{1,5},{5,1},{2,6},{6,2},{3,7},{7,3},{8,12},{12,8},{9,1... | collective-permute-start | bytes 1474568 | tf_op jit(solution)/shard_map/ppermute | solution.py:21
  107.6 16.2 %collective-permute-start.27 = (bf16[64,5120]{1,0:T(8,128)(2,1)S(1)}, bf16[64,5120]{1,0:T(8,128)(2,1)S(1)}, u32[]{:S(2)}, u32[]{:S(2)}) collective-permute-start(bf16[64,5120]{1,0:T(8,128)(2,1)S(1)} %get-tuple-element.58), channel_id=1, source_target_pairs={{0,1},{1,2},{2,3},{3,0},{4,5},{5,6},{6,7},{7,4},{8,9},{9,10},{10,1... | collective-permute-start | bytes 1966088 | tf_op jit(solution)/shard_map/ppermute | solution.py:21
  120.9 8.7 %collective-permute-start.31 = (bf16[64,2560]{1,0:T(8,128)(2,1)S(1)}, bf16[64,2560]{1,0:T(8,128)(2,1)S(1)}, u32[]{:S(2)}, u32[]{:S(2)}) collective-permute-start(bf16[64,2560]{1,0:T(8,128)(2,1)S(1)} %get-tuple-element.83), channel_id=1, source_target_pairs={{0,3},{1,0},{2,1},{3,2},{4,7},{5,4},{6,5},{7,6},{8,11},{9,8},{10,9... | collective-permute-start | bytes 983048 | tf_op jit(solution)/shard_map/ppermute | solution.py:21
  122.0 8.7 %collective-permute-start.25 = (bf16[64,2560]{1,0:T(8,128)(2,1)S(1)}, bf16[64,2560]{1,0:T(8,128)(2,1)S(1)}, u32[]{:S(2)}, u32[]{:S(2)}) collective-permute-start(bf16[64,2560]{1,0:T(8,128)(2,1)S(1)} %get-tuple-element.84), channel_id=1, source_target_pairs={{0,1},{1,2},{2,3},{3,0},{4,5},{5,6},{6,7},{7,4},{8,9},{9,10},{10,1... | collective-permute-start | bytes 983048 | tf_op jit(solution)/shard_map/ppermute | solution.py:21
  124.1 20.9 %copy-start.5 = (f32[1,5120]{1,0:T(1,128)S(1)}, f32[1,5120]{1,0:T(1,128)}, u32[]{:S(2)}) copy-start(f32[1,5120]{1,0:T(1,128)} %get-tuple-element.26) | copy-start | bytes 61444
  124.1 20.8 %collective-permute-start.33 = (bf16[64,5120]{1,0:T(8,128)(2,1)S(1)}, bf16[64,5120]{1,0:T(8,128)(2,1)S(1)}, u32[]{:S(2)}, u32[]{:S(2)}) collective-permute-start(bf16[64,5120]{1,0:T(8,128)(2,1)S(1)} %add_convert_fusion), channel_id=1, source_target_pairs={{0,4},{4,0},{1,5},{5,1},{2,6},{6,2},{3,7},{7,3},{8,12},{12,8},{9,1... | collective-permute-start | bytes 1966088 | tf_op jit(solution)/shard_map/ppermute | solution.py:21
  126.9 11.0 %collective-permute-start.29 = (bf16[64,2560]{1,0:T(8,128)(2,1)S(1)}, bf16[64,2560]{1,0:T(8,128)(2,1)S(1)}, u32[]{:S(2)}, u32[]{:S(2)}) collective-permute-start(bf16[64,2560]{1,0:T(8,128)(2,1)S(1)} %get-tuple-element.44), channel_id=1, source_target_pairs={{0,1},{1,2},{2,3},{3,0},{4,5},{5,6},{6,7},{7,4},{8,9},{9,10},{10,1... | collective-permute-start | bytes 983048 | tf_op jit(solution)/shard_map/ppermute | solution.py:21
  126.9 11.0 %collective-permute-start.30 = (bf16[64,2560]{1,0:T(8,128)(2,1)S(1)}, bf16[64,2560]{1,0:T(8,128)(2,1)S(1)}, u32[]{:S(2)}, u32[]{:S(2)}) collective-permute-start(bf16[64,2560]{1,0:T(8,128)(2,1)S(1)} %get-tuple-element.45), channel_id=1, source_target_pairs={{0,3},{1,0},{2,1},{3,2},{4,7},{5,4},{6,5},{7,6},{8,11},{9,8},{10,9... | collective-permute-start | bytes 983048 | tf_op jit(solution)/shard_map/ppermute | solution.py:21
  130.9 14.1 %collective-permute-start.26 = (bf16[64,2560]{1,0:T(8,128)(2,1)S(1)}, bf16[64,2560]{1,0:T(8,128)(2,1)S(1)}, u32[]{:S(2)}, u32[]{:S(2)}) collective-permute-start(bf16[64,2560]{1,0:T(8,128)(2,1)S(1)} %get-tuple-element.48), channel_id=1, source_target_pairs={{0,1},{1,2},{2,3},{3,0},{4,5},{5,6},{6,7},{7,4},{8,9},{9,10},{10,1... | collective-permute-start | bytes 983048 | tf_op jit(solution)/shard_map/ppermute | solution.py:21
  130.9 14.0 %collective-permute-start.32 = (bf16[64,2560]{1,0:T(8,128)(2,1)S(1)}, bf16[64,2560]{1,0:T(8,128)(2,1)S(1)}, u32[]{:S(2)}, u32[]{:S(2)}) collective-permute-start(bf16[64,2560]{1,0:T(8,128)(2,1)S(1)} %get-tuple-element.47), channel_id=1, source_target_pairs={{0,3},{1,0},{2,1},{3,2},{4,7},{5,4},{6,5},{7,6},{8,11},{9,8},{10,9... | collective-permute-start | bytes 983048 | tf_op jit(solution)/shard_map/ppermute | solution.py:21
  162.5 15.4 %copy-start.4 = (f32[64,5120]{1,0:T(8,128)S(1)}, f32[64,5120]{1,0:T(8,128)}, u32[]{:S(2)}) copy-start(f32[64,5120]{1,0:T(8,128)} %param.8) | copy-start | bytes 3932164

commit v5 on v4

--- a/solution.py
+++ b/solution.py
@@ -93,38 +93,49 @@
     ).astype(BF16)
 
 
-def first_kernel(head, q0, q1, qb, k0, k1, kb, v0, v1, vb, query_ref, keys_ref, values_ref, out_ref):
-    half = q0.shape[0]
-    for dx, (q, k, v) in enumerate(((q0, k0, v0), (q1, k1, v1))):
-        rows = slice(dx * half, (dx + 1) * half)
-        query_ref[rows] = normed(q[...] + qb[rows].astype(F32))
-        keys_ref[rows] = normed(k[...] + kb[rows].astype(F32))
-        values_ref[rows] = (v[...] + vb[rows].astype(F32)).astype(BF16)
-    out_ref[...] = attend(query_ref[half : half + head], keys_ref[...], values_ref[...])
+def first_kernel(head, q, qb, k, kb, v, vb, query_ref, keys_ref, values_ref, out_ref):
+    half = v.shape[0] // 2
+    for h in range(v.shape[1] // HEAD_DIM):
+        at = slice(h * HEAD_DIM, (h + 1) * HEAD_DIM)
+        query = normed(q[:, at] + qb[:, at].astype(F32))
+        keys = normed(k[:, at] + kb[:, at].astype(F32))
+        values = (v[:, at] + vb[:, at].astype(F32)).astype(BF16)
+        query_ref[:, at], keys_ref[:, at], values_ref[:, at] = query, keys, values
+        out_ref[:, at] = attend(query[half : half + head], keys, values)
 
 
 def second_kernel(head, query_ref, keys_ref, values_ref, out_ref):
     half = query_ref.shape[0] // 2
-    query = jnp.concatenate([query_ref[:half], query_ref[half + head :]], axis=0)
-    out_ref[...] = attend(query, keys_ref[...], values_ref[...])
-
-
-def attention_call(kernel, operands, heights, shapes):
-    count, width = operands[-1].shape
-
-    def spec(rows):
-        return pl.BlockSpec((rows, HEAD_DIM), lambda h: (0, h))
-
+    for h in range(query_ref.shape[1] // HEAD_DIM):
+        at = slice(h * HEAD_DIM, (h + 1) * HEAD_DIM)
+        query = jnp.concatenate([query_ref[:half, at], query_ref[half + head :, at]], axis=0)
+        out_ref[:, at] = attend(query, keys_ref[:, at], values_ref[:, at])
+
+
+def last_kernel(matrices, f0, f1, far, extra, *refs):
+    rows, count = far.shape[1], f0.shape[0]
+    half, each = count // 2, len(matrices)
+    for i, j in enumerate(matrices):
+        mate = far[3 + j] if j < 2 else extra[...]
+        weight = jnp.concatenate([far[j], mate], axis=0)
+        own_ref, mate_ref = refs[2 * each + 2 * i : 2 * each + 2 * i + 2]
+        for dx, f in enumerate((f0, f1)):
+            total = refs[2 * i + dx][...] + jnp.dot(
+                f[:, 6 * rows :], weight, preferred_element_type=F32
+            )
+            own_ref[dx * half : (dx + 1) * half] = total[:half]
+            mate_ref[dx * half : (dx + 1) * half] = total[half:].astype(BF16)
+
+
+def local_call(kernel, operands, shapes, flops):
+    whole = pl.BlockSpec(memory_space=pltpu.VMEM)
     return pl.pallas_call(
         kernel,
-        out_shape=[jax.ShapeDtypeStruct((rows, width), BF16) for rows in shapes],
-        grid=(width // HEAD_DIM,),
-        in_specs=[spec(rows) for rows in heights],
-        out_specs=[spec(rows) for rows in shapes],
-        compiler_params=pltpu.CompilerParams(vmem_limit_bytes=16 * 1024 * 1024),
-        cost_estimate=pl.CostEstimate(
-            flops=4 * shapes[-1] * count * width, bytes_accessed=8 * count * width, transcendentals=0
-        ),
+        out_shape=[jax.ShapeDtypeStruct(*shape) for shape in shapes],
+        in_specs=[whole] * len(operands),
+        out_specs=[whole] * len(shapes),
+        compiler_params=pltpu.CompilerParams(vmem_limit_bytes=24 * 1024 * 1024),
+        cost_estimate=pl.CostEstimate(flops=flops, bytes_accessed=1000, transcendentals=0),
     )(*operands)
 
 
@@ -178,26 +189,31 @@
     begun = [[held(x) for x in product(0, [own[j], a1[j], p[j], pa[j], b1[j], pb[j]])] for j in range(2)]
     begun.append([held(x) for x in product(0, [own[2], a1[2]])])
     begun[2] = [held(x) for x in plus(begun[2], product(2 * rows, [xv[0], xv[1], b1[2], xv[2]]))]
-    last = [[far[0], far[3]], [far[1], far[4]], [far[2], vfar]]
-    begun = [plus(x, product(6 * rows, blocks)) for x, blocks in zip(begun, last)]
-    parts = []
-    for j in range(3):
-        mates = jnp.concatenate([x[count // 2 :] for x in begun[j]], axis=0).astype(BF16)
-        parts += [*begun[j], send(mates, "core", 1)]
-
-    cut, half, head = width // 2, count // 2, 3 * tokens
-    query, keys, values, attended = attention_call(
-        functools.partial(first_kernel, head), parts, (half, half, count) * 3,
-        (count, count, count, head),
+    columns = wqkv.shape[2]
+    one = (count, columns)
+    q, q_mates, k, k_mates = local_call(
+        functools.partial(last_kernel, (0, 1)), (*features, far, far, *begun[0], *begun[1]),
+        [(one, F32), (one, BF16)] * 2, 1000,
+    )
+    v, v_mates = local_call(
+        functools.partial(last_kernel, (2,)), (*features, far, vfar, *begun[2]),
+        [(one, F32), (one, BF16)], 8 * count * rows * columns,
+    )
+    parts = (q, send(q_mates, "core", 1), k, send(k_mates, "core", 1), v, send(v_mates, "core", 1))
+
+    cut, head = width // 2, 3 * tokens
+    query, keys, values, attended = local_call(
+        functools.partial(first_kernel, head), parts, [(one, BF16)] * 3 + [((head, columns), BF16)],
+        4 * head * count * columns,
     )
     first = jnp.dot(attended, wo, preferred_element_type=F32).astype(BF16)
     far1, above1, below1 = (first[i * tokens : (i + 1) * tokens] for i in range(3))
     up1, down1 = send(above1, "z", 1), send(below1, "z", -1)
     quarter = cut // 2
     joins = [send(far1[:, :quarter], "xh", 1), send(far1[:, quarter:], "xh", 1)]
-    (attended,) = attention_call(
+    (attended,) = local_call(
         functools.partial(second_kernel, head), (after(query, joins[0]), keys, values),
-        (count,) * 3, (count - head,),
+        [((count - head, columns), BF16)], 4 * (count - head) * count * columns,
     )
     rest = jnp.dot(attended, wo, preferred_element_type=F32)
     far0, above0, below0, near0, near1 = (rest[i * tokens : (i + 1) * tokens] for i in range(5))

time: 179 us -> 175 us (0.978)
  matrix products: 19.8 us -> 15.3 us
    dot_general x14 -> x8, matrix products: 15.4 us -> 10.9 us  [product(): jnp.dot(f[:, begin:stop], weight, preferred_element_type=F32)]
    pallas_call x2 -> x4, Pallas kernels: 6.36 us -> 6.45 us  [local_call(): pl.pallas_call(kernel, out_shape=[jax.ShapeDtypeStruct(*shape) for shape...]
  transfers between devices with their start and end apart: 34 -> 34, of which waited for: 19 -> 20; matrix products, arithmetic and copies ran while one was open for 13% -> 10% of each run, Pallas kernels for 2% -> 3%
where the time goes in v5:
time: 175 us
  waiting for transfers between devices  61.6 us (35%)
  starting transfers between devices  48.4 us (28%)
  blocking collectives  31.7 us (18%)
  matrix products  15.3 us (9%)
  Pallas kernels  9.64 us (6%)
  other arithmetic  4.03 us (2%)
  local copies, waits for them, and re-layouts  2.67 us (2%)
    ppermute x34, waiting for transfers between devices, send(): lax.ppermute(array, axis, [(i, (i + shift) % size) for i in range(size)])  61.6 us
    ppermute x34, starting transfers between devices, send(): lax.ppermute(array, axis, [(i, (i + shift) % size) for i in range(size)])  48.4 us
    all_to_all x1, blocking collectives, on_device(): lax.all_to_all(term.reshape(steps, tokens // steps, width), TM, 0, 0)  16.7 us
    all_to_all x1, blocking collectives, on_device(): total = lax.all_to_all(total, TM, 0, 0).reshape(tokens, width)  15.1 us
    dot_general x8, matrix products, product(): jnp.dot(f[:, begin:stop], weight, preferred_element_type=F32)  10.9 us
    pallas_call x4, Pallas kernels, local_call(): pl.pallas_call(kernel, out_shape=[jax.ShapeDtypeStruct(*shape) for shape...  6.45 us
  transfers between devices with their start and end apart: 34, of which 20 were waited for; matrix products, arithmetic and copies ran while one was open for 10% of the time, Pallas kernels for 3%

profile of v5, /device:TPU:1, one launch (start us, length us, event | category | flops | bytes accessed | tf_op | source)
XLA Modules:
  0.0 174.8 jit_solution(13113801484246128076)
XLA Ops:
  0.8 3.2 %shard_map.73 = (bf16[64,2560]{1,0:T(8,128)(2,1)}, bf16[64,2560]{1,0:T(8,128)(2,1)}, f32[1,5120]{1,0:T(1,128)}) custom-call(s32[1]{0:T(128)S(6)} %copy.27.t_ref, f32[1,64,5120]{2,1,0:T(8,128)} %state_ref.1, f32[3,50,5120]{2,1,0:T(8,128)} %bitcast.90, f32[50]{0:T(128)} %coef_ref.1), custom_call_target="tpu_custom_call" | custom-call | flops 1000 | bytes 1000 | tf_op jit(solution)/shard_map/pallas_call | solution.py:60
  3.9 1.4 collective-permute-start
  5.4 2.8 %collective-permute-start.2 = (bf16[3,320,640]{2,1,0:T(8,128)(2,1)S(1)}, bf16[3,320,640]{2,1,0:T(8,128)(2,1)S(1)}, u32[]{:S(2)}, u32[]{:S(2)}) collective-permute-start(bf16[3,320,640]{2,1,0:T(8,128)(2,1)S(1)} %copy-done), channel_id=1, source_target_pairs={{0,48},{16,0},{32,16},{48,32},{1,49},{17,1},{33,17},{49,33},{2,50}... | collective-permute-start | bytes 3686408 | tf_op jit(solution)/shard_map/ppermute | solution.py:21
  8.3 1.3 collective-permute-start.7
  10.6 3.8 %collective-permute-start.1 = (bf16[2,64,2560]{2,1,0:T(8,128)(2,1)S(1)}, bf16[2,64,2560]{2,1,0:T(8,128)(2,1)S(1)}, u32[]{:S(2)}, u32[]{:S(2)}) collective-permute-start(bf16[2,64,2560]{2,1,0:T(8,128)(2,1)S(1)} %pad_maximum_fusion.5), channel_id=1, source_target_pairs={{0,3},{1,0},{2,1},{3,2},{4,7},{5,4},{6,5},{7,6},{8,11},{9,8},{10,9... | collective-permute-start | bytes 1966088 | tf_op jit(solution)/shard_map/ppermute | solution.py:21
  14.6 13.2 %collective-permute-done.7 = bf16[2,320,640]{2,1,0:T(8,128)(2,1)S(1)} collective-permute-done((bf16[2,320,640]{2,1,0:T(8,128)(2,1)S(1)}, bf16[2,320,640]{2,1,0:T(8,128)(2,1)S(1)}, u32[]{:S(2)}, u32[]{:S(2)}) %collective-permute-start.7) | collective-permute-done | bytes 819232 | tf_op jit(solution)/shard_map/ppermute | solution.py:21
  27.8 2.7 %collective-permute-start.8 = (bf16[2,64,2560]{2,1,0:T(8,128)(2,1)S(1)}, bf16[2,64,2560]{2,1,0:T(8,128)(2,1)S(1)}, u32[]{:S(2)}, u32[]{:S(2)}) collective-permute-start(bf16[2,64,2560]{2,1,0:T(8,128)(2,1)S(1)} %pad_maximum_fusion.5), channel_id=1, source_target_pairs={{0,4},{4,0},{1,5},{5,1},{2,6},{6,2},{3,7},{7,3},{8,12},{12,8},{9,1... | collective-permute-start | bytes 1966088 | tf_op jit(solution)/shard_map/ppermute | solution.py:21
  31.0 2.4 %collective-permute-start.13 = (bf16[2,320,640]{2,1,0:T(8,128)(2,1)S(1)}, bf16[2,320,640]{2,1,0:T(8,128)(2,1)S(1)}, u32[]{:S(2)}, u32[]{:S(2)}) collective-permute-start(bf16[2,320,640]{2,1,0:T(8,128)(2,1)S(1)} %collective-permute-done.7), channel_id=1, source_target_pairs={{0,48},{16,0},{32,16},{48,32},{1,49},{17,1},{33,17},{49,33},{2,50}... | collective-permute-start | bytes 2457608 | tf_op jit(solution)/shard_map/ppermute | solution.py:21
  33.4 1.2 collective-permute-done.2
  34.6 3.1 %collective-permute-done.3 = bf16[3,320,640]{2,1,0:T(8,128)(2,1)S(1)} collective-permute-done((bf16[3,320,640]{2,1,0:T(8,128)(2,1)S(1)}, bf16[3,320,640]{2,1,0:T(8,128)(2,1)S(1)}, u32[]{:S(2)}, u32[]{:S(2)}) %collective-permute-start.3) | collective-permute-done | bytes 1228832 | tf_op jit(solution)/shard_map/ppermute | solution.py:21
  37.7 3.8 %collective-permute-start.4 = (bf16[2,32,2560]{2,1,0:T(8,128)(2,1)S(1)}, bf16[2,32,2560]{2,1,0:T(8,128)(2,1)S(1)}, u32[]{:S(2)}, u32[]{:S(2)}) collective-permute-start(bf16[2,32,2560]{2,1,0:T(8,128)(2,1)S(1)} %slice.208), channel_id=1, source_target_pairs={{0,3},{1,0},{2,1},{3,2},{4,7},{5,4},{6,5},{7,6},{8,11},{9,8},{10,9... | collective-permute-start | bytes 983048 | tf_op jit(solution)/shard_map/ppermute | solution.py:21
  42.0 2.3 %collective-permute-done.8 = bf16[2,64,2560]{2,1,0:T(8,128)(2,1)S(1)} collective-permute-done((bf16[2,64,2560]{2,1,0:T(8,128)(2,1)S(1)}, bf16[2,64,2560]{2,1,0:T(8,128)(2,1)S(1)}, u32[]{:S(2)}, u32[]{:S(2)}) %collective-permute-start.8) | collective-permute-done | bytes 655392 | tf_op jit(solution)/shard_map/ppermute | solution.py:21
  44.4 1.2 collective-permute-start.19
  46.5 3.1 %collective-permute-done.6 = bf16[2,32,2560]{2,1,0:T(8,128)(2,1)S(1)} collective-permute-done((bf16[2,32,2560]{2,1,0:T(8,128)(2,1)S(1)}, bf16[2,32,2560]{2,1,0:T(8,128)(2,1)S(1)}, u32[]{:S(2)}, u32[]{:S(2)}) %collective-permute-start.6) | collective-permute-done | bytes 327712 | tf_op jit(solution)/shard_map/ppermute | solution.py:21
  49.9 1.2 collective-permute-start.10
  52.4 2.4 %collective-permute-start.14 = (bf16[5,160,640]{2,1,0:T(8,128)(2,1)S(1)}, bf16[5,160,640]{2,1,0:T(8,128)(2,1)S(1)}, u32[]{:S(2)}, u32[]{:S(2)}) collective-permute-start(bf16[5,160,640]{2,1,0:T(8,128)(2,1)S(1)} %pad_maximum_fusion.2), channel_id=1, source_target_pairs={{0,48},{16,0},{32,16},{48,32},{1,49},{17,1},{33,17},{49,33},{2,50}... | collective-permute-start | bytes 3072008 | tf_op jit(solution)/shard_map/ppermute | solution.py:21
  55.5 1.8 %fusion.6.refs_0_ = f32[512,640]{1,0:T(8,128)S(1)} fusion(bf16[1920,640]{1,0:T(8,128)(2,1)S(1)} %get-tuple-element.85, bf16[512,2560]{1,0:T(8,128)(2,1)S(1)} %bitcast.83), kind=kOutput, calls=%fused_computation.8 | convolution fusion | flops 1258291200 | bytes 5734400 | tf_op jit(solution)/shard_map/dot_general | solution.py:183
  57.2 5.4 %collective-permute-done.9 = bf16[2,64,2560]{2,1,0:T(8,128)(2,1)S(1)} collective-permute-done((bf16[2,64,2560]{2,1,0:T(8,128)(2,1)S(1)}, bf16[2,64,2560]{2,1,0:T(8,128)(2,1)S(1)}, u32[]{:S(2)}, u32[]{:S(2)}) %collective-permute-start.9) | collective-permute-done | bytes 655392 | tf_op jit(solution)/shard_map/ppermute | solution.py:21
  62.7 1.5 collective-permute-done.10
  64.7 1.8 %fusion.4.refs_2_ = f32[512,640]{1,0:T(8,128)S(1)} fusion(bf16[1920,640]{1,0:T(8,128)(2,1)S(1)} %get-tuple-element.84, bf16[512,2560]{1,0:T(8,128)(2,1)S(1)} %bitcast.84), kind=kOutput, calls=%fused_computation.6 | convolution fusion | flops 1258291200 | bytes 5734400 | tf_op jit(solution)/shard_map/dot_general | solution.py:183
  67.5 2.9 %collective-permute-done.11 = bf16[2,32,2560]{2,1,0:T(8,128)(2,1)S(1)} collective-permute-done((bf16[2,32,2560]{2,1,0:T(8,128)(2,1)S(1)}, bf16[2,32,2560]{2,1,0:T(8,128)(2,1)S(1)}, u32[]{:S(2)}, u32[]{:S(2)}) %collective-permute-start.11) | collective-permute-done | bytes 327712 | tf_op jit(solution)/shard_map/ppermute | solution.py:21
  70.4 3.6 %collective-permute-done.12 = bf16[2,32,2560]{2,1,0:T(8,128)(2,1)S(1)} collective-permute-done((bf16[2,32,2560]{2,1,0:T(8,128)(2,1)S(1)}, bf16[2,32,2560]{2,1,0:T(8,128)(2,1)S(1)}, u32[]{:S(2)}, u32[]{:S(2)}) %collective-permute-start.12) | collective-permute-done | bytes 327712 | tf_op jit(solution)/shard_map/ppermute | solution.py:21
  74.2 1.8 %fusion.2.refs_1_ = f32[512,640]{1,0:T(8,128)S(1)} fusion(bf16[1920,640]{1,0:T(8,128)(2,1)S(1)} %get-tuple-element.85, bf16[512,2560]{1,0:T(8,128)(2,1)S(1)} %bitcast.76), kind=kOutput, calls=%fused_computation.4 | convolution fusion | flops 1258291200 | bytes 5734400 | tf_op jit(solution)/shard_map/dot_general | solution.py:183
  75.9 1.8 %fusion.refs_3_ = f32[512,640]{1,0:T(8,128)S(1)} fusion(bf16[1920,640]{1,0:T(8,128)(2,1)S(1)} %get-tuple-element.84, bf16[512,2560]{1,0:T(8,128)(2,1)S(1)} %bitcast.77), kind=kOutput, calls=%fused_computation.2 | convolution fusion | flops 1258291200 | bytes 5734400 | tf_op jit(solution)/shard_map/dot_general | solution.py:183
  78.7 2.6 %collective-permute-start.20 = (bf16[160,640]{1,0:T(8,128)(2,1)S(1)}, bf16[160,640]{1,0:T(8,128)(2,1)S(1)}, u32[]{:S(2)}, u32[]{:S(2)}) collective-permute-start(bf16[160,640]{1,0:T(8,128)(2,1)S(1)} %get-tuple-element.47), channel_id=1, source_target_pairs={{0,48},{16,0},{32,16},{48,32},{1,49},{17,1},{33,17},{49,33},{2,50}... | collective-permute-start | bytes 614408 | tf_op jit(solution)/shard_map/ppermute | solution.py:21
  81.4 1.2 convolution_add_fusion.refs_0_
  82.6 1.2 fusion.13
  84.2 2.5 %shard_map.74 = (f32[512,640]{1,0:T(8,128)S(1)}, bf16[512,640]{1,0:T(8,128)(2,1)S(1)}, f32[512,640]{1,0:T(8,128)S(1)}, bf16[512,640]{1,0:T(8,128)(2,1)S(1)}) custom-call(bf16[512,2560]{1,0:T(8,128)(2,1)S(1)} %bitcast.86, bf16[512,2560]{1,0:T(8,128)(2,1)S(1)} %bitcast.80, bf16[5,320,640]{2,1,0:T(8,128)(2,1)S(1)} %constant_dynamic-update-slice_fusion.10.far.extra, ...), custom_call_target="tpu_custom_call" | custom-call | flops 1000 | bytes 1000 | tf_op jit(solution)/shard_map/pallas_call | solution.py:132
  86.7 5.6 %collective-permute-start.17 = (bf16[512,640]{1,0:T(8,128)(2,1)S(1)}, bf16[512,640]{1,0:T(8,128)(2,1)S(1)}, u32[]{:S(2)}, u32[]{:S(2)}) collective-permute-start(bf16[512,640]{1,0:T(8,128)(2,1)S(1)} %get-tuple-element.43), channel_id=1, source_target_pairs={{0,8},{8,0},{1,9},{9,1},{2,10},{10,2},{3,11},{11,3},{4,12},{12,4},... | collective-permute-start | bytes 1966088 | tf_op jit(solution)/shard_map/ppermute | solution.py:21
  92.5 1.3 shard_map.75
  95.0 1.3 collective-permute-done.22.vb
  96.3 1.5 shard_map.76
  97.8 1.7 convolution_convert_fusion
  99.5 2.8 %collective-permute-start.23 = (bf16[64,1280]{1,0:T(8,128)(2,1)S(1)}, bf16[64,1280]{1,0:T(8,128)(2,1)S(1)}, u32[]{:S(2)}, u32[]{:S(2)}) collective-permute-start(bf16[64,1280]{1,0:T(8,128)(2,1)S(1)} %slice.239), channel_id=1, source_target_pairs={{0,4},{4,0},{1,5},{5,1},{2,6},{6,2},{3,7},{7,3},{8,12},{12,8},{9,1... | collective-permute-start | bytes 491528 | tf_op jit(solution)/shard_map/ppermute | solution.py:21
  102.9 1.4 collective-permute-start.27
  104.3 2.3 %collective-permute-done.23 = bf16[64,1280]{1,0:T(8,128)(2,1)S(1)} collective-permute-done((bf16[64,1280]{1,0:T(8,128)(2,1)S(1)}, bf16[64,1280]{1,0:T(8,128)(2,1)S(1)}, u32[]{:S(2)}, u32[]{:S(2)}) %collective-permute-start.23) | collective-permute-done | bytes 163872 | tf_op jit(solution)/shard_map/ppermute | solution.py:21
  107.7 2.7 %fusion.40 = (bf16[320,5120]{1,0:T(8,128)(2,1)S(1)}, f32[320,5120]{1,0:T(8,128)S(1)}) fusion(bf16[320,640]{1,0:T(8,128)(2,1)S(1)} %shard_map.77, bf16[640,5120]{1,0:T(8,128)(2,1)S(1)} %bitcast.89), kind=kOutput, calls=%fused_computation.88 | convolution fusion | flops 2098790400 | bytes 16793600 | tf_op jit(solution)/shard_map/dot_general | solution.py:218
  110.4 6.8 %collective-permute-done.24 = bf16[64,3840]{1,0:T(8,128)(2,1)S(1)} collective-permute-done((bf16[64,3840]{1,0:T(8,128)(2,1)S(1)}, bf16[64,3840]{1,0:T(8,128)(2,1)S(1)}, u32[]{:S(2)}, u32[]{:S(2)}) %collective-permute-start.24) | collective-permute-done | bytes 491552 | tf_op jit(solution)/shard_map/ppermute | solution.py:21
  117.5 1.4 collective-permute-start.25
  119.6 2.8 %collective-permute-start.33 = (bf16[64,5120]{1,0:T(8,128)(2,1)S(1)}, bf16[64,5120]{1,0:T(8,128)(2,1)S(1)}, u32[]{:S(2)}, u32[]{:S(2)}) collective-permute-start(bf16[64,5120]{1,0:T(8,128)(2,1)S(1)} %add_convert_fusion), channel_id=1, source_target_pairs={{0,4},{4,0},{1,5},{5,1},{2,6},{6,2},{3,7},{7,3},{8,12},{12,8},{9,1... | collective-permute-start | bytes 1966088 | tf_op jit(solution)/shard_map/ppermute | solution.py:21
  122.5 2.7 %collective-permute-start.30 = (bf16[64,2560]{1,0:T(8,128)(2,1)S(1)}, bf16[64,2560]{1,0:T(8,128)(2,1)S(1)}, u32[]{:S(2)}, u32[]{:S(2)}) collective-permute-start(bf16[64,2560]{1,0:T(8,128)(2,1)S(1)} %get-tuple-element.57), channel_id=1, source_target_pairs={{0,3},{1,0},{2,1},{3,2},{4,7},{5,4},{6,5},{7,6},{8,11},{9,8},{10,9... | collective-permute-start | bytes 983048 | tf_op jit(solution)/shard_map/ppermute | solution.py:21
  125.7 1.1 collective-permute-done.25
  127.1 2.6 %collective-permute-start.32 = (bf16[64,2560]{1,0:T(8,128)(2,1)S(1)}, bf16[64,2560]{1,0:T(8,128)(2,1)S(1)}, u32[]{:S(2)}, u32[]{:S(2)}) collective-permute-start(bf16[64,2560]{1,0:T(8,128)(2,1)S(1)} %get-tuple-element.59), channel_id=1, source_target_pairs={{0,3},{1,0},{2,1},{3,2},{4,7},{5,4},{6,5},{7,6},{8,11},{9,8},{10,9... | collective-permute-start | bytes 983048 | tf_op jit(solution)/shard_map/ppermute | solution.py:21
  129.7 4.1 %collective-permute-done.29 = bf16[64,2560]{1,0:T(8,128)(2,1)S(1)} collective-permute-done((bf16[64,2560]{1,0:T(8,128)(2,1)S(1)}, bf16[64,2560]{1,0:T(8,128)(2,1)S(1)}, u32[]{:S(2)}, u32[]{:S(2)}) %collective-permute-start.29) | collective-permute-done | bytes 327712 | tf_op jit(solution)/shard_map/ppermute | solution.py:21
  133.8 7.0 %collective-permute-done.26 = bf16[64,2560]{1,0:T(8,128)(2,1)S(1)} collective-permute-done((bf16[64,2560]{1,0:T(8,128)(2,1)S(1)}, bf16[64,2560]{1,0:T(8,128)(2,1)S(1)}, u32[]{:S(2)}, u32[]{:S(2)}) %collective-permute-start.26) | collective-permute-done | bytes 327712 | tf_op jit(solution)/shard_map/ppermute | solution.py:21
  141.5 16.7 %all_to_all.10 = bf16[16,4,5120]{2,1,0:T(4,128)(2,1)S(1)} all-to-all(bf16[16,4,5120]{2,1,0:T(4,128)(2,1)S(1)} %reshape.14), channel_id=1, replica_groups=mesh['xl'=2,'y'=4,'core'=2,'xh'=2,'z'=4] {'xl','y','core'}, dimensions={0} | all-to-all | bytes 1310720 | tf_op jit(solution)/shard_map/all_to_all | solution.py:240
  158.4 15.1 %all_to_all.11 = bf16[16,4,5120]{2,1,0:T(4,128)(2,1)S(1)} all-to-all(bf16[16,4,5120]{2,1,0:T(4,128)(2,1)S(1)} %reduce-window_convert_fusion), channel_id=1, replica_groups=mesh['xl'=2,'y'=4,'core'=2,'xh'=2,'z'=4] {'xl','y','core'}, dimensions={0} | all-to-all | bytes 1310720 | tf_op jit(solution)/shard_map/all_to_all | solution.py:242
  173.6 1.2 add_bitcast_fusion
  (109 shorter events, 14.3 us)
Async XLA Ops:
  0.0 5.4 %copy-start = (bf16[3,320,640]{2,1,0:T(8,128)(2,1)S(1)}, bf16[3,320,640]{2,1,0:T(8,128)(2,1)}, u32[]{:S(2)}) copy-start(bf16[3,320,640]{2,1,0:T(8,128)(2,1)} %param.12) | copy-start | bytes 3686404
  3.9 5.6 %collective-permute-start = (bf16[64,2560]{1,0:T(8,128)(2,1)}, bf16[64,2560]{1,0:T(8,128)(2,1)S(1)}, u32[]{:S(2)}, u32[]{:S(2)}) collective-permute-start(bf16[64,2560]{1,0:T(8,128)(2,1)} %get-tuple-element.34), channel_id=1, source_target_pairs={{0,8},{8,0},{1,9},{9,1},{2,10},{10,2},{3,11},{11,3},{4,12},{12,4},... | collective-permute-start | bytes 983048 | tf_op jit(solution)/shard_map/ppermute | solution.py:21
  5.4 29.2 %collective-permute-start.2 = (bf16[3,320,640]{2,1,0:T(8,128)(2,1)S(1)}, bf16[3,320,640]{2,1,0:T(8,128)(2,1)S(1)}, u32[]{:S(2)}, u32[]{:S(2)}) collective-permute-start(bf16[3,320,640]{2,1,0:T(8,128)(2,1)S(1)} %copy-done), channel_id=1, source_target_pairs={{0,48},{16,0},{32,16},{48,32},{1,49},{17,1},{33,17},{49,33},{2,50}... | collective-permute-start | bytes 3686408 | tf_op jit(solution)/shard_map/ppermute | solution.py:21
  8.2 29.5 %collective-permute-start.3 = (bf16[3,320,640]{2,1,0:T(8,128)(2,1)S(1)}, bf16[3,320,640]{2,1,0:T(8,128)(2,1)S(1)}, u32[]{:S(2)}, u32[]{:S(2)}) collective-permute-start(bf16[3,320,640]{2,1,0:T(8,128)(2,1)S(1)} %copy-done), channel_id=1, source_target_pairs={{0,16},{16,32},{32,48},{48,0},{1,17},{17,33},{33,49},{49,1},{2,18}... | collective-permute-start | bytes 3686408 | tf_op jit(solution)/shard_map/ppermute | solution.py:21
  8.3 19.6 %collective-permute-start.7 = (bf16[2,320,640]{2,1,0:T(8,128)(2,1)S(1)}, bf16[2,320,640]{2,1,0:T(8,128)(2,1)S(1)}, u32[]{:S(2)}, u32[]{:S(2)}) collective-permute-start(bf16[2,320,640]{2,1,0:T(8,128)(2,1)S(1)} %slice.162), channel_id=1, source_target_pairs={{0,64},{64,0},{1,65},{65,1},{2,66},{66,2},{3,67},{67,3},{4,68},{68... | collective-permute-start | bytes 2457608 | tf_op jit(solution)/shard_map/ppermute | solution.py:21
  10.6 20.0 %collective-permute-start.1 = (bf16[2,64,2560]{2,1,0:T(8,128)(2,1)S(1)}, bf16[2,64,2560]{2,1,0:T(8,128)(2,1)S(1)}, u32[]{:S(2)}, u32[]{:S(2)}) collective-permute-start(bf16[2,64,2560]{2,1,0:T(8,128)(2,1)S(1)} %pad_maximum_fusion.5), channel_id=1, source_target_pairs={{0,3},{1,0},{2,1},{3,2},{4,7},{5,4},{6,5},{7,6},{8,11},{9,8},{10,9... | collective-permute-start | bytes 1966088 | tf_op jit(solution)/shard_map/ppermute | solution.py:21
  14.4 16.5 %collective-permute-start.5 = (bf16[2,64,2560]{2,1,0:T(8,128)(2,1)S(1)}, bf16[2,64,2560]{2,1,0:T(8,128)(2,1)S(1)}, u32[]{:S(2)}, u32[]{:S(2)}) collective-permute-start(bf16[2,64,2560]{2,1,0:T(8,128)(2,1)S(1)} %pad_maximum_fusion.5), channel_id=1, source_target_pairs={{0,1},{1,2},{2,3},{3,0},{4,5},{5,6},{6,7},{7,4},{8,9},{9,10},{10,1... | collective-permute-start | bytes 1966088 | tf_op jit(solution)/shard_map/ppermute | solution.py:21
  27.8 16.5 %collective-permute-start.8 = (bf16[2,64,2560]{2,1,0:T(8,128)(2,1)S(1)}, bf16[2,64,2560]{2,1,0:T(8,128)(2,1)S(1)}, u32[]{:S(2)}, u32[]{:S(2)}) collective-permute-start(bf16[2,64,2560]{2,1,0:T(8,128)(2,1)S(1)} %pad_maximum_fusion.5), channel_id=1, source_target_pairs={{0,4},{4,0},{1,5},{5,1},{2,6},{6,2},{3,7},{7,3},{8,12},{12,8},{9,1... | collective-permute-start | bytes 1966088 | tf_op jit(solution)/shard_map/ppermute | solution.py:21
  31.0 21.1 %collective-permute-start.13 = (bf16[2,320,640]{2,1,0:T(8,128)(2,1)S(1)}, bf16[2,320,640]{2,1,0:T(8,128)(2,1)S(1)}, u32[]{:S(2)}, u32[]{:S(2)}) collective-permute-start(bf16[2,320,640]{2,1,0:T(8,128)(2,1)S(1)} %collective-permute-done.7), channel_id=1, source_target_pairs={{0,48},{16,0},{32,16},{48,32},{1,49},{17,1},{33,17},{49,33},{2,50}... | collective-permute-start | bytes 2457608 | tf_op jit(solution)/shard_map/ppermute | solution.py:21
  33.3 21.4 %collective-permute-start.15 = (bf16[2,320,640]{2,1,0:T(8,128)(2,1)S(1)}, bf16[2,320,640]{2,1,0:T(8,128)(2,1)S(1)}, u32[]{:S(2)}, u32[]{:S(2)}) collective-permute-start(bf16[2,320,640]{2,1,0:T(8,128)(2,1)S(1)} %collective-permute-done.7), channel_id=1, source_target_pairs={{0,16},{16,32},{32,48},{48,0},{1,17},{17,33},{33,49},{49,1},{2,18}... | collective-permute-start | bytes 2457608 | tf_op jit(solution)/shard_map/ppermute | solution.py:21
  34.6 7.0 %copy-start.3 = (bf16[3,320,640]{2,1,0:T(8,128)(2,1)}, bf16[3,320,640]{2,1,0:T(8,128)(2,1)S(1)}, u32[]{:S(2)}) copy-start(bf16[3,320,640]{2,1,0:T(8,128)(2,1)S(1)} %collective-permute-done.2) | copy-start | bytes 3686404
  37.7 3.9 %copy-start.1 = (bf16[3,320,640]{2,1,0:T(8,128)(2,1)}, bf16[3,320,640]{2,1,0:T(8,128)(2,1)S(1)}, u32[]{:S(2)}) copy-start(bf16[3,320,640]{2,1,0:T(8,128)(2,1)S(1)} %collective-permute-done.3) | copy-start | bytes 3686404
  37.7 8.8 %collective-permute-start.4 = (bf16[2,32,2560]{2,1,0:T(8,128)(2,1)S(1)}, bf16[2,32,2560]{2,1,0:T(8,128)(2,1)S(1)}, u32[]{:S(2)}, u32[]{:S(2)}) collective-permute-start(bf16[2,32,2560]{2,1,0:T(8,128)(2,1)S(1)} %slice.208), channel_id=1, source_target_pairs={{0,3},{1,0},{2,1},{3,2},{4,7},{5,4},{6,5},{7,6},{8,11},{9,8},{10,9... | collective-permute-start | bytes 983048 | tf_op jit(solution)/shard_map/ppermute | solution.py:21
  41.4 8.2 %collective-permute-start.6 = (bf16[2,32,2560]{2,1,0:T(8,128)(2,1)S(1)}, bf16[2,32,2560]{2,1,0:T(8,128)(2,1)S(1)}, u32[]{:S(2)}, u32[]{:S(2)}) collective-permute-start(bf16[2,32,2560]{2,1,0:T(8,128)(2,1)S(1)} %slice.209), channel_id=1, source_target_pairs={{0,1},{1,2},{2,3},{3,0},{4,5},{5,6},{6,7},{7,4},{8,9},{9,10},{10,1... | collective-permute-start | bytes 983048 | tf_op jit(solution)/shard_map/ppermute | solution.py:21
  41.9 9.3 %copy-start.4 = (bf16[64,2560]{1,0:T(8,128)(2,1)S(1)}, bf16[64,2560]{1,0:T(8,128)(2,1)}, u32[]{:S(2)}) copy-start(bf16[64,2560]{1,0:T(8,128)(2,1)} %get-tuple-element.33) | copy-start | bytes 983044
  44.4 34.1 %collective-permute-start.19 = (bf16[3,320,640]{2,1,0:T(8,128)(2,1)S(1)}, bf16[3,320,640]{2,1,0:T(8,128)(2,1)S(1)}, u32[]{:S(2)}, u32[]{:S(2)}) collective-permute-start(bf16[3,320,640]{2,1,0:T(8,128)(2,1)S(1)} %pad_maximum_fusion.1), channel_id=1, source_target_pairs={{0,64},{64,0},{1,65},{65,1},{2,66},{66,2},{3,67},{67,3},{4,68},{68... | collective-permute-start | bytes 3686408 | tf_op jit(solution)/shard_map/ppermute | solution.py:21
  49.6 13.1 %collective-permute-start.9 = (bf16[2,64,2560]{2,1,0:T(8,128)(2,1)S(1)}, bf16[2,64,2560]{2,1,0:T(8,128)(2,1)S(1)}, u32[]{:S(2)}, u32[]{:S(2)}) collective-permute-start(bf16[2,64,2560]{2,1,0:T(8,128)(2,1)S(1)} %collective-permute-done.8), channel_id=1, source_target_pairs={{0,3},{1,0},{2,1},{3,2},{4,7},{5,4},{6,5},{7,6},{8,11},{9,8},{10,9... | collective-permute-start | bytes 1966088 | tf_op jit(solution)/shard_map/ppermute | solution.py:21
  49.9 14.3 %collective-permute-start.10 = (bf16[2,64,2560]{2,1,0:T(8,128)(2,1)S(1)}, bf16[2,64,2560]{2,1,0:T(8,128)(2,1)S(1)}, u32[]{:S(2)}, u32[]{:S(2)}) collective-permute-start(bf16[2,64,2560]{2,1,0:T(8,128)(2,1)S(1)} %collective-permute-done.8), channel_id=1, source_target_pairs={{0,1},{1,2},{2,3},{3,0},{4,5},{5,6},{6,7},{7,4},{8,9},{9,10},{10,1... | collective-permute-start | bytes 1966088 | tf_op jit(solution)/shard_map/ppermute | solution.py:21
  51.2 1.1 slice-start.3
  52.0 2.8 %slice-start.2 = ((bf16[3,320,640]{2,1,0:T(8,128)(2,1)}), bf16[3,160,640]{2,1,0:T(8,128)(2,1)S(1)}, s32[]{:S(2)}) async-start(bf16[3,320,640]{2,1,0:T(8,128)(2,1)} %copy-done.1), calls=%async_computation.4 | async-start | bytes 1228800 | tf_op jit(solution)/shard_map/slice | solution.py:166
  52.4 2.8 %copy-start.2 = (bf16[3,320,640]{2,1,0:T(8,128)(2,1)S(1)}, bf16[3,320,640]{2,1,0:T(8,128)(2,1)}, u32[]{:S(2)}) copy-start(bf16[3,320,640]{2,1,0:T(8,128)(2,1)} %copy-done.1) | copy-start | bytes 3686404
  52.4 31.5 %collective-permute-start.14 = (bf16[5,160,640]{2,1,0:T(8,128)(2,1)S(1)}, bf16[5,160,640]{2,1,0:T(8,128)(2,1)S(1)}, u32[]{:S(2)}, u32[]{:S(2)}) collective-permute-start(bf16[5,160,640]{2,1,0:T(8,128)(2,1)S(1)} %pad_maximum_fusion.2), channel_id=1, source_target_pairs={{0,48},{16,0},{32,16},{48,32},{1,49},{17,1},{33,17},{49,33},{2,50}... | collective-permute-start | bytes 3072008 | tf_op jit(solution)/shard_map/ppermute | solution.py:21
  55.0 29.1 %collective-permute-start.16 = (bf16[5,160,640]{2,1,0:T(8,128)(2,1)S(1)}, bf16[5,160,640]{2,1,0:T(8,128)(2,1)S(1)}, u32[]{:S(2)}, u32[]{:S(2)}) collective-permute-start(bf16[5,160,640]{2,1,0:T(8,128)(2,1)S(1)} %pad_maximum_fusion.3), channel_id=1, source_target_pairs={{0,16},{16,32},{32,48},{48,0},{1,17},{17,33},{33,49},{49,1},{2,18}... | collective-permute-start | bytes 3072008 | tf_op jit(solution)/shard_map/ppermute | solution.py:21
  64.1 6.2 %collective-permute-start.11 = (bf16[2,32,2560]{2,1,0:T(8,128)(2,1)S(1)}, bf16[2,32,2560]{2,1,0:T(8,128)(2,1)S(1)}, u32[]{:S(2)}, u32[]{:S(2)}) collective-permute-start(bf16[2,32,2560]{2,1,0:T(8,128)(2,1)S(1)} %slice.210), channel_id=1, source_target_pairs={{0,3},{1,0},{2,1},{3,2},{4,7},{5,4},{6,5},{7,6},{8,11},{9,8},{10,9... | collective-permute-start | bytes 983048 | tf_op jit(solution)/shard_map/ppermute | solution.py:21
  66.5 7.5 %collective-permute-start.12 = (bf16[2,32,2560]{2,1,0:T(8,128)(2,1)S(1)}, bf16[2,32,2560]{2,1,0:T(8,128)(2,1)S(1)}, u32[]{:S(2)}, u32[]{:S(2)}) collective-permute-start(bf16[2,32,2560]{2,1,0:T(8,128)(2,1)S(1)} %slice.211), channel_id=1, source_target_pairs={{0,1},{1,2},{2,3},{3,0},{4,5},{5,6},{6,7},{7,4},{8,9},{9,10},{10,1... | collective-permute-start | bytes 983048 | tf_op jit(solution)/shard_map/ppermute | solution.py:21
  78.5 13.9 %collective-permute-start.21 = (bf16[160,640]{1,0:T(8,128)(2,1)S(1)}, bf16[160,640]{1,0:T(8,128)(2,1)S(1)}, u32[]{:S(2)}, u32[]{:S(2)}) collective-permute-start(bf16[160,640]{1,0:T(8,128)(2,1)S(1)} %get-tuple-element.48), channel_id=1, source_target_pairs={{0,16},{16,32},{32,48},{48,0},{1,17},{17,33},{33,49},{49,1},{2,18}... | collective-permute-start | bytes 614408 | tf_op jit(solution)/shard_map/ppermute | solution.py:21
  78.7 13.8 %collective-permute-start.20 = (bf16[160,640]{1,0:T(8,128)(2,1)S(1)}, bf16[160,640]{1,0:T(8,128)(2,1)S(1)}, u32[]{:S(2)}, u32[]{:S(2)}) collective-permute-start(bf16[160,640]{1,0:T(8,128)(2,1)S(1)} %get-tuple-element.47), channel_id=1, source_target_pairs={{0,48},{16,0},{32,16},{48,32},{1,49},{17,1},{33,17},{49,33},{2,50}... | collective-permute-start | bytes 614408 | tf_op jit(solution)/shard_map/ppermute | solution.py:21
  84.2 13.5 %slice-start = ((s8[6553600]{0:T(1024)(128)(4,1)}), s8[4194304]{0:T(1024)(128)(4,1)S(1)}, s32[]{:S(2)}) async-start(s8[6553600]{0:T(1024)(128)(4,1)} %bitcast.88), calls=%async_computation.2 | async-start | bytes 8388608
  86.7 7.8 %collective-permute-start.17 = (bf16[512,640]{1,0:T(8,128)(2,1)S(1)}, bf16[512,640]{1,0:T(8,128)(2,1)S(1)}, u32[]{:S(2)}, u32[]{:S(2)}) collective-permute-start(bf16[512,640]{1,0:T(8,128)(2,1)S(1)} %get-tuple-element.43), channel_id=1, source_target_pairs={{0,8},{8,0},{1,9},{9,1},{2,10},{10,2},{3,11},{11,3},{4,12},{12,4},... | collective-permute-start | bytes 1966088 | tf_op jit(solution)/shard_map/ppermute | solution.py:21
  92.3 2.7 %collective-permute-start.18 = (bf16[512,640]{1,0:T(8,128)(2,1)S(1)}, bf16[512,640]{1,0:T(8,128)(2,1)S(1)}, u32[]{:S(2)}, u32[]{:S(2)}) collective-permute-start(bf16[512,640]{1,0:T(8,128)(2,1)S(1)} %get-tuple-element.45), channel_id=1, source_target_pairs={{0,8},{8,0},{1,9},{9,1},{2,10},{10,2},{3,11},{11,3},{4,12},{12,4},... | collective-permute-start | bytes 1966088 | tf_op jit(solution)/shard_map/ppermute | solution.py:21
  92.5 5.3 %slice-start.1 = ((s8[6553600]{0:T(1024)(128)(4,1)}), s8[2359296]{0:T(1024)(128)(4,1)S(1)}, s32[]{:S(2)}) async-start(s8[6553600]{0:T(1024)(128)(4,1)} %bitcast.88), calls=%async_computation.3 | async-start | bytes 4718592
  93.8 2.4 %collective-permute-start.22 = (bf16[512,640]{1,0:T(8,128)(2,1)S(1)}, bf16[512,640]{1,0:T(8,128)(2,1)S(1)}, u32[]{:S(2)}, u32[]{:S(2)}) collective-permute-start(bf16[512,640]{1,0:T(8,128)(2,1)S(1)} %get-tuple-element.50), channel_id=1, source_target_pairs={{0,8},{8,0},{1,9},{9,1},{2,10},{10,2},{3,11},{11,3},{4,12},{12,4},... | collective-permute-start | bytes 1966088 | tf_op jit(solution)/shard_map/ppermute | solution.py:21
  99.5 7.0 %collective-permute-start.23 = (bf16[64,1280]{1,0:T(8,128)(2,1)S(1)}, bf16[64,1280]{1,0:T(8,128)(2,1)S(1)}, u32[]{:S(2)}, u32[]{:S(2)}) collective-permute-start(bf16[64,1280]{1,0:T(8,128)(2,1)S(1)} %slice.239), channel_id=1, source_target_pairs={{0,4},{4,0},{1,5},{5,1},{2,6},{6,2},{3,7},{7,3},{8,12},{12,8},{9,1... | collective-permute-start | bytes 491528 | tf_op jit(solution)/shard_map/ppermute | solution.py:21
  102.5 16.5 %collective-permute-start.28 = (bf16[64,5120]{1,0:T(8,128)(2,1)S(1)}, bf16[64,5120]{1,0:T(8,128)(2,1)S(1)}, u32[]{:S(2)}, u32[]{:S(2)}) collective-permute-start(bf16[64,5120]{1,0:T(8,128)(2,1)S(1)} %get-tuple-element.66), channel_id=1, source_target_pairs={{0,3},{1,0},{2,1},{3,2},{4,7},{5,4},{6,5},{7,6},{8,11},{9,8},{10,9... | collective-permute-start | bytes 1966088 | tf_op jit(solution)/shard_map/ppermute | solution.py:21
  102.6 14.6 %collective-permute-start.24 = (bf16[64,3840]{1,0:T(8,128)(2,1)S(1)}, bf16[64,3840]{1,0:T(8,128)(2,1)S(1)}, u32[]{:S(2)}, u32[]{:S(2)}) collective-permute-start(bf16[64,3840]{1,0:T(8,128)(2,1)S(1)} %slice.243), channel_id=1, source_target_pairs={{0,4},{4,0},{1,5},{5,1},{2,6},{6,2},{3,7},{7,3},{8,12},{12,8},{9,1... | collective-permute-start | bytes 1474568 | tf_op jit(solution)/shard_map/ppermute | solution.py:21
  102.9 16.5 %collective-permute-start.27 = (bf16[64,5120]{1,0:T(8,128)(2,1)S(1)}, bf16[64,5120]{1,0:T(8,128)(2,1)S(1)}, u32[]{:S(2)}, u32[]{:S(2)}) collective-permute-start(bf16[64,5120]{1,0:T(8,128)(2,1)S(1)} %get-tuple-element.65), channel_id=1, source_target_pairs={{0,1},{1,2},{2,3},{3,0},{4,5},{5,6},{6,7},{7,4},{8,9},{9,10},{10,1... | collective-permute-start | bytes 1966088 | tf_op jit(solution)/shard_map/ppermute | solution.py:21
  117.5 8.2 %collective-permute-start.31 = (bf16[64,2560]{1,0:T(8,128)(2,1)S(1)}, bf16[64,2560]{1,0:T(8,128)(2,1)S(1)}, u32[]{:S(2)}, u32[]{:S(2)}) collective-permute-start(bf16[64,2560]{1,0:T(8,128)(2,1)S(1)} %get-tuple-element.90), channel_id=1, source_target_pairs={{0,3},{1,0},{2,1},{3,2},{4,7},{5,4},{6,5},{7,6},{8,11},{9,8},{10,9... | collective-permute-start | bytes 983048 | tf_op jit(solution)/shard_map/ppermute | solution.py:21
  117.5 23.3 %copy-start.6 = (f32[1,5120]{1,0:T(1,128)S(1)}, f32[1,5120]{1,0:T(1,128)}, u32[]{:S(2)}) copy-start(f32[1,5120]{1,0:T(1,128)} %get-tuple-element.32) | copy-start | bytes 61444
  117.5 9.3 %collective-permute-start.25 = (bf16[64,2560]{1,0:T(8,128)(2,1)S(1)}, bf16[64,2560]{1,0:T(8,128)(2,1)S(1)}, u32[]{:S(2)}, u32[]{:S(2)}) collective-permute-start(bf16[64,2560]{1,0:T(8,128)(2,1)S(1)} %get-tuple-element.91), channel_id=1, source_target_pairs={{0,1},{1,2},{2,3},{3,0},{4,5},{5,6},{6,7},{7,4},{8,9},{9,10},{10,1... | collective-permute-start | bytes 983048 | tf_op jit(solution)/shard_map/ppermute | solution.py:21
  119.6 21.2 %collective-permute-start.33 = (bf16[64,5120]{1,0:T(8,128)(2,1)S(1)}, bf16[64,5120]{1,0:T(8,128)(2,1)S(1)}, u32[]{:S(2)}, u32[]{:S(2)}) collective-permute-start(bf16[64,5120]{1,0:T(8,128)(2,1)S(1)} %add_convert_fusion), channel_id=1, source_target_pairs={{0,4},{4,0},{1,5},{5,1},{2,6},{6,2},{3,7},{7,3},{8,12},{12,8},{9,1... | collective-permute-start | bytes 1966088 | tf_op jit(solution)/shard_map/ppermute | solution.py:21
  122.5 11.4 %collective-permute-start.29 = (bf16[64,2560]{1,0:T(8,128)(2,1)S(1)}, bf16[64,2560]{1,0:T(8,128)(2,1)S(1)}, u32[]{:S(2)}, u32[]{:S(2)}) collective-permute-start(bf16[64,2560]{1,0:T(8,128)(2,1)S(1)} %get-tuple-element.56), channel_id=1, source_target_pairs={{0,1},{1,2},{2,3},{3,0},{4,5},{5,6},{6,7},{7,4},{8,9},{9,10},{10,1... | collective-permute-start | bytes 983048 | tf_op jit(solution)/shard_map/ppermute | solution.py:21
  122.5 11.4 %collective-permute-start.30 = (bf16[64,2560]{1,0:T(8,128)(2,1)S(1)}, bf16[64,2560]{1,0:T(8,128)(2,1)S(1)}, u32[]{:S(2)}, u32[]{:S(2)}) collective-permute-start(bf16[64,2560]{1,0:T(8,128)(2,1)S(1)} %get-tuple-element.57), channel_id=1, source_target_pairs={{0,3},{1,0},{2,1},{3,2},{4,7},{5,4},{6,5},{7,6},{8,11},{9,8},{10,9... | collective-permute-start | bytes 983048 | tf_op jit(solution)/shard_map/ppermute | solution.py:21
  126.9 13.9 %collective-permute-start.26 = (bf16[64,2560]{1,0:T(8,128)(2,1)S(1)}, bf16[64,2560]{1,0:T(8,128)(2,1)S(1)}, u32[]{:S(2)}, u32[]{:S(2)}) collective-permute-start(bf16[64,2560]{1,0:T(8,128)(2,1)S(1)} %get-tuple-element.60), channel_id=1, source_target_pairs={{0,1},{1,2},{2,3},{3,0},{4,5},{5,6},{6,7},{7,4},{8,9},{9,10},{10,1... | collective-permute-start | bytes 983048 | tf_op jit(solution)/shard_map/ppermute | solution.py:21
  127.1 13.8 %collective-permute-start.32 = (bf16[64,2560]{1,0:T(8,128)(2,1)S(1)}, bf16[64,2560]{1,0:T(8,128)(2,1)S(1)}, u32[]{:S(2)}, u32[]{:S(2)}) collective-permute-start(bf16[64,2560]{1,0:T(8,128)(2,1)S(1)} %get-tuple-element.59), channel_id=1, source_target_pairs={{0,3},{1,0},{2,1},{3,2},{4,7},{5,4},{6,5},{7,6},{8,11},{9,8},{10,9... | collective-permute-start | bytes 983048 | tf_op jit(solution)/shard_map/ppermute | solution.py:21
  158.1 15.4 %copy-start.5 = (f32[64,5120]{1,0:T(8,128)S(1)}, f32[64,5120]{1,0:T(8,128)}, u32[]{:S(2)}) copy-start(f32[64,5120]{1,0:T(8,128)} %param.8) | copy-start | bytes 3932164

commit v6 on v5

--- a/solution.py
+++ b/solution.py
@@ -37,7 +37,7 @@
     center = jnp.mean(state, axis=-1, keepdims=True)
     moved = state - center
     spread = jnp.mean(moved * moved, axis=-1, keepdims=True)
-    scratch[...] = moved * lax.rsqrt(spread + 1e-06) * (1.0 + scale_row) + shift_row
+    scratch[...] = (moved * lax.rsqrt(spread + 1e-06) * (1.0 + scale_row) + shift_row).astype(BF16)
     xl, y, core = (lax.axis_index(a) for a in TM)
     ny, wide = 4, 2 * rows
     low = core == 0
@@ -50,8 +50,8 @@
             mine.append(jnp.where(low, first, second))
             other.append(jnp.where(low, second, first))
         here = slice(place * rows, (place + 2) * rows)
-        mine_ref[:, here] = jnp.concatenate(mine, axis=1).astype(BF16)
-        other_ref[:, here] = jnp.concatenate(other, axis=1).astype(BF16)
+        mine_ref[:, here] = jnp.concatenate(mine, axis=1)
+        other_ref[:, here] = jnp.concatenate(other, axis=1)
 
 
 def modulate(states, t_index, mod_table, coef, rows):
@@ -73,7 +73,7 @@
                 pl.BlockSpec((tokens, width // 2), lambda i, t: (0, 0)),
                 pl.BlockSpec((1, width), lambda i, t: (0, 0)),
             ],
-            scratch_shapes=[pltpu.VMEM((tokens, width), F32)],
+            scratch_shapes=[pltpu.VMEM((tokens, width), BF16)],
         ),
         compiler_params=pltpu.CompilerParams(vmem_limit_bytes=VMEM_BYTES),
         cost_estimate=pl.CostEstimate(flops=1000, bytes_accessed=1000, transcendentals=0),
@@ -113,16 +113,16 @@
 
 
 def last_kernel(matrices, f0, f1, far, extra, *refs):
-    rows, count = far.shape[1], f0.shape[0]
+    rows, count, columns = far.shape[1], f0.shape[0], far.shape[2]
     half, each = count // 2, len(matrices)
-    for i, j in enumerate(matrices):
-        mate = far[3 + j] if j < 2 else extra[...]
-        weight = jnp.concatenate([far[j], mate], axis=0)
-        own_ref, mate_ref = refs[2 * each + 2 * i : 2 * each + 2 * i + 2]
-        for dx, f in enumerate((f0, f1)):
-            total = refs[2 * i + dx][...] + jnp.dot(
-                f[:, 6 * rows :], weight, preferred_element_type=F32
-            )
+    mates = [far[3 + j] if j < 2 else extra[...] for j in matrices]
+    weights = [jnp.concatenate([far[j], mate], axis=0) for j, mate in zip(matrices, mates)]
+    weight = jnp.concatenate(weights, axis=1)
+    for dx, f in enumerate((f0, f1)):
+        products = jnp.dot(f[:, 6 * rows :], weight, preferred_element_type=F32)
+        for i in range(each):
+            own_ref, mate_ref = refs[2 * each + 2 * i : 2 * each + 2 * i + 2]
+            total = refs[2 * i + dx][...] + products[:, i * columns : (i + 1) * columns]
             own_ref[dx * half : (dx + 1) * half] = total[:half]
             mate_ref[dx * half : (dx + 1) * half] = total[half:].astype(BF16)
 

time: 175 us -> 175 us (level)
  no operation moved by 1% of the time
where the time goes in v6:
time: 175 us
  waiting for transfers between devices  61.6 us (35%)
  starting transfers between devices  48.4 us (28%)
  blocking collectives  32 us (18%)
  matrix products  15.3 us (9%)
  Pallas kernels  9.42 us (5%)
  other arithmetic  4.03 us (2%)
  local copies, waits for them, and re-layouts  2.67 us (2%)
    ppermute x34, waiting for transfers between devices, send(): lax.ppermute(array, axis, [(i, (i + shift) % size) for i in range(size)])  61.6 us
    ppermute x34, starting transfers between devices, send(): lax.ppermute(array, axis, [(i, (i + shift) % size) for i in range(size)])  48.4 us
    all_to_all x1, blocking collectives, on_device(): lax.all_to_all(term.reshape(steps, tokens // steps, width), TM, 0, 0)  17 us
    all_to_all x1, blocking collectives, on_device(): total = lax.all_to_all(total, TM, 0, 0).reshape(tokens, width)  15.1 us
    dot_general x8, matrix products, product(): jnp.dot(f[:, begin:stop], weight, preferred_element_type=F32)  10.9 us
    pallas_call x4, Pallas kernels, local_call(): pl.pallas_call(kernel, out_shape=[jax.ShapeDtypeStruct(*shape) for shape...  6.17 us
  transfers between devices with their start and end apart: 34, of which 20 were waited for; matrix products, arithmetic and copies ran while one was open for 10% of the time, Pallas kernels for 3%

profile of v6, /device:TPU:1, one launch (start us, length us, event | category | flops | bytes accessed | tf_op | source)
XLA Modules:
  0.0 174.8 jit_solution(3077694916283091363)
XLA Ops:
  0.8 3.2 %shard_map.73 = (bf16[64,2560]{1,0:T(8,128)(2,1)}, bf16[64,2560]{1,0:T(8,128)(2,1)}, f32[1,5120]{1,0:T(1,128)}) custom-call(s32[1]{0:T(128)S(6)} %copy.27.t_ref, f32[1,64,5120]{2,1,0:T(8,128)} %state_ref.1, f32[3,50,5120]{2,1,0:T(8,128)} %bitcast.90, f32[50]{0:T(128)} %coef_ref.1), custom_call_target="tpu_custom_call" | custom-call | flops 1000 | bytes 1000 | tf_op jit(solution)/shard_map/pallas_call | solution.py:60
  4.0 1.4 collective-permute-start
  5.4 2.8 %collective-permute-start.2 = (bf16[3,320,640]{2,1,0:T(8,128)(2,1)S(1)}, bf16[3,320,640]{2,1,0:T(8,128)(2,1)S(1)}, u32[]{:S(2)}, u32[]{:S(2)}) collective-permute-start(bf16[3,320,640]{2,1,0:T(8,128)(2,1)S(1)} %copy-done), channel_id=1, source_target_pairs={{0,48},{16,0},{32,16},{48,32},{1,49},{17,1},{33,17},{49,33},{2,50}... | collective-permute-start | bytes 3686408 | tf_op jit(solution)/shard_map/ppermute | solution.py:21
  8.3 1.3 collective-permute-start.7
  10.7 3.8 %collective-permute-start.1 = (bf16[2,64,2560]{2,1,0:T(8,128)(2,1)S(1)}, bf16[2,64,2560]{2,1,0:T(8,128)(2,1)S(1)}, u32[]{:S(2)}, u32[]{:S(2)}) collective-permute-start(bf16[2,64,2560]{2,1,0:T(8,128)(2,1)S(1)} %pad_maximum_fusion.5), channel_id=1, source_target_pairs={{0,3},{1,0},{2,1},{3,2},{4,7},{5,4},{6,5},{7,6},{8,11},{9,8},{10,9... | collective-permute-start | bytes 1966088 | tf_op jit(solution)/shard_map/ppermute | solution.py:21
  14.6 13.2 %collective-permute-done.7 = bf16[2,320,640]{2,1,0:T(8,128)(2,1)S(1)} collective-permute-done((bf16[2,320,640]{2,1,0:T(8,128)(2,1)S(1)}, bf16[2,320,640]{2,1,0:T(8,128)(2,1)S(1)}, u32[]{:S(2)}, u32[]{:S(2)}) %collective-permute-start.7) | collective-permute-done | bytes 819232 | tf_op jit(solution)/shard_map/ppermute | solution.py:21
  27.9 2.7 %collective-permute-start.8 = (bf16[2,64,2560]{2,1,0:T(8,128)(2,1)S(1)}, bf16[2,64,2560]{2,1,0:T(8,128)(2,1)S(1)}, u32[]{:S(2)}, u32[]{:S(2)}) collective-permute-start(bf16[2,64,2560]{2,1,0:T(8,128)(2,1)S(1)} %pad_maximum_fusion.5), channel_id=1, source_target_pairs={{0,4},{4,0},{1,5},{5,1},{2,6},{6,2},{3,7},{7,3},{8,12},{12,8},{9,1... | collective-permute-start | bytes 1966088 | tf_op jit(solution)/shard_map/ppermute | solution.py:21
  31.0 2.4 %collective-permute-start.13 = (bf16[2,320,640]{2,1,0:T(8,128)(2,1)S(1)}, bf16[2,320,640]{2,1,0:T(8,128)(2,1)S(1)}, u32[]{:S(2)}, u32[]{:S(2)}) collective-permute-start(bf16[2,320,640]{2,1,0:T(8,128)(2,1)S(1)} %collective-permute-done.7), channel_id=1, source_target_pairs={{0,48},{16,0},{32,16},{48,32},{1,49},{17,1},{33,17},{49,33},{2,50}... | collective-permute-start | bytes 2457608 | tf_op jit(solution)/shard_map/ppermute | solution.py:21
  33.5 1.2 collective-permute-done.2
  34.6 3.1 %collective-permute-done.3 = bf16[3,320,640]{2,1,0:T(8,128)(2,1)S(1)} collective-permute-done((bf16[3,320,640]{2,1,0:T(8,128)(2,1)S(1)}, bf16[3,320,640]{2,1,0:T(8,128)(2,1)S(1)}, u32[]{:S(2)}, u32[]{:S(2)}) %collective-permute-start.3) | collective-permute-done | bytes 1228832 | tf_op jit(solution)/shard_map/ppermute | solution.py:21
  37.7 3.8 %collective-permute-start.4 = (bf16[2,32,2560]{2,1,0:T(8,128)(2,1)S(1)}, bf16[2,32,2560]{2,1,0:T(8,128)(2,1)S(1)}, u32[]{:S(2)}, u32[]{:S(2)}) collective-permute-start(bf16[2,32,2560]{2,1,0:T(8,128)(2,1)S(1)} %slice.208), channel_id=1, source_target_pairs={{0,3},{1,0},{2,1},{3,2},{4,7},{5,4},{6,5},{7,6},{8,11},{9,8},{10,9... | collective-permute-start | bytes 983048 | tf_op jit(solution)/shard_map/ppermute | solution.py:21
  42.1 2.3 %collective-permute-done.8 = bf16[2,64,2560]{2,1,0:T(8,128)(2,1)S(1)} collective-permute-done((bf16[2,64,2560]{2,1,0:T(8,128)(2,1)S(1)}, bf16[2,64,2560]{2,1,0:T(8,128)(2,1)S(1)}, u32[]{:S(2)}, u32[]{:S(2)}) %collective-permute-start.8) | collective-permute-done | bytes 655392 | tf_op jit(solution)/shard_map/ppermute | solution.py:21
  44.4 1.2 collective-permute-start.19
  46.5 3.1 %collective-permute-done.6 = bf16[2,32,2560]{2,1,0:T(8,128)(2,1)S(1)} collective-permute-done((bf16[2,32,2560]{2,1,0:T(8,128)(2,1)S(1)}, bf16[2,32,2560]{2,1,0:T(8,128)(2,1)S(1)}, u32[]{:S(2)}, u32[]{:S(2)}) %collective-permute-start.6) | collective-permute-done | bytes 327712 | tf_op jit(solution)/shard_map/ppermute | solution.py:21
  49.9 1.2 collective-permute-start.10
  52.5 2.4 %collective-permute-start.14 = (bf16[5,160,640]{2,1,0:T(8,128)(2,1)S(1)}, bf16[5,160,640]{2,1,0:T(8,128)(2,1)S(1)}, u32[]{:S(2)}, u32[]{:S(2)}) collective-permute-start(bf16[5,160,640]{2,1,0:T(8,128)(2,1)S(1)} %pad_maximum_fusion.2), channel_id=1, source_target_pairs={{0,48},{16,0},{32,16},{48,32},{1,49},{17,1},{33,17},{49,33},{2,50}... | collective-permute-start | bytes 3072008 | tf_op jit(solution)/shard_map/ppermute | solution.py:21
  55.5 1.8 %fusion.6.refs_0_ = f32[512,640]{1,0:T(8,128)S(1)} fusion(bf16[1920,640]{1,0:T(8,128)(2,1)S(1)} %get-tuple-element.85, bf16[512,2560]{1,0:T(8,128)(2,1)S(1)} %bitcast.83), kind=kOutput, calls=%fused_computation.8 | convolution fusion | flops 1258291200 | bytes 5734400 | tf_op jit(solution)/shard_map/dot_general | solution.py:183
  57.3 5.4 %collective-permute-done.9 = bf16[2,64,2560]{2,1,0:T(8,128)(2,1)S(1)} collective-permute-done((bf16[2,64,2560]{2,1,0:T(8,128)(2,1)S(1)}, bf16[2,64,2560]{2,1,0:T(8,128)(2,1)S(1)}, u32[]{:S(2)}, u32[]{:S(2)}) %collective-permute-start.9) | collective-permute-done | bytes 655392 | tf_op jit(solution)/shard_map/ppermute | solution.py:21
  62.7 1.5 collective-permute-done.10
  64.7 1.8 %fusion.4.refs_2_ = f32[512,640]{1,0:T(8,128)S(1)} fusion(bf16[1920,640]{1,0:T(8,128)(2,1)S(1)} %get-tuple-element.84, bf16[512,2560]{1,0:T(8,128)(2,1)S(1)} %bitcast.84), kind=kOutput, calls=%fused_computation.6 | convolution fusion | flops 1258291200 | bytes 5734400 | tf_op jit(solution)/shard_map/dot_general | solution.py:183
  67.5 2.9 %collective-permute-done.11 = bf16[2,32,2560]{2,1,0:T(8,128)(2,1)S(1)} collective-permute-done((bf16[2,32,2560]{2,1,0:T(8,128)(2,1)S(1)}, bf16[2,32,2560]{2,1,0:T(8,128)(2,1)S(1)}, u32[]{:S(2)}, u32[]{:S(2)}) %collective-permute-start.11) | collective-permute-done | bytes 327712 | tf_op jit(solution)/shard_map/ppermute | solution.py:21
  70.4 3.6 %collective-permute-done.12 = bf16[2,32,2560]{2,1,0:T(8,128)(2,1)S(1)} collective-permute-done((bf16[2,32,2560]{2,1,0:T(8,128)(2,1)S(1)}, bf16[2,32,2560]{2,1,0:T(8,128)(2,1)S(1)}, u32[]{:S(2)}, u32[]{:S(2)}) %collective-permute-start.12) | collective-permute-done | bytes 327712 | tf_op jit(solution)/shard_map/ppermute | solution.py:21
  74.2 1.8 %fusion.2.refs_1_ = f32[512,640]{1,0:T(8,128)S(1)} fusion(bf16[1920,640]{1,0:T(8,128)(2,1)S(1)} %get-tuple-element.85, bf16[512,2560]{1,0:T(8,128)(2,1)S(1)} %bitcast.76), kind=kOutput, calls=%fused_computation.4 | convolution fusion | flops 1258291200 | bytes 5734400 | tf_op jit(solution)/shard_map/dot_general | solution.py:183
  76.0 1.8 %fusion.refs_3_ = f32[512,640]{1,0:T(8,128)S(1)} fusion(bf16[1920,640]{1,0:T(8,128)(2,1)S(1)} %get-tuple-element.84, bf16[512,2560]{1,0:T(8,128)(2,1)S(1)} %bitcast.77), kind=kOutput, calls=%fused_computation.2 | convolution fusion | flops 1258291200 | bytes 5734400 | tf_op jit(solution)/shard_map/dot_general | solution.py:183
  78.7 2.6 %collective-permute-start.20 = (bf16[160,640]{1,0:T(8,128)(2,1)S(1)}, bf16[160,640]{1,0:T(8,128)(2,1)S(1)}, u32[]{:S(2)}, u32[]{:S(2)}) collective-permute-start(bf16[160,640]{1,0:T(8,128)(2,1)S(1)} %get-tuple-element.47), channel_id=1, source_target_pairs={{0,48},{16,0},{32,16},{48,32},{1,49},{17,1},{33,17},{49,33},{2,50}... | collective-permute-start | bytes 614408 | tf_op jit(solution)/shard_map/ppermute | solution.py:21
  81.4 1.2 convolution_add_fusion.refs_0_
  82.6 1.2 fusion.13
  84.3 2.2 %shard_map.74 = (f32[512,640]{1,0:T(8,128)S(1)}, bf16[512,640]{1,0:T(8,128)(2,1)S(1)}, f32[512,640]{1,0:T(8,128)S(1)}, bf16[512,640]{1,0:T(8,128)(2,1)S(1)}) custom-call(bf16[512,2560]{1,0:T(8,128)(2,1)S(1)} %bitcast.86, bf16[512,2560]{1,0:T(8,128)(2,1)S(1)} %bitcast.80, bf16[5,320,640]{2,1,0:T(8,128)(2,1)S(1)} %constant_dynamic-update-slice_fusion.10.far.extra, ...), custom_call_target="tpu_custom_call" | custom-call | flops 1000 | bytes 1000 | tf_op jit(solution)/shard_map/pallas_call | solution.py:132
  86.5 5.6 %collective-permute-start.17 = (bf16[512,640]{1,0:T(8,128)(2,1)S(1)}, bf16[512,640]{1,0:T(8,128)(2,1)S(1)}, u32[]{:S(2)}, u32[]{:S(2)}) collective-permute-start(bf16[512,640]{1,0:T(8,128)(2,1)S(1)} %get-tuple-element.43), channel_id=1, source_target_pairs={{0,8},{8,0},{1,9},{9,1},{2,10},{10,2},{3,11},{11,3},{4,12},{12,4},... | collective-permute-start | bytes 1966088 | tf_op jit(solution)/shard_map/ppermute | solution.py:21
  92.2 1.3 shard_map.75
  94.8 1.3 collective-permute-done.22.vb
  96.0 1.5 shard_map.76
  97.6 1.7 convolution_convert_fusion
  99.3 2.8 %collective-permute-start.23 = (bf16[64,1280]{1,0:T(8,128)(2,1)S(1)}, bf16[64,1280]{1,0:T(8,128)(2,1)S(1)}, u32[]{:S(2)}, u32[]{:S(2)}) collective-permute-start(bf16[64,1280]{1,0:T(8,128)(2,1)S(1)} %slice.239), channel_id=1, source_target_pairs={{0,4},{4,0},{1,5},{5,1},{2,6},{6,2},{3,7},{7,3},{8,12},{12,8},{9,1... | collective-permute-start | bytes 491528 | tf_op jit(solution)/shard_map/ppermute | solution.py:21
  102.7 1.4 collective-permute-start.27
  104.0 2.3 %collective-permute-done.23 = bf16[64,1280]{1,0:T(8,128)(2,1)S(1)} collective-permute-done((bf16[64,1280]{1,0:T(8,128)(2,1)S(1)}, bf16[64,1280]{1,0:T(8,128)(2,1)S(1)}, u32[]{:S(2)}, u32[]{:S(2)}) %collective-permute-start.23) | collective-permute-done | bytes 163872 | tf_op jit(solution)/shard_map/ppermute | solution.py:21
  106.3 1.1 shard_map.77
  107.4 2.7 %fusion.40 = (bf16[320,5120]{1,0:T(8,128)(2,1)S(1)}, f32[320,5120]{1,0:T(8,128)S(1)}) fusion(bf16[320,640]{1,0:T(8,128)(2,1)S(1)} %shard_map.77, bf16[640,5120]{1,0:T(8,128)(2,1)S(1)} %bitcast.89), kind=kOutput, calls=%fused_computation.88 | convolution fusion | flops 2098790400 | bytes 16793600 | tf_op jit(solution)/shard_map/dot_general | solution.py:218
  110.2 6.8 %collective-permute-done.24 = bf16[64,3840]{1,0:T(8,128)(2,1)S(1)} collective-permute-done((bf16[64,3840]{1,0:T(8,128)(2,1)S(1)}, bf16[64,3840]{1,0:T(8,128)(2,1)S(1)}, u32[]{:S(2)}, u32[]{:S(2)}) %collective-permute-start.24) | collective-permute-done | bytes 491552 | tf_op jit(solution)/shard_map/ppermute | solution.py:21
  117.3 1.4 collective-permute-start.25
  119.4 2.8 %collective-permute-start.33 = (bf16[64,5120]{1,0:T(8,128)(2,1)S(1)}, bf16[64,5120]{1,0:T(8,128)(2,1)S(1)}, u32[]{:S(2)}, u32[]{:S(2)}) collective-permute-start(bf16[64,5120]{1,0:T(8,128)(2,1)S(1)} %add_convert_fusion), channel_id=1, source_target_pairs={{0,4},{4,0},{1,5},{5,1},{2,6},{6,2},{3,7},{7,3},{8,12},{12,8},{9,1... | collective-permute-start | bytes 1966088 | tf_op jit(solution)/shard_map/ppermute | solution.py:21
  122.2 2.7 %collective-permute-start.30 = (bf16[64,2560]{1,0:T(8,128)(2,1)S(1)}, bf16[64,2560]{1,0:T(8,128)(2,1)S(1)}, u32[]{:S(2)}, u32[]{:S(2)}) collective-permute-start(bf16[64,2560]{1,0:T(8,128)(2,1)S(1)} %get-tuple-element.57), channel_id=1, source_target_pairs={{0,3},{1,0},{2,1},{3,2},{4,7},{5,4},{6,5},{7,6},{8,11},{9,8},{10,9... | collective-permute-start | bytes 983048 | tf_op jit(solution)/shard_map/ppermute | solution.py:21
  126.8 2.6 %collective-permute-start.32 = (bf16[64,2560]{1,0:T(8,128)(2,1)S(1)}, bf16[64,2560]{1,0:T(8,128)(2,1)S(1)}, u32[]{:S(2)}, u32[]{:S(2)}) collective-permute-start(bf16[64,2560]{1,0:T(8,128)(2,1)S(1)} %get-tuple-element.59), channel_id=1, source_target_pairs={{0,3},{1,0},{2,1},{3,2},{4,7},{5,4},{6,5},{7,6},{8,11},{9,8},{10,9... | collective-permute-start | bytes 983048 | tf_op jit(solution)/shard_map/ppermute | solution.py:21
  129.4 4.1 %collective-permute-done.29 = bf16[64,2560]{1,0:T(8,128)(2,1)S(1)} collective-permute-done((bf16[64,2560]{1,0:T(8,128)(2,1)S(1)}, bf16[64,2560]{1,0:T(8,128)(2,1)S(1)}, u32[]{:S(2)}, u32[]{:S(2)}) %collective-permute-start.29) | collective-permute-done | bytes 327712 | tf_op jit(solution)/shard_map/ppermute | solution.py:21
  133.6 7.0 %collective-permute-done.26 = bf16[64,2560]{1,0:T(8,128)(2,1)S(1)} collective-permute-done((bf16[64,2560]{1,0:T(8,128)(2,1)S(1)}, bf16[64,2560]{1,0:T(8,128)(2,1)S(1)}, u32[]{:S(2)}, u32[]{:S(2)}) %collective-permute-start.26) | collective-permute-done | bytes 327712 | tf_op jit(solution)/shard_map/ppermute | solution.py:21
  141.2 17.0 %all_to_all.10 = bf16[16,4,5120]{2,1,0:T(4,128)(2,1)S(1)} all-to-all(bf16[16,4,5120]{2,1,0:T(4,128)(2,1)S(1)} %reshape.14), channel_id=1, replica_groups=mesh['xl'=2,'y'=4,'core'=2,'xh'=2,'z'=4] {'xl','y','core'}, dimensions={0} | all-to-all | bytes 1310720 | tf_op jit(solution)/shard_map/all_to_all | solution.py:240
  158.5 15.1 %all_to_all.11 = bf16[16,4,5120]{2,1,0:T(4,128)(2,1)S(1)} all-to-all(bf16[16,4,5120]{2,1,0:T(4,128)(2,1)S(1)} %reduce-window_convert_fusion), channel_id=1, replica_groups=mesh['xl'=2,'y'=4,'core'=2,'xh'=2,'z'=4] {'xl','y','core'}, dimensions={0} | all-to-all | bytes 1310720 | tf_op jit(solution)/shard_map/all_to_all | solution.py:242
  173.6 1.2 add_bitcast_fusion
  (109 shorter events, 14.3 us)
Async XLA Ops:
  0.0 5.4 %copy-start = (bf16[3,320,640]{2,1,0:T(8,128)(2,1)S(1)}, bf16[3,320,640]{2,1,0:T(8,128)(2,1)}, u32[]{:S(2)}) copy-start(bf16[3,320,640]{2,1,0:T(8,128)(2,1)} %param.12) | copy-start | bytes 3686404
  4.0 5.6 %collective-permute-start = (bf16[64,2560]{1,0:T(8,128)(2,1)}, bf16[64,2560]{1,0:T(8,128)(2,1)S(1)}, u32[]{:S(2)}, u32[]{:S(2)}) collective-permute-start(bf16[64,2560]{1,0:T(8,128)(2,1)} %get-tuple-element.34), channel_id=1, source_target_pairs={{0,8},{8,0},{1,9},{9,1},{2,10},{10,2},{3,11},{11,3},{4,12},{12,4},... | collective-permute-start | bytes 983048 | tf_op jit(solution)/shard_map/ppermute | solution.py:21
  5.4 29.2 %collective-permute-start.2 = (bf16[3,320,640]{2,1,0:T(8,128)(2,1)S(1)}, bf16[3,320,640]{2,1,0:T(8,128)(2,1)S(1)}, u32[]{:S(2)}, u32[]{:S(2)}) collective-permute-start(bf16[3,320,640]{2,1,0:T(8,128)(2,1)S(1)} %copy-done), channel_id=1, source_target_pairs={{0,48},{16,0},{32,16},{48,32},{1,49},{17,1},{33,17},{49,33},{2,50}... | collective-permute-start | bytes 3686408 | tf_op jit(solution)/shard_map/ppermute | solution.py:21
  8.2 29.5 %collective-permute-start.3 = (bf16[3,320,640]{2,1,0:T(8,128)(2,1)S(1)}, bf16[3,320,640]{2,1,0:T(8,128)(2,1)S(1)}, u32[]{:S(2)}, u32[]{:S(2)}) collective-permute-start(bf16[3,320,640]{2,1,0:T(8,128)(2,1)S(1)} %copy-done), channel_id=1, source_target_pairs={{0,16},{16,32},{32,48},{48,0},{1,17},{17,33},{33,49},{49,1},{2,18}... | collective-permute-start | bytes 3686408 | tf_op jit(solution)/shard_map/ppermute | solution.py:21
  8.3 19.6 %collective-permute-start.7 = (bf16[2,320,640]{2,1,0:T(8,128)(2,1)S(1)}, bf16[2,320,640]{2,1,0:T(8,128)(2,1)S(1)}, u32[]{:S(2)}, u32[]{:S(2)}) collective-permute-start(bf16[2,320,640]{2,1,0:T(8,128)(2,1)S(1)} %slice.162), channel_id=1, source_target_pairs={{0,64},{64,0},{1,65},{65,1},{2,66},{66,2},{3,67},{67,3},{4,68},{68... | collective-permute-start | bytes 2457608 | tf_op jit(solution)/shard_map/ppermute | solution.py:21
  10.7 20.0 %collective-permute-start.1 = (bf16[2,64,2560]{2,1,0:T(8,128)(2,1)S(1)}, bf16[2,64,2560]{2,1,0:T(8,128)(2,1)S(1)}, u32[]{:S(2)}, u32[]{:S(2)}) collective-permute-start(bf16[2,64,2560]{2,1,0:T(8,128)(2,1)S(1)} %pad_maximum_fusion.5), channel_id=1, source_target_pairs={{0,3},{1,0},{2,1},{3,2},{4,7},{5,4},{6,5},{7,6},{8,11},{9,8},{10,9... | collective-permute-start | bytes 1966088 | tf_op jit(solution)/shard_map/ppermute | solution.py:21
  14.5 16.5 %collective-permute-start.5 = (bf16[2,64,2560]{2,1,0:T(8,128)(2,1)S(1)}, bf16[2,64,2560]{2,1,0:T(8,128)(2,1)S(1)}, u32[]{:S(2)}, u32[]{:S(2)}) collective-permute-start(bf16[2,64,2560]{2,1,0:T(8,128)(2,1)S(1)} %pad_maximum_fusion.5), channel_id=1, source_target_pairs={{0,1},{1,2},{2,3},{3,0},{4,5},{5,6},{6,7},{7,4},{8,9},{9,10},{10,1... | collective-permute-start | bytes 1966088 | tf_op jit(solution)/shard_map/ppermute | solution.py:21
  27.9 16.5 %collective-permute-start.8 = (bf16[2,64,2560]{2,1,0:T(8,128)(2,1)S(1)}, bf16[2,64,2560]{2,1,0:T(8,128)(2,1)S(1)}, u32[]{:S(2)}, u32[]{:S(2)}) collective-permute-start(bf16[2,64,2560]{2,1,0:T(8,128)(2,1)S(1)} %pad_maximum_fusion.5), channel_id=1, source_target_pairs={{0,4},{4,0},{1,5},{5,1},{2,6},{6,2},{3,7},{7,3},{8,12},{12,8},{9,1... | collective-permute-start | bytes 1966088 | tf_op jit(solution)/shard_map/ppermute | solution.py:21
  31.0 21.1 %collective-permute-start.13 = (bf16[2,320,640]{2,1,0:T(8,128)(2,1)S(1)}, bf16[2,320,640]{2,1,0:T(8,128)(2,1)S(1)}, u32[]{:S(2)}, u32[]{:S(2)}) collective-permute-start(bf16[2,320,640]{2,1,0:T(8,128)(2,1)S(1)} %collective-permute-done.7), channel_id=1, source_target_pairs={{0,48},{16,0},{32,16},{48,32},{1,49},{17,1},{33,17},{49,33},{2,50}... | collective-permute-start | bytes 2457608 | tf_op jit(solution)/shard_map/ppermute | solution.py:21
  33.4 21.4 %collective-permute-start.15 = (bf16[2,320,640]{2,1,0:T(8,128)(2,1)S(1)}, bf16[2,320,640]{2,1,0:T(8,128)(2,1)S(1)}, u32[]{:S(2)}, u32[]{:S(2)}) collective-permute-start(bf16[2,320,640]{2,1,0:T(8,128)(2,1)S(1)} %collective-permute-done.7), channel_id=1, source_target_pairs={{0,16},{16,32},{32,48},{48,0},{1,17},{17,33},{33,49},{49,1},{2,18}... | collective-permute-start | bytes 2457608 | tf_op jit(solution)/shard_map/ppermute | solution.py:21
  34.6 7.0 %copy-start.3 = (bf16[3,320,640]{2,1,0:T(8,128)(2,1)}, bf16[3,320,640]{2,1,0:T(8,128)(2,1)S(1)}, u32[]{:S(2)}) copy-start(bf16[3,320,640]{2,1,0:T(8,128)(2,1)S(1)} %collective-permute-done.2) | copy-start | bytes 3686404
  37.7 3.9 %copy-start.1 = (bf16[3,320,640]{2,1,0:T(8,128)(2,1)}, bf16[3,320,640]{2,1,0:T(8,128)(2,1)S(1)}, u32[]{:S(2)}) copy-start(bf16[3,320,640]{2,1,0:T(8,128)(2,1)S(1)} %collective-permute-done.3) | copy-start | bytes 3686404
  37.7 8.8 %collective-permute-start.4 = (bf16[2,32,2560]{2,1,0:T(8,128)(2,1)S(1)}, bf16[2,32,2560]{2,1,0:T(8,128)(2,1)S(1)}, u32[]{:S(2)}, u32[]{:S(2)}) collective-permute-start(bf16[2,32,2560]{2,1,0:T(8,128)(2,1)S(1)} %slice.208), channel_id=1, source_target_pairs={{0,3},{1,0},{2,1},{3,2},{4,7},{5,4},{6,5},{7,6},{8,11},{9,8},{10,9... | collective-permute-start | bytes 983048 | tf_op jit(solution)/shard_map/ppermute | solution.py:21
  41.5 8.2 %collective-permute-start.6 = (bf16[2,32,2560]{2,1,0:T(8,128)(2,1)S(1)}, bf16[2,32,2560]{2,1,0:T(8,128)(2,1)S(1)}, u32[]{:S(2)}, u32[]{:S(2)}) collective-permute-start(bf16[2,32,2560]{2,1,0:T(8,128)(2,1)S(1)} %slice.209), channel_id=1, source_target_pairs={{0,1},{1,2},{2,3},{3,0},{4,5},{5,6},{6,7},{7,4},{8,9},{9,10},{10,1... | collective-permute-start | bytes 983048 | tf_op jit(solution)/shard_map/ppermute | solution.py:21
  41.9 9.3 %copy-start.4 = (bf16[64,2560]{1,0:T(8,128)(2,1)S(1)}, bf16[64,2560]{1,0:T(8,128)(2,1)}, u32[]{:S(2)}) copy-start(bf16[64,2560]{1,0:T(8,128)(2,1)} %get-tuple-element.33) | copy-start | bytes 983044
  44.4 34.1 %collective-permute-start.19 = (bf16[3,320,640]{2,1,0:T(8,128)(2,1)S(1)}, bf16[3,320,640]{2,1,0:T(8,128)(2,1)S(1)}, u32[]{:S(2)}, u32[]{:S(2)}) collective-permute-start(bf16[3,320,640]{2,1,0:T(8,128)(2,1)S(1)} %pad_maximum_fusion.1), channel_id=1, source_target_pairs={{0,64},{64,0},{1,65},{65,1},{2,66},{66,2},{3,67},{67,3},{4,68},{68... | collective-permute-start | bytes 3686408 | tf_op jit(solution)/shard_map/ppermute | solution.py:21
  49.6 13.1 %collective-permute-start.9 = (bf16[2,64,2560]{2,1,0:T(8,128)(2,1)S(1)}, bf16[2,64,2560]{2,1,0:T(8,128)(2,1)S(1)}, u32[]{:S(2)}, u32[]{:S(2)}) collective-permute-start(bf16[2,64,2560]{2,1,0:T(8,128)(2,1)S(1)} %collective-permute-done.8), channel_id=1, source_target_pairs={{0,3},{1,0},{2,1},{3,2},{4,7},{5,4},{6,5},{7,6},{8,11},{9,8},{10,9... | collective-permute-start | bytes 1966088 | tf_op jit(solution)/shard_map/ppermute | solution.py:21
  49.9 14.3 %collective-permute-start.10 = (bf16[2,64,2560]{2,1,0:T(8,128)(2,1)S(1)}, bf16[2,64,2560]{2,1,0:T(8,128)(2,1)S(1)}, u32[]{:S(2)}, u32[]{:S(2)}) collective-permute-start(bf16[2,64,2560]{2,1,0:T(8,128)(2,1)S(1)} %collective-permute-done.8), channel_id=1, source_target_pairs={{0,1},{1,2},{2,3},{3,0},{4,5},{5,6},{6,7},{7,4},{8,9},{9,10},{10,1... | collective-permute-start | bytes 1966088 | tf_op jit(solution)/shard_map/ppermute | solution.py:21
  51.3 1.1 slice-start.3
  52.1 2.8 %slice-start.2 = ((bf16[3,320,640]{2,1,0:T(8,128)(2,1)}), bf16[3,160,640]{2,1,0:T(8,128)(2,1)S(1)}, s32[]{:S(2)}) async-start(bf16[3,320,640]{2,1,0:T(8,128)(2,1)} %copy-done.1), calls=%async_computation.4 | async-start | bytes 1228800 | tf_op jit(solution)/shard_map/slice | solution.py:166
  52.5 2.8 %copy-start.2 = (bf16[3,320,640]{2,1,0:T(8,128)(2,1)S(1)}, bf16[3,320,640]{2,1,0:T(8,128)(2,1)}, u32[]{:S(2)}) copy-start(bf16[3,320,640]{2,1,0:T(8,128)(2,1)} %copy-done.1) | copy-start | bytes 3686404
  52.5 31.5 %collective-permute-start.14 = (bf16[5,160,640]{2,1,0:T(8,128)(2,1)S(1)}, bf16[5,160,640]{2,1,0:T(8,128)(2,1)S(1)}, u32[]{:S(2)}, u32[]{:S(2)}) collective-permute-start(bf16[5,160,640]{2,1,0:T(8,128)(2,1)S(1)} %pad_maximum_fusion.2), channel_id=1, source_target_pairs={{0,48},{16,0},{32,16},{48,32},{1,49},{17,1},{33,17},{49,33},{2,50}... | collective-permute-start | bytes 3072008 | tf_op jit(solution)/shard_map/ppermute | solution.py:21
  55.0 29.1 %collective-permute-start.16 = (bf16[5,160,640]{2,1,0:T(8,128)(2,1)S(1)}, bf16[5,160,640]{2,1,0:T(8,128)(2,1)S(1)}, u32[]{:S(2)}, u32[]{:S(2)}) collective-permute-start(bf16[5,160,640]{2,1,0:T(8,128)(2,1)S(1)} %pad_maximum_fusion.3), channel_id=1, source_target_pairs={{0,16},{16,32},{32,48},{48,0},{1,17},{17,33},{33,49},{49,1},{2,18}... | collective-permute-start | bytes 3072008 | tf_op jit(solution)/shard_map/ppermute | solution.py:21
  64.2 6.2 %collective-permute-start.11 = (bf16[2,32,2560]{2,1,0:T(8,128)(2,1)S(1)}, bf16[2,32,2560]{2,1,0:T(8,128)(2,1)S(1)}, u32[]{:S(2)}, u32[]{:S(2)}) collective-permute-start(bf16[2,32,2560]{2,1,0:T(8,128)(2,1)S(1)} %slice.210), channel_id=1, source_target_pairs={{0,3},{1,0},{2,1},{3,2},{4,7},{5,4},{6,5},{7,6},{8,11},{9,8},{10,9... | collective-permute-start | bytes 983048 | tf_op jit(solution)/shard_map/ppermute | solution.py:21
  66.5 7.5 %collective-permute-start.12 = (bf16[2,32,2560]{2,1,0:T(8,128)(2,1)S(1)}, bf16[2,32,2560]{2,1,0:T(8,128)(2,1)S(1)}, u32[]{:S(2)}, u32[]{:S(2)}) collective-permute-start(bf16[2,32,2560]{2,1,0:T(8,128)(2,1)S(1)} %slice.211), channel_id=1, source_target_pairs={{0,1},{1,2},{2,3},{3,0},{4,5},{5,6},{6,7},{7,4},{8,9},{9,10},{10,1... | collective-permute-start | bytes 983048 | tf_op jit(solution)/shard_map/ppermute | solution.py:21
  78.6 13.6 %collective-permute-start.21 = (bf16[160,640]{1,0:T(8,128)(2,1)S(1)}, bf16[160,640]{1,0:T(8,128)(2,1)S(1)}, u32[]{:S(2)}, u32[]{:S(2)}) collective-permute-start(bf16[160,640]{1,0:T(8,128)(2,1)S(1)} %get-tuple-element.48), channel_id=1, source_target_pairs={{0,16},{16,32},{32,48},{48,0},{1,17},{17,33},{33,49},{49,1},{2,18}... | collective-permute-start | bytes 614408 | tf_op jit(solution)/shard_map/ppermute | solution.py:21
  78.7 13.5 %collective-permute-start.20 = (bf16[160,640]{1,0:T(8,128)(2,1)S(1)}, bf16[160,640]{1,0:T(8,128)(2,1)S(1)}, u32[]{:S(2)}, u32[]{:S(2)}) collective-permute-start(bf16[160,640]{1,0:T(8,128)(2,1)S(1)} %get-tuple-element.47), channel_id=1, source_target_pairs={{0,48},{16,0},{32,16},{48,32},{1,49},{17,1},{33,17},{49,33},{2,50}... | collective-permute-start | bytes 614408 | tf_op jit(solution)/shard_map/ppermute | solution.py:21
  84.3 13.3 %slice-start = ((s8[6553600]{0:T(1024)(128)(4,1)}), s8[4194304]{0:T(1024)(128)(4,1)S(1)}, s32[]{:S(2)}) async-start(s8[6553600]{0:T(1024)(128)(4,1)} %bitcast.88), calls=%async_computation.2 | async-start | bytes 8388608
  86.5 7.8 %collective-permute-start.17 = (bf16[512,640]{1,0:T(8,128)(2,1)S(1)}, bf16[512,640]{1,0:T(8,128)(2,1)S(1)}, u32[]{:S(2)}, u32[]{:S(2)}) collective-permute-start(bf16[512,640]{1,0:T(8,128)(2,1)S(1)} %get-tuple-element.43), channel_id=1, source_target_pairs={{0,8},{8,0},{1,9},{9,1},{2,10},{10,2},{3,11},{11,3},{4,12},{12,4},... | collective-permute-start | bytes 1966088 | tf_op jit(solution)/shard_map/ppermute | solution.py:21
  92.1 2.7 %collective-permute-start.18 = (bf16[512,640]{1,0:T(8,128)(2,1)S(1)}, bf16[512,640]{1,0:T(8,128)(2,1)S(1)}, u32[]{:S(2)}, u32[]{:S(2)}) collective-permute-start(bf16[512,640]{1,0:T(8,128)(2,1)S(1)} %get-tuple-element.45), channel_id=1, source_target_pairs={{0,8},{8,0},{1,9},{9,1},{2,10},{10,2},{3,11},{11,3},{4,12},{12,4},... | collective-permute-start | bytes 1966088 | tf_op jit(solution)/shard_map/ppermute | solution.py:21
  92.2 5.3 %slice-start.1 = ((s8[6553600]{0:T(1024)(128)(4,1)}), s8[2359296]{0:T(1024)(128)(4,1)S(1)}, s32[]{:S(2)}) async-start(s8[6553600]{0:T(1024)(128)(4,1)} %bitcast.88), calls=%async_computation.3 | async-start | bytes 4718592
  93.6 2.4 %collective-permute-start.22 = (bf16[512,640]{1,0:T(8,128)(2,1)S(1)}, bf16[512,640]{1,0:T(8,128)(2,1)S(1)}, u32[]{:S(2)}, u32[]{:S(2)}) collective-permute-start(bf16[512,640]{1,0:T(8,128)(2,1)S(1)} %get-tuple-element.50), channel_id=1, source_target_pairs={{0,8},{8,0},{1,9},{9,1},{2,10},{10,2},{3,11},{11,3},{4,12},{12,4},... | collective-permute-start | bytes 1966088 | tf_op jit(solution)/shard_map/ppermute | solution.py:21
  99.3 7.0 %collective-permute-start.23 = (bf16[64,1280]{1,0:T(8,128)(2,1)S(1)}, bf16[64,1280]{1,0:T(8,128)(2,1)S(1)}, u32[]{:S(2)}, u32[]{:S(2)}) collective-permute-start(bf16[64,1280]{1,0:T(8,128)(2,1)S(1)} %slice.239), channel_id=1, source_target_pairs={{0,4},{4,0},{1,5},{5,1},{2,6},{6,2},{3,7},{7,3},{8,12},{12,8},{9,1... | collective-permute-start | bytes 491528 | tf_op jit(solution)/shard_map/ppermute | solution.py:21
  102.3 16.5 %collective-permute-start.28 = (bf16[64,5120]{1,0:T(8,128)(2,1)S(1)}, bf16[64,5120]{1,0:T(8,128)(2,1)S(1)}, u32[]{:S(2)}, u32[]{:S(2)}) collective-permute-start(bf16[64,5120]{1,0:T(8,128)(2,1)S(1)} %get-tuple-element.66), channel_id=1, source_target_pairs={{0,3},{1,0},{2,1},{3,2},{4,7},{5,4},{6,5},{7,6},{8,11},{9,8},{10,9... | collective-permute-start | bytes 1966088 | tf_op jit(solution)/shard_map/ppermute | solution.py:21
  102.3 14.6 %collective-permute-start.24 = (bf16[64,3840]{1,0:T(8,128)(2,1)S(1)}, bf16[64,3840]{1,0:T(8,128)(2,1)S(1)}, u32[]{:S(2)}, u32[]{:S(2)}) collective-permute-start(bf16[64,3840]{1,0:T(8,128)(2,1)S(1)} %slice.243), channel_id=1, source_target_pairs={{0,4},{4,0},{1,5},{5,1},{2,6},{6,2},{3,7},{7,3},{8,12},{12,8},{9,1... | collective-permute-start | bytes 1474568 | tf_op jit(solution)/shard_map/ppermute | solution.py:21
  102.7 16.5 %collective-permute-start.27 = (bf16[64,5120]{1,0:T(8,128)(2,1)S(1)}, bf16[64,5120]{1,0:T(8,128)(2,1)S(1)}, u32[]{:S(2)}, u32[]{:S(2)}) collective-permute-start(bf16[64,5120]{1,0:T(8,128)(2,1)S(1)} %get-tuple-element.65), channel_id=1, source_target_pairs={{0,1},{1,2},{2,3},{3,0},{4,5},{5,6},{6,7},{7,4},{8,9},{9,10},{10,1... | collective-permute-start | bytes 1966088 | tf_op jit(solution)/shard_map/ppermute | solution.py:21
  117.2 8.2 %collective-permute-start.31 = (bf16[64,2560]{1,0:T(8,128)(2,1)S(1)}, bf16[64,2560]{1,0:T(8,128)(2,1)S(1)}, u32[]{:S(2)}, u32[]{:S(2)}) collective-permute-start(bf16[64,2560]{1,0:T(8,128)(2,1)S(1)} %get-tuple-element.90), channel_id=1, source_target_pairs={{0,3},{1,0},{2,1},{3,2},{4,7},{5,4},{6,5},{7,6},{8,11},{9,8},{10,9... | collective-permute-start | bytes 983048 | tf_op jit(solution)/shard_map/ppermute | solution.py:21
  117.3 23.3 %copy-start.6 = (f32[1,5120]{1,0:T(1,128)S(1)}, f32[1,5120]{1,0:T(1,128)}, u32[]{:S(2)}) copy-start(f32[1,5120]{1,0:T(1,128)} %get-tuple-element.32) | copy-start | bytes 61444
  117.3 9.2 %collective-permute-start.25 = (bf16[64,2560]{1,0:T(8,128)(2,1)S(1)}, bf16[64,2560]{1,0:T(8,128)(2,1)S(1)}, u32[]{:S(2)}, u32[]{:S(2)}) collective-permute-start(bf16[64,2560]{1,0:T(8,128)(2,1)S(1)} %get-tuple-element.91), channel_id=1, source_target_pairs={{0,1},{1,2},{2,3},{3,0},{4,5},{5,6},{6,7},{7,4},{8,9},{9,10},{10,1... | collective-permute-start | bytes 983048 | tf_op jit(solution)/shard_map/ppermute | solution.py:21
  119.4 21.2 %collective-permute-start.33 = (bf16[64,5120]{1,0:T(8,128)(2,1)S(1)}, bf16[64,5120]{1,0:T(8,128)(2,1)S(1)}, u32[]{:S(2)}, u32[]{:S(2)}) collective-permute-start(bf16[64,5120]{1,0:T(8,128)(2,1)S(1)} %add_convert_fusion), channel_id=1, source_target_pairs={{0,4},{4,0},{1,5},{5,1},{2,6},{6,2},{3,7},{7,3},{8,12},{12,8},{9,1... | collective-permute-start | bytes 1966088 | tf_op jit(solution)/shard_map/ppermute | solution.py:21
  122.2 11.3 %collective-permute-start.29 = (bf16[64,2560]{1,0:T(8,128)(2,1)S(1)}, bf16[64,2560]{1,0:T(8,128)(2,1)S(1)}, u32[]{:S(2)}, u32[]{:S(2)}) collective-permute-start(bf16[64,2560]{1,0:T(8,128)(2,1)S(1)} %get-tuple-element.56), channel_id=1, source_target_pairs={{0,1},{1,2},{2,3},{3,0},{4,5},{5,6},{6,7},{7,4},{8,9},{9,10},{10,1... | collective-permute-start | bytes 983048 | tf_op jit(solution)/shard_map/ppermute | solution.py:21
  122.2 11.3 %collective-permute-start.30 = (bf16[64,2560]{1,0:T(8,128)(2,1)S(1)}, bf16[64,2560]{1,0:T(8,128)(2,1)S(1)}, u32[]{:S(2)}, u32[]{:S(2)}) collective-permute-start(bf16[64,2560]{1,0:T(8,128)(2,1)S(1)} %get-tuple-element.57), channel_id=1, source_target_pairs={{0,3},{1,0},{2,1},{3,2},{4,7},{5,4},{6,5},{7,6},{8,11},{9,8},{10,9... | collective-permute-start | bytes 983048 | tf_op jit(solution)/shard_map/ppermute | solution.py:21
  126.7 13.9 %collective-permute-start.26 = (bf16[64,2560]{1,0:T(8,128)(2,1)S(1)}, bf16[64,2560]{1,0:T(8,128)(2,1)S(1)}, u32[]{:S(2)}, u32[]{:S(2)}) collective-permute-start(bf16[64,2560]{1,0:T(8,128)(2,1)S(1)} %get-tuple-element.60), channel_id=1, source_target_pairs={{0,1},{1,2},{2,3},{3,0},{4,5},{5,6},{6,7},{7,4},{8,9},{9,10},{10,1... | collective-permute-start | bytes 983048 | tf_op jit(solution)/shard_map/ppermute | solution.py:21
  126.8 13.8 %collective-permute-start.32 = (bf16[64,2560]{1,0:T(8,128)(2,1)S(1)}, bf16[64,2560]{1,0:T(8,128)(2,1)S(1)}, u32[]{:S(2)}, u32[]{:S(2)}) collective-permute-start(bf16[64,2560]{1,0:T(8,128)(2,1)S(1)} %get-tuple-element.59), channel_id=1, source_target_pairs={{0,3},{1,0},{2,1},{3,2},{4,7},{5,4},{6,5},{7,6},{8,11},{9,8},{10,9... | collective-permute-start | bytes 983048 | tf_op jit(solution)/shard_map/ppermute | solution.py:21
  158.2 15.4 %copy-start.5 = (f32[64,5120]{1,0:T(8,128)S(1)}, f32[64,5120]{1,0:T(8,128)}, u32[]{:S(2)}) copy-start(f32[64,5120]{1,0:T(8,128)} %param.8) | copy-start | bytes 3932164

commit v7 on v5

--- a/solution.py
+++ b/solution.py
@@ -86,7 +86,7 @@
 
 def attend(query, keys, values):
     scores = lax.dot_general(query, keys, (((1,), (1,)), ((), ())), preferred_element_type=F32)
-    expo = jnp.exp(scores * HEAD_DIM ** (-0.5))
+    expo = jnp.exp2(scores * (HEAD_DIM ** (-0.5) * 1.4426950408889634))
     total = jnp.sum(expo, axis=-1, keepdims=True)
     return (
         jnp.dot(expo.astype(BF16), values, preferred_element_type=F32) * (1.0 / total)

time: 175 us -> 175 us (level)
  no operation moved by 1% of the time
where the time goes in v7:
time: 175 us
  waiting for transfers between devices  61.6 us (35%)
  starting transfers between devices  48.4 us (28%)
  blocking collectives  31.7 us (18%)
  matrix products  15.3 us (9%)
  Pallas kernels  9.58 us (5%)
  other arithmetic  4.03 us (2%)
  local copies, waits for them, and re-layouts  2.67 us (2%)
    ppermute x34, waiting for transfers between devices, send(): lax.ppermute(array, axis, [(i, (i + shift) % size) for i in range(size)])  61.6 us
    ppermute x34, starting transfers between devices, send(): lax.ppermute(array, axis, [(i, (i + shift) % size) for i in range(size)])  48.4 us
    all_to_all x1, blocking collectives, on_device(): lax.all_to_all(term.reshape(steps, tokens // steps, width), TM, 0, 0)  16.7 us
    all_to_all x1, blocking collectives, on_device(): total = lax.all_to_all(total, TM, 0, 0).reshape(tokens, width)  15.1 us
    dot_general x8, matrix products, product(): jnp.dot(f[:, begin:stop], weight, preferred_element_type=F32)  10.9 us
    pallas_call x4, Pallas kernels, local_call(): pl.pallas_call(kernel, out_shape=[jax.ShapeDtypeStruct(*shape) for shape...  6.39 us
  transfers between devices with their start and end apart: 34, of which 20 were waited for; matrix products, arithmetic and copies ran while one was open for 10% of the time, Pallas kernels for 3%

profile of v7, /device:TPU:1, one launch (start us, length us, event | category | flops | bytes accessed | tf_op | source)
XLA Modules:
  0.0 174.7 jit_solution(4773584413278275267)
XLA Ops:
  0.8 3.2 %shard_map.73 = (bf16[64,2560]{1,0:T(8,128)(2,1)}, bf16[64,2560]{1,0:T(8,128)(2,1)}, f32[1,5120]{1,0:T(1,128)}) custom-call(s32[1]{0:T(128)S(6)} %copy.27.t_ref, f32[1,64,5120]{2,1,0:T(8,128)} %state_ref.1, f32[3,50,5120]{2,1,0:T(8,128)} %bitcast.90, f32[50]{0:T(128)} %coef_ref.1), custom_call_target="tpu_custom_call" | custom-call | flops 1000 | bytes 1000 | tf_op jit(solution)/shard_map/pallas_call | solution.py:60
  3.9 1.4 collective-permute-start
  5.4 2.8 %collective-permute-start.2 = (bf16[3,320,640]{2,1,0:T(8,128)(2,1)S(1)}, bf16[3,320,640]{2,1,0:T(8,128)(2,1)S(1)}, u32[]{:S(2)}, u32[]{:S(2)}) collective-permute-start(bf16[3,320,640]{2,1,0:T(8,128)(2,1)S(1)} %copy-done), channel_id=1, source_target_pairs={{0,48},{16,0},{32,16},{48,32},{1,49},{17,1},{33,17},{49,33},{2,50}... | collective-permute-start | bytes 3686408 | tf_op jit(solution)/shard_map/ppermute | solution.py:21
  8.3 1.3 collective-permute-start.7
  10.6 3.8 %collective-permute-start.1 = (bf16[2,64,2560]{2,1,0:T(8,128)(2,1)S(1)}, bf16[2,64,2560]{2,1,0:T(8,128)(2,1)S(1)}, u32[]{:S(2)}, u32[]{:S(2)}) collective-permute-start(bf16[2,64,2560]{2,1,0:T(8,128)(2,1)S(1)} %pad_maximum_fusion.5), channel_id=1, source_target_pairs={{0,3},{1,0},{2,1},{3,2},{4,7},{5,4},{6,5},{7,6},{8,11},{9,8},{10,9... | collective-permute-start | bytes 1966088 | tf_op jit(solution)/shard_map/ppermute | solution.py:21
  14.6 13.2 %collective-permute-done.7 = bf16[2,320,640]{2,1,0:T(8,128)(2,1)S(1)} collective-permute-done((bf16[2,320,640]{2,1,0:T(8,128)(2,1)S(1)}, bf16[2,320,640]{2,1,0:T(8,128)(2,1)S(1)}, u32[]{:S(2)}, u32[]{:S(2)}) %collective-permute-start.7) | collective-permute-done | bytes 819232 | tf_op jit(solution)/shard_map/ppermute | solution.py:21
  27.8 2.7 %collective-permute-start.8 = (bf16[2,64,2560]{2,1,0:T(8,128)(2,1)S(1)}, bf16[2,64,2560]{2,1,0:T(8,128)(2,1)S(1)}, u32[]{:S(2)}, u32[]{:S(2)}) collective-permute-start(bf16[2,64,2560]{2,1,0:T(8,128)(2,1)S(1)} %pad_maximum_fusion.5), channel_id=1, source_target_pairs={{0,4},{4,0},{1,5},{5,1},{2,6},{6,2},{3,7},{7,3},{8,12},{12,8},{9,1... | collective-permute-start | bytes 1966088 | tf_op jit(solution)/shard_map/ppermute | solution.py:21
  31.0 2.4 %collective-permute-start.13 = (bf16[2,320,640]{2,1,0:T(8,128)(2,1)S(1)}, bf16[2,320,640]{2,1,0:T(8,128)(2,1)S(1)}, u32[]{:S(2)}, u32[]{:S(2)}) collective-permute-start(bf16[2,320,640]{2,1,0:T(8,128)(2,1)S(1)} %collective-permute-done.7), channel_id=1, source_target_pairs={{0,48},{16,0},{32,16},{48,32},{1,49},{17,1},{33,17},{49,33},{2,50}... | collective-permute-start | bytes 2457608 | tf_op jit(solution)/shard_map/ppermute | solution.py:21
  33.4 1.2 collective-permute-done.2
  34.6 3.1 %collective-permute-done.3 = bf16[3,320,640]{2,1,0:T(8,128)(2,1)S(1)} collective-permute-done((bf16[3,320,640]{2,1,0:T(8,128)(2,1)S(1)}, bf16[3,320,640]{2,1,0:T(8,128)(2,1)S(1)}, u32[]{:S(2)}, u32[]{:S(2)}) %collective-permute-start.3) | collective-permute-done | bytes 1228832 | tf_op jit(solution)/shard_map/ppermute | solution.py:21
  37.7 3.8 %collective-permute-start.4 = (bf16[2,32,2560]{2,1,0:T(8,128)(2,1)S(1)}, bf16[2,32,2560]{2,1,0:T(8,128)(2,1)S(1)}, u32[]{:S(2)}, u32[]{:S(2)}) collective-permute-start(bf16[2,32,2560]{2,1,0:T(8,128)(2,1)S(1)} %slice.208), channel_id=1, source_target_pairs={{0,3},{1,0},{2,1},{3,2},{4,7},{5,4},{6,5},{7,6},{8,11},{9,8},{10,9... | collective-permute-start | bytes 983048 | tf_op jit(solution)/shard_map/ppermute | solution.py:21
  42.0 2.3 %collective-permute-done.8 = bf16[2,64,2560]{2,1,0:T(8,128)(2,1)S(1)} collective-permute-done((bf16[2,64,2560]{2,1,0:T(8,128)(2,1)S(1)}, bf16[2,64,2560]{2,1,0:T(8,128)(2,1)S(1)}, u32[]{:S(2)}, u32[]{:S(2)}) %collective-permute-start.8) | collective-permute-done | bytes 655392 | tf_op jit(solution)/shard_map/ppermute | solution.py:21
  44.4 1.2 collective-permute-start.19
  46.5 3.1 %collective-permute-done.6 = bf16[2,32,2560]{2,1,0:T(8,128)(2,1)S(1)} collective-permute-done((bf16[2,32,2560]{2,1,0:T(8,128)(2,1)S(1)}, bf16[2,32,2560]{2,1,0:T(8,128)(2,1)S(1)}, u32[]{:S(2)}, u32[]{:S(2)}) %collective-permute-start.6) | collective-permute-done | bytes 327712 | tf_op jit(solution)/shard_map/ppermute | solution.py:21
  49.9 1.2 collective-permute-start.10
  52.4 2.4 %collective-permute-start.14 = (bf16[5,160,640]{2,1,0:T(8,128)(2,1)S(1)}, bf16[5,160,640]{2,1,0:T(8,128)(2,1)S(1)}, u32[]{:S(2)}, u32[]{:S(2)}) collective-permute-start(bf16[5,160,640]{2,1,0:T(8,128)(2,1)S(1)} %pad_maximum_fusion.2), channel_id=1, source_target_pairs={{0,48},{16,0},{32,16},{48,32},{1,49},{17,1},{33,17},{49,33},{2,50}... | collective-permute-start | bytes 3072008 | tf_op jit(solution)/shard_map/ppermute | solution.py:21
  55.5 1.8 %fusion.6.refs_0_ = f32[512,640]{1,0:T(8,128)S(1)} fusion(bf16[1920,640]{1,0:T(8,128)(2,1)S(1)} %get-tuple-element.85, bf16[512,2560]{1,0:T(8,128)(2,1)S(1)} %bitcast.83), kind=kOutput, calls=%fused_computation.8 | convolution fusion | flops 1258291200 | bytes 5734400 | tf_op jit(solution)/shard_map/dot_general | solution.py:183
  57.2 5.4 %collective-permute-done.9 = bf16[2,64,2560]{2,1,0:T(8,128)(2,1)S(1)} collective-permute-done((bf16[2,64,2560]{2,1,0:T(8,128)(2,1)S(1)}, bf16[2,64,2560]{2,1,0:T(8,128)(2,1)S(1)}, u32[]{:S(2)}, u32[]{:S(2)}) %collective-permute-start.9) | collective-permute-done | bytes 655392 | tf_op jit(solution)/shard_map/ppermute | solution.py:21
  62.7 1.5 collective-permute-done.10
  64.7 1.8 %fusion.4.refs_2_ = f32[512,640]{1,0:T(8,128)S(1)} fusion(bf16[1920,640]{1,0:T(8,128)(2,1)S(1)} %get-tuple-element.84, bf16[512,2560]{1,0:T(8,128)(2,1)S(1)} %bitcast.84), kind=kOutput, calls=%fused_computation.6 | convolution fusion | flops 1258291200 | bytes 5734400 | tf_op jit(solution)/shard_map/dot_general | solution.py:183
  67.5 2.9 %collective-permute-done.11 = bf16[2,32,2560]{2,1,0:T(8,128)(2,1)S(1)} collective-permute-done((bf16[2,32,2560]{2,1,0:T(8,128)(2,1)S(1)}, bf16[2,32,2560]{2,1,0:T(8,128)(2,1)S(1)}, u32[]{:S(2)}, u32[]{:S(2)}) %collective-permute-start.11) | collective-permute-done | bytes 327712 | tf_op jit(solution)/shard_map/ppermute | solution.py:21
  70.4 3.6 %collective-permute-done.12 = bf16[2,32,2560]{2,1,0:T(8,128)(2,1)S(1)} collective-permute-done((bf16[2,32,2560]{2,1,0:T(8,128)(2,1)S(1)}, bf16[2,32,2560]{2,1,0:T(8,128)(2,1)S(1)}, u32[]{:S(2)}, u32[]{:S(2)}) %collective-permute-start.12) | collective-permute-done | bytes 327712 | tf_op jit(solution)/shard_map/ppermute | solution.py:21
  74.2 1.8 %fusion.2.refs_1_ = f32[512,640]{1,0:T(8,128)S(1)} fusion(bf16[1920,640]{1,0:T(8,128)(2,1)S(1)} %get-tuple-element.85, bf16[512,2560]{1,0:T(8,128)(2,1)S(1)} %bitcast.76), kind=kOutput, calls=%fused_computation.4 | convolution fusion | flops 1258291200 | bytes 5734400 | tf_op jit(solution)/shard_map/dot_general | solution.py:183
  75.9 1.8 %fusion.refs_3_ = f32[512,640]{1,0:T(8,128)S(1)} fusion(bf16[1920,640]{1,0:T(8,128)(2,1)S(1)} %get-tuple-element.84, bf16[512,2560]{1,0:T(8,128)(2,1)S(1)} %bitcast.77), kind=kOutput, calls=%fused_computation.2 | convolution fusion | flops 1258291200 | bytes 5734400 | tf_op jit(solution)/shard_map/dot_general | solution.py:183
  78.7 2.6 %collective-permute-start.20 = (bf16[160,640]{1,0:T(8,128)(2,1)S(1)}, bf16[160,640]{1,0:T(8,128)(2,1)S(1)}, u32[]{:S(2)}, u32[]{:S(2)}) collective-permute-start(bf16[160,640]{1,0:T(8,128)(2,1)S(1)} %get-tuple-element.47), channel_id=1, source_target_pairs={{0,48},{16,0},{32,16},{48,32},{1,49},{17,1},{33,17},{49,33},{2,50}... | collective-permute-start | bytes 614408 | tf_op jit(solution)/shard_map/ppermute | solution.py:21
  81.4 1.2 convolution_add_fusion.refs_0_
  82.6 1.2 fusion.13
  84.2 2.5 %shard_map.74 = (f32[512,640]{1,0:T(8,128)S(1)}, bf16[512,640]{1,0:T(8,128)(2,1)S(1)}, f32[512,640]{1,0:T(8,128)S(1)}, bf16[512,640]{1,0:T(8,128)(2,1)S(1)}) custom-call(bf16[512,2560]{1,0:T(8,128)(2,1)S(1)} %bitcast.86, bf16[512,2560]{1,0:T(8,128)(2,1)S(1)} %bitcast.80, bf16[5,320,640]{2,1,0:T(8,128)(2,1)S(1)} %constant_dynamic-update-slice_fusion.10.far.extra, ...), custom_call_target="tpu_custom_call" | custom-call | flops 1000 | bytes 1000 | tf_op jit(solution)/shard_map/pallas_call | solution.py:132
  86.7 5.6 %collective-permute-start.17 = (bf16[512,640]{1,0:T(8,128)(2,1)S(1)}, bf16[512,640]{1,0:T(8,128)(2,1)S(1)}, u32[]{:S(2)}, u32[]{:S(2)}) collective-permute-start(bf16[512,640]{1,0:T(8,128)(2,1)S(1)} %get-tuple-element.43), channel_id=1, source_target_pairs={{0,8},{8,0},{1,9},{9,1},{2,10},{10,2},{3,11},{11,3},{4,12},{12,4},... | collective-permute-start | bytes 1966088 | tf_op jit(solution)/shard_map/ppermute | solution.py:21
  92.5 1.3 shard_map.75
  95.0 1.3 collective-permute-done.22.vb
  96.3 1.5 shard_map.76
  97.7 1.7 convolution_convert_fusion
  99.5 2.8 %collective-permute-start.23 = (bf16[64,1280]{1,0:T(8,128)(2,1)S(1)}, bf16[64,1280]{1,0:T(8,128)(2,1)S(1)}, u32[]{:S(2)}, u32[]{:S(2)}) collective-permute-start(bf16[64,1280]{1,0:T(8,128)(2,1)S(1)} %slice.239), channel_id=1, source_target_pairs={{0,4},{4,0},{1,5},{5,1},{2,6},{6,2},{3,7},{7,3},{8,12},{12,8},{9,1... | collective-permute-start | bytes 491528 | tf_op jit(solution)/shard_map/ppermute | solution.py:21
  102.8 1.4 collective-permute-start.27
  104.2 2.3 %collective-permute-done.23 = bf16[64,1280]{1,0:T(8,128)(2,1)S(1)} collective-permute-done((bf16[64,1280]{1,0:T(8,128)(2,1)S(1)}, bf16[64,1280]{1,0:T(8,128)(2,1)S(1)}, u32[]{:S(2)}, u32[]{:S(2)}) %collective-permute-start.23) | collective-permute-done | bytes 163872 | tf_op jit(solution)/shard_map/ppermute | solution.py:21
  107.6 2.7 %fusion.40 = (bf16[320,5120]{1,0:T(8,128)(2,1)S(1)}, f32[320,5120]{1,0:T(8,128)S(1)}) fusion(bf16[320,640]{1,0:T(8,128)(2,1)S(1)} %shard_map.77, bf16[640,5120]{1,0:T(8,128)(2,1)S(1)} %bitcast.89), kind=kOutput, calls=%fused_computation.88 | convolution fusion | flops 2098790400 | bytes 16793600 | tf_op jit(solution)/shard_map/dot_general | solution.py:218
  110.4 6.8 %collective-permute-done.24 = bf16[64,3840]{1,0:T(8,128)(2,1)S(1)} collective-permute-done((bf16[64,3840]{1,0:T(8,128)(2,1)S(1)}, bf16[64,3840]{1,0:T(8,128)(2,1)S(1)}, u32[]{:S(2)}, u32[]{:S(2)}) %collective-permute-start.24) | collective-permute-done | bytes 491552 | tf_op jit(solution)/shard_map/ppermute | solution.py:21
  117.5 1.4 collective-permute-start.25
  119.6 2.8 %collective-permute-start.33 = (bf16[64,5120]{1,0:T(8,128)(2,1)S(1)}, bf16[64,5120]{1,0:T(8,128)(2,1)S(1)}, u32[]{:S(2)}, u32[]{:S(2)}) collective-permute-start(bf16[64,5120]{1,0:T(8,128)(2,1)S(1)} %add_convert_fusion), channel_id=1, source_target_pairs={{0,4},{4,0},{1,5},{5,1},{2,6},{6,2},{3,7},{7,3},{8,12},{12,8},{9,1... | collective-permute-start | bytes 1966088 | tf_op jit(solution)/shard_map/ppermute | solution.py:21
  122.4 2.7 %collective-permute-start.30 = (bf16[64,2560]{1,0:T(8,128)(2,1)S(1)}, bf16[64,2560]{1,0:T(8,128)(2,1)S(1)}, u32[]{:S(2)}, u32[]{:S(2)}) collective-permute-start(bf16[64,2560]{1,0:T(8,128)(2,1)S(1)} %get-tuple-element.57), channel_id=1, source_target_pairs={{0,3},{1,0},{2,1},{3,2},{4,7},{5,4},{6,5},{7,6},{8,11},{9,8},{10,9... | collective-permute-start | bytes 983048 | tf_op jit(solution)/shard_map/ppermute | solution.py:21
  125.6 1.1 collective-permute-done.25
  127.0 2.6 %collective-permute-start.32 = (bf16[64,2560]{1,0:T(8,128)(2,1)S(1)}, bf16[64,2560]{1,0:T(8,128)(2,1)S(1)}, u32[]{:S(2)}, u32[]{:S(2)}) collective-permute-start(bf16[64,2560]{1,0:T(8,128)(2,1)S(1)} %get-tuple-element.59), channel_id=1, source_target_pairs={{0,3},{1,0},{2,1},{3,2},{4,7},{5,4},{6,5},{7,6},{8,11},{9,8},{10,9... | collective-permute-start | bytes 983048 | tf_op jit(solution)/shard_map/ppermute | solution.py:21
  129.7 4.1 %collective-permute-done.29 = bf16[64,2560]{1,0:T(8,128)(2,1)S(1)} collective-permute-done((bf16[64,2560]{1,0:T(8,128)(2,1)S(1)}, bf16[64,2560]{1,0:T(8,128)(2,1)S(1)}, u32[]{:S(2)}, u32[]{:S(2)}) %collective-permute-start.29) | collective-permute-done | bytes 327712 | tf_op jit(solution)/shard_map/ppermute | solution.py:21
  133.8 7.0 %collective-permute-done.26 = bf16[64,2560]{1,0:T(8,128)(2,1)S(1)} collective-permute-done((bf16[64,2560]{1,0:T(8,128)(2,1)S(1)}, bf16[64,2560]{1,0:T(8,128)(2,1)S(1)}, u32[]{:S(2)}, u32[]{:S(2)}) %collective-permute-start.26) | collective-permute-done | bytes 327712 | tf_op jit(solution)/shard_map/ppermute | solution.py:21
  141.4 16.7 %all_to_all.10 = bf16[16,4,5120]{2,1,0:T(4,128)(2,1)S(1)} all-to-all(bf16[16,4,5120]{2,1,0:T(4,128)(2,1)S(1)} %reshape.14), channel_id=1, replica_groups=mesh['xl'=2,'y'=4,'core'=2,'xh'=2,'z'=4] {'xl','y','core'}, dimensions={0} | all-to-all | bytes 1310720 | tf_op jit(solution)/shard_map/all_to_all | solution.py:240
  158.3 15.1 %all_to_all.11 = bf16[16,4,5120]{2,1,0:T(4,128)(2,1)S(1)} all-to-all(bf16[16,4,5120]{2,1,0:T(4,128)(2,1)S(1)} %reduce-window_convert_fusion), channel_id=1, replica_groups=mesh['xl'=2,'y'=4,'core'=2,'xh'=2,'z'=4] {'xl','y','core'}, dimensions={0} | all-to-all | bytes 1310720 | tf_op jit(solution)/shard_map/all_to_all | solution.py:242
  173.5 1.2 add_bitcast_fusion
  (109 shorter events, 14.3 us)
Async XLA Ops:
  0.0 5.4 %copy-start = (bf16[3,320,640]{2,1,0:T(8,128)(2,1)S(1)}, bf16[3,320,640]{2,1,0:T(8,128)(2,1)}, u32[]{:S(2)}) copy-start(bf16[3,320,640]{2,1,0:T(8,128)(2,1)} %param.12) | copy-start | bytes 3686404
  3.9 5.6 %collective-permute-start = (bf16[64,2560]{1,0:T(8,128)(2,1)}, bf16[64,2560]{1,0:T(8,128)(2,1)S(1)}, u32[]{:S(2)}, u32[]{:S(2)}) collective-permute-start(bf16[64,2560]{1,0:T(8,128)(2,1)} %get-tuple-element.34), channel_id=1, source_target_pairs={{0,8},{8,0},{1,9},{9,1},{2,10},{10,2},{3,11},{11,3},{4,12},{12,4},... | collective-permute-start | bytes 983048 | tf_op jit(solution)/shard_map/ppermute | solution.py:21
  5.4 29.2 %collective-permute-start.2 = (bf16[3,320,640]{2,1,0:T(8,128)(2,1)S(1)}, bf16[3,320,640]{2,1,0:T(8,128)(2,1)S(1)}, u32[]{:S(2)}, u32[]{:S(2)}) collective-permute-start(bf16[3,320,640]{2,1,0:T(8,128)(2,1)S(1)} %copy-done), channel_id=1, source_target_pairs={{0,48},{16,0},{32,16},{48,32},{1,49},{17,1},{33,17},{49,33},{2,50}... | collective-permute-start | bytes 3686408 | tf_op jit(solution)/shard_map/ppermute | solution.py:21
  8.2 29.5 %collective-permute-start.3 = (bf16[3,320,640]{2,1,0:T(8,128)(2,1)S(1)}, bf16[3,320,640]{2,1,0:T(8,128)(2,1)S(1)}, u32[]{:S(2)}, u32[]{:S(2)}) collective-permute-start(bf16[3,320,640]{2,1,0:T(8,128)(2,1)S(1)} %copy-done), channel_id=1, source_target_pairs={{0,16},{16,32},{32,48},{48,0},{1,17},{17,33},{33,49},{49,1},{2,18}... | collective-permute-start | bytes 3686408 | tf_op jit(solution)/shard_map/ppermute | solution.py:21
  8.3 19.6 %collective-permute-start.7 = (bf16[2,320,640]{2,1,0:T(8,128)(2,1)S(1)}, bf16[2,320,640]{2,1,0:T(8,128)(2,1)S(1)}, u32[]{:S(2)}, u32[]{:S(2)}) collective-permute-start(bf16[2,320,640]{2,1,0:T(8,128)(2,1)S(1)} %slice.162), channel_id=1, source_target_pairs={{0,64},{64,0},{1,65},{65,1},{2,66},{66,2},{3,67},{67,3},{4,68},{68... | collective-permute-start | bytes 2457608 | tf_op jit(solution)/shard_map/ppermute | solution.py:21
  10.6 20.0 %collective-permute-start.1 = (bf16[2,64,2560]{2,1,0:T(8,128)(2,1)S(1)}, bf16[2,64,2560]{2,1,0:T(8,128)(2,1)S(1)}, u32[]{:S(2)}, u32[]{:S(2)}) collective-permute-start(bf16[2,64,2560]{2,1,0:T(8,128)(2,1)S(1)} %pad_maximum_fusion.5), channel_id=1, source_target_pairs={{0,3},{1,0},{2,1},{3,2},{4,7},{5,4},{6,5},{7,6},{8,11},{9,8},{10,9... | collective-permute-start | bytes 1966088 | tf_op jit(solution)/shard_map/ppermute | solution.py:21
  14.4 16.5 %collective-permute-start.5 = (bf16[2,64,2560]{2,1,0:T(8,128)(2,1)S(1)}, bf16[2,64,2560]{2,1,0:T(8,128)(2,1)S(1)}, u32[]{:S(2)}, u32[]{:S(2)}) collective-permute-start(bf16[2,64,2560]{2,1,0:T(8,128)(2,1)S(1)} %pad_maximum_fusion.5), channel_id=1, source_target_pairs={{0,1},{1,2},{2,3},{3,0},{4,5},{5,6},{6,7},{7,4},{8,9},{9,10},{10,1... | collective-permute-start | bytes 1966088 | tf_op jit(solution)/shard_map/ppermute | solution.py:21
  27.8 16.5 %collective-permute-start.8 = (bf16[2,64,2560]{2,1,0:T(8,128)(2,1)S(1)}, bf16[2,64,2560]{2,1,0:T(8,128)(2,1)S(1)}, u32[]{:S(2)}, u32[]{:S(2)}) collective-permute-start(bf16[2,64,2560]{2,1,0:T(8,128)(2,1)S(1)} %pad_maximum_fusion.5), channel_id=1, source_target_pairs={{0,4},{4,0},{1,5},{5,1},{2,6},{6,2},{3,7},{7,3},{8,12},{12,8},{9,1... | collective-permute-start | bytes 1966088 | tf_op jit(solution)/shard_map/ppermute | solution.py:21
  31.0 21.1 %collective-permute-start.13 = (bf16[2,320,640]{2,1,0:T(8,128)(2,1)S(1)}, bf16[2,320,640]{2,1,0:T(8,128)(2,1)S(1)}, u32[]{:S(2)}, u32[]{:S(2)}) collective-permute-start(bf16[2,320,640]{2,1,0:T(8,128)(2,1)S(1)} %collective-permute-done.7), channel_id=1, source_target_pairs={{0,48},{16,0},{32,16},{48,32},{1,49},{17,1},{33,17},{49,33},{2,50}... | collective-permute-start | bytes 2457608 | tf_op jit(solution)/shard_map/ppermute | solution.py:21
  33.3 21.4 %collective-permute-start.15 = (bf16[2,320,640]{2,1,0:T(8,128)(2,1)S(1)}, bf16[2,320,640]{2,1,0:T(8,128)(2,1)S(1)}, u32[]{:S(2)}, u32[]{:S(2)}) collective-permute-start(bf16[2,320,640]{2,1,0:T(8,128)(2,1)S(1)} %collective-permute-done.7), channel_id=1, source_target_pairs={{0,16},{16,32},{32,48},{48,0},{1,17},{17,33},{33,49},{49,1},{2,18}... | collective-permute-start | bytes 2457608 | tf_op jit(solution)/shard_map/ppermute | solution.py:21
  34.6 7.0 %copy-start.3 = (bf16[3,320,640]{2,1,0:T(8,128)(2,1)}, bf16[3,320,640]{2,1,0:T(8,128)(2,1)S(1)}, u32[]{:S(2)}) copy-start(bf16[3,320,640]{2,1,0:T(8,128)(2,1)S(1)} %collective-permute-done.2) | copy-start | bytes 3686404
  37.7 3.9 %copy-start.1 = (bf16[3,320,640]{2,1,0:T(8,128)(2,1)}, bf16[3,320,640]{2,1,0:T(8,128)(2,1)S(1)}, u32[]{:S(2)}) copy-start(bf16[3,320,640]{2,1,0:T(8,128)(2,1)S(1)} %collective-permute-done.3) | copy-start | bytes 3686404
  37.7 8.8 %collective-permute-start.4 = (bf16[2,32,2560]{2,1,0:T(8,128)(2,1)S(1)}, bf16[2,32,2560]{2,1,0:T(8,128)(2,1)S(1)}, u32[]{:S(2)}, u32[]{:S(2)}) collective-permute-start(bf16[2,32,2560]{2,1,0:T(8,128)(2,1)S(1)} %slice.208), channel_id=1, source_target_pairs={{0,3},{1,0},{2,1},{3,2},{4,7},{5,4},{6,5},{7,6},{8,11},{9,8},{10,9... | collective-permute-start | bytes 983048 | tf_op jit(solution)/shard_map/ppermute | solution.py:21
  41.4 8.2 %collective-permute-start.6 = (bf16[2,32,2560]{2,1,0:T(8,128)(2,1)S(1)}, bf16[2,32,2560]{2,1,0:T(8,128)(2,1)S(1)}, u32[]{:S(2)}, u32[]{:S(2)}) collective-permute-start(bf16[2,32,2560]{2,1,0:T(8,128)(2,1)S(1)} %slice.209), channel_id=1, source_target_pairs={{0,1},{1,2},{2,3},{3,0},{4,5},{5,6},{6,7},{7,4},{8,9},{9,10},{10,1... | collective-permute-start | bytes 983048 | tf_op jit(solution)/shard_map/ppermute | solution.py:21
  41.9 9.3 %copy-start.4 = (bf16[64,2560]{1,0:T(8,128)(2,1)S(1)}, bf16[64,2560]{1,0:T(8,128)(2,1)}, u32[]{:S(2)}) copy-start(bf16[64,2560]{1,0:T(8,128)(2,1)} %get-tuple-element.33) | copy-start | bytes 983044
  44.4 34.1 %collective-permute-start.19 = (bf16[3,320,640]{2,1,0:T(8,128)(2,1)S(1)}, bf16[3,320,640]{2,1,0:T(8,128)(2,1)S(1)}, u32[]{:S(2)}, u32[]{:S(2)}) collective-permute-start(bf16[3,320,640]{2,1,0:T(8,128)(2,1)S(1)} %pad_maximum_fusion.1), channel_id=1, source_target_pairs={{0,64},{64,0},{1,65},{65,1},{2,66},{66,2},{3,67},{67,3},{4,68},{68... | collective-permute-start | bytes 3686408 | tf_op jit(solution)/shard_map/ppermute | solution.py:21
  49.6 13.1 %collective-permute-start.9 = (bf16[2,64,2560]{2,1,0:T(8,128)(2,1)S(1)}, bf16[2,64,2560]{2,1,0:T(8,128)(2,1)S(1)}, u32[]{:S(2)}, u32[]{:S(2)}) collective-permute-start(bf16[2,64,2560]{2,1,0:T(8,128)(2,1)S(1)} %collective-permute-done.8), channel_id=1, source_target_pairs={{0,3},{1,0},{2,1},{3,2},{4,7},{5,4},{6,5},{7,6},{8,11},{9,8},{10,9... | collective-permute-start | bytes 1966088 | tf_op jit(solution)/shard_map/ppermute | solution.py:21
  49.9 14.3 %collective-permute-start.10 = (bf16[2,64,2560]{2,1,0:T(8,128)(2,1)S(1)}, bf16[2,64,2560]{2,1,0:T(8,128)(2,1)S(1)}, u32[]{:S(2)}, u32[]{:S(2)}) collective-permute-start(bf16[2,64,2560]{2,1,0:T(8,128)(2,1)S(1)} %collective-permute-done.8), channel_id=1, source_target_pairs={{0,1},{1,2},{2,3},{3,0},{4,5},{5,6},{6,7},{7,4},{8,9},{9,10},{10,1... | collective-permute-start | bytes 1966088 | tf_op jit(solution)/shard_map/ppermute | solution.py:21
  51.2 1.1 slice-start.3
  52.0 2.8 %slice-start.2 = ((bf16[3,320,640]{2,1,0:T(8,128)(2,1)}), bf16[3,160,640]{2,1,0:T(8,128)(2,1)S(1)}, s32[]{:S(2)}) async-start(bf16[3,320,640]{2,1,0:T(8,128)(2,1)} %copy-done.1), calls=%async_computation.4 | async-start | bytes 1228800 | tf_op jit(solution)/shard_map/slice | solution.py:166
  52.4 2.8 %copy-start.2 = (bf16[3,320,640]{2,1,0:T(8,128)(2,1)S(1)}, bf16[3,320,640]{2,1,0:T(8,128)(2,1)}, u32[]{:S(2)}) copy-start(bf16[3,320,640]{2,1,0:T(8,128)(2,1)} %copy-done.1) | copy-start | bytes 3686404
  52.4 31.5 %collective-permute-start.14 = (bf16[5,160,640]{2,1,0:T(8,128)(2,1)S(1)}, bf16[5,160,640]{2,1,0:T(8,128)(2,1)S(1)}, u32[]{:S(2)}, u32[]{:S(2)}) collective-permute-start(bf16[5,160,640]{2,1,0:T(8,128)(2,1)S(1)} %pad_maximum_fusion.2), channel_id=1, source_target_pairs={{0,48},{16,0},{32,16},{48,32},{1,49},{17,1},{33,17},{49,33},{2,50}... | collective-permute-start | bytes 3072008 | tf_op jit(solution)/shard_map/ppermute | solution.py:21
  55.0 29.1 %collective-permute-start.16 = (bf16[5,160,640]{2,1,0:T(8,128)(2,1)S(1)}, bf16[5,160,640]{2,1,0:T(8,128)(2,1)S(1)}, u32[]{:S(2)}, u32[]{:S(2)}) collective-permute-start(bf16[5,160,640]{2,1,0:T(8,128)(2,1)S(1)} %pad_maximum_fusion.3), channel_id=1, source_target_pairs={{0,16},{16,32},{32,48},{48,0},{1,17},{17,33},{33,49},{49,1},{2,18}... | collective-permute-start | bytes 3072008 | tf_op jit(solution)/shard_map/ppermute | solution.py:21
  64.1 6.2 %collective-permute-start.11 = (bf16[2,32,2560]{2,1,0:T(8,128)(2,1)S(1)}, bf16[2,32,2560]{2,1,0:T(8,128)(2,1)S(1)}, u32[]{:S(2)}, u32[]{:S(2)}) collective-permute-start(bf16[2,32,2560]{2,1,0:T(8,128)(2,1)S(1)} %slice.210), channel_id=1, source_target_pairs={{0,3},{1,0},{2,1},{3,2},{4,7},{5,4},{6,5},{7,6},{8,11},{9,8},{10,9... | collective-permute-start | bytes 983048 | tf_op jit(solution)/shard_map/ppermute | solution.py:21
  66.5 7.5 %collective-permute-start.12 = (bf16[2,32,2560]{2,1,0:T(8,128)(2,1)S(1)}, bf16[2,32,2560]{2,1,0:T(8,128)(2,1)S(1)}, u32[]{:S(2)}, u32[]{:S(2)}) collective-permute-start(bf16[2,32,2560]{2,1,0:T(8,128)(2,1)S(1)} %slice.211), channel_id=1, source_target_pairs={{0,1},{1,2},{2,3},{3,0},{4,5},{5,6},{6,7},{7,4},{8,9},{9,10},{10,1... | collective-permute-start | bytes 983048 | tf_op jit(solution)/shard_map/ppermute | solution.py:21
  78.5 13.9 %collective-permute-start.21 = (bf16[160,640]{1,0:T(8,128)(2,1)S(1)}, bf16[160,640]{1,0:T(8,128)(2,1)S(1)}, u32[]{:S(2)}, u32[]{:S(2)}) collective-permute-start(bf16[160,640]{1,0:T(8,128)(2,1)S(1)} %get-tuple-element.48), channel_id=1, source_target_pairs={{0,16},{16,32},{32,48},{48,0},{1,17},{17,33},{33,49},{49,1},{2,18}... | collective-permute-start | bytes 614408 | tf_op jit(solution)/shard_map/ppermute | solution.py:21
  78.7 13.8 %collective-permute-start.20 = (bf16[160,640]{1,0:T(8,128)(2,1)S(1)}, bf16[160,640]{1,0:T(8,128)(2,1)S(1)}, u32[]{:S(2)}, u32[]{:S(2)}) collective-permute-start(bf16[160,640]{1,0:T(8,128)(2,1)S(1)} %get-tuple-element.47), channel_id=1, source_target_pairs={{0,48},{16,0},{32,16},{48,32},{1,49},{17,1},{33,17},{49,33},{2,50}... | collective-permute-start | bytes 614408 | tf_op jit(solution)/shard_map/ppermute | solution.py:21
  84.2 13.5 %slice-start = ((s8[6553600]{0:T(1024)(128)(4,1)}), s8[4194304]{0:T(1024)(128)(4,1)S(1)}, s32[]{:S(2)}) async-start(s8[6553600]{0:T(1024)(128)(4,1)} %bitcast.88), calls=%async_computation.2 | async-start | bytes 8388608
  86.7 7.8 %collective-permute-start.17 = (bf16[512,640]{1,0:T(8,128)(2,1)S(1)}, bf16[512,640]{1,0:T(8,128)(2,1)S(1)}, u32[]{:S(2)}, u32[]{:S(2)}) collective-permute-start(bf16[512,640]{1,0:T(8,128)(2,1)S(1)} %get-tuple-element.43), channel_id=1, source_target_pairs={{0,8},{8,0},{1,9},{9,1},{2,10},{10,2},{3,11},{11,3},{4,12},{12,4},... | collective-permute-start | bytes 1966088 | tf_op jit(solution)/shard_map/ppermute | solution.py:21
  92.3 2.7 %collective-permute-start.18 = (bf16[512,640]{1,0:T(8,128)(2,1)S(1)}, bf16[512,640]{1,0:T(8,128)(2,1)S(1)}, u32[]{:S(2)}, u32[]{:S(2)}) collective-permute-start(bf16[512,640]{1,0:T(8,128)(2,1)S(1)} %get-tuple-element.45), channel_id=1, source_target_pairs={{0,8},{8,0},{1,9},{9,1},{2,10},{10,2},{3,11},{11,3},{4,12},{12,4},... | collective-permute-start | bytes 1966088 | tf_op jit(solution)/shard_map/ppermute | solution.py:21
  92.5 5.3 %slice-start.1 = ((s8[6553600]{0:T(1024)(128)(4,1)}), s8[2359296]{0:T(1024)(128)(4,1)S(1)}, s32[]{:S(2)}) async-start(s8[6553600]{0:T(1024)(128)(4,1)} %bitcast.88), calls=%async_computation.3 | async-start | bytes 4718592
  93.8 2.4 %collective-permute-start.22 = (bf16[512,640]{1,0:T(8,128)(2,1)S(1)}, bf16[512,640]{1,0:T(8,128)(2,1)S(1)}, u32[]{:S(2)}, u32[]{:S(2)}) collective-permute-start(bf16[512,640]{1,0:T(8,128)(2,1)S(1)} %get-tuple-element.50), channel_id=1, source_target_pairs={{0,8},{8,0},{1,9},{9,1},{2,10},{10,2},{3,11},{11,3},{4,12},{12,4},... | collective-permute-start | bytes 1966088 | tf_op jit(solution)/shard_map/ppermute | solution.py:21
  99.5 7.0 %collective-permute-start.23 = (bf16[64,1280]{1,0:T(8,128)(2,1)S(1)}, bf16[64,1280]{1,0:T(8,128)(2,1)S(1)}, u32[]{:S(2)}, u32[]{:S(2)}) collective-permute-start(bf16[64,1280]{1,0:T(8,128)(2,1)S(1)} %slice.239), channel_id=1, source_target_pairs={{0,4},{4,0},{1,5},{5,1},{2,6},{6,2},{3,7},{7,3},{8,12},{12,8},{9,1... | collective-permute-start | bytes 491528 | tf_op jit(solution)/shard_map/ppermute | solution.py:21
  102.4 16.5 %collective-permute-start.28 = (bf16[64,5120]{1,0:T(8,128)(2,1)S(1)}, bf16[64,5120]{1,0:T(8,128)(2,1)S(1)}, u32[]{:S(2)}, u32[]{:S(2)}) collective-permute-start(bf16[64,5120]{1,0:T(8,128)(2,1)S(1)} %get-tuple-element.66), channel_id=1, source_target_pairs={{0,3},{1,0},{2,1},{3,2},{4,7},{5,4},{6,5},{7,6},{8,11},{9,8},{10,9... | collective-permute-start | bytes 1966088 | tf_op jit(solution)/shard_map/ppermute | solution.py:21
  102.5 14.6 %collective-permute-start.24 = (bf16[64,3840]{1,0:T(8,128)(2,1)S(1)}, bf16[64,3840]{1,0:T(8,128)(2,1)S(1)}, u32[]{:S(2)}, u32[]{:S(2)}) collective-permute-start(bf16[64,3840]{1,0:T(8,128)(2,1)S(1)} %slice.243), channel_id=1, source_target_pairs={{0,4},{4,0},{1,5},{5,1},{2,6},{6,2},{3,7},{7,3},{8,12},{12,8},{9,1... | collective-permute-start | bytes 1474568 | tf_op jit(solution)/shard_map/ppermute | solution.py:21
  102.8 16.5 %collective-permute-start.27 = (bf16[64,5120]{1,0:T(8,128)(2,1)S(1)}, bf16[64,5120]{1,0:T(8,128)(2,1)S(1)}, u32[]{:S(2)}, u32[]{:S(2)}) collective-permute-start(bf16[64,5120]{1,0:T(8,128)(2,1)S(1)} %get-tuple-element.65), channel_id=1, source_target_pairs={{0,1},{1,2},{2,3},{3,0},{4,5},{5,6},{6,7},{7,4},{8,9},{9,10},{10,1... | collective-permute-start | bytes 1966088 | tf_op jit(solution)/shard_map/ppermute | solution.py:21
  117.4 8.2 %collective-permute-start.31 = (bf16[64,2560]{1,0:T(8,128)(2,1)S(1)}, bf16[64,2560]{1,0:T(8,128)(2,1)S(1)}, u32[]{:S(2)}, u32[]{:S(2)}) collective-permute-start(bf16[64,2560]{1,0:T(8,128)(2,1)S(1)} %get-tuple-element.90), channel_id=1, source_target_pairs={{0,3},{1,0},{2,1},{3,2},{4,7},{5,4},{6,5},{7,6},{8,11},{9,8},{10,9... | collective-permute-start | bytes 983048 | tf_op jit(solution)/shard_map/ppermute | solution.py:21
  117.5 23.3 %copy-start.6 = (f32[1,5120]{1,0:T(1,128)S(1)}, f32[1,5120]{1,0:T(1,128)}, u32[]{:S(2)}) copy-start(f32[1,5120]{1,0:T(1,128)} %get-tuple-element.32) | copy-start | bytes 61444
  117.5 9.3 %collective-permute-start.25 = (bf16[64,2560]{1,0:T(8,128)(2,1)S(1)}, bf16[64,2560]{1,0:T(8,128)(2,1)S(1)}, u32[]{:S(2)}, u32[]{:S(2)}) collective-permute-start(bf16[64,2560]{1,0:T(8,128)(2,1)S(1)} %get-tuple-element.91), channel_id=1, source_target_pairs={{0,1},{1,2},{2,3},{3,0},{4,5},{5,6},{6,7},{7,4},{8,9},{9,10},{10,1... | collective-permute-start | bytes 983048 | tf_op jit(solution)/shard_map/ppermute | solution.py:21
  119.6 21.2 %collective-permute-start.33 = (bf16[64,5120]{1,0:T(8,128)(2,1)S(1)}, bf16[64,5120]{1,0:T(8,128)(2,1)S(1)}, u32[]{:S(2)}, u32[]{:S(2)}) collective-permute-start(bf16[64,5120]{1,0:T(8,128)(2,1)S(1)} %add_convert_fusion), channel_id=1, source_target_pairs={{0,4},{4,0},{1,5},{5,1},{2,6},{6,2},{3,7},{7,3},{8,12},{12,8},{9,1... | collective-permute-start | bytes 1966088 | tf_op jit(solution)/shard_map/ppermute | solution.py:21
  122.4 11.4 %collective-permute-start.29 = (bf16[64,2560]{1,0:T(8,128)(2,1)S(1)}, bf16[64,2560]{1,0:T(8,128)(2,1)S(1)}, u32[]{:S(2)}, u32[]{:S(2)}) collective-permute-start(bf16[64,2560]{1,0:T(8,128)(2,1)S(1)} %get-tuple-element.56), channel_id=1, source_target_pairs={{0,1},{1,2},{2,3},{3,0},{4,5},{5,6},{6,7},{7,4},{8,9},{9,10},{10,1... | collective-permute-start | bytes 983048 | tf_op jit(solution)/shard_map/ppermute | solution.py:21
  122.4 11.4 %collective-permute-start.30 = (bf16[64,2560]{1,0:T(8,128)(2,1)S(1)}, bf16[64,2560]{1,0:T(8,128)(2,1)S(1)}, u32[]{:S(2)}, u32[]{:S(2)}) collective-permute-start(bf16[64,2560]{1,0:T(8,128)(2,1)S(1)} %get-tuple-element.57), channel_id=1, source_target_pairs={{0,3},{1,0},{2,1},{3,2},{4,7},{5,4},{6,5},{7,6},{8,11},{9,8},{10,9... | collective-permute-start | bytes 983048 | tf_op jit(solution)/shard_map/ppermute | solution.py:21
  126.9 13.9 %collective-permute-start.26 = (bf16[64,2560]{1,0:T(8,128)(2,1)S(1)}, bf16[64,2560]{1,0:T(8,128)(2,1)S(1)}, u32[]{:S(2)}, u32[]{:S(2)}) collective-permute-start(bf16[64,2560]{1,0:T(8,128)(2,1)S(1)} %get-tuple-element.60), channel_id=1, source_target_pairs={{0,1},{1,2},{2,3},{3,0},{4,5},{5,6},{6,7},{7,4},{8,9},{9,10},{10,1... | collective-permute-start | bytes 983048 | tf_op jit(solution)/shard_map/ppermute | solution.py:21
  127.0 13.8 %collective-permute-start.32 = (bf16[64,2560]{1,0:T(8,128)(2,1)S(1)}, bf16[64,2560]{1,0:T(8,128)(2,1)S(1)}, u32[]{:S(2)}, u32[]{:S(2)}) collective-permute-start(bf16[64,2560]{1,0:T(8,128)(2,1)S(1)} %get-tuple-element.59), channel_id=1, source_target_pairs={{0,3},{1,0},{2,1},{3,2},{4,7},{5,4},{6,5},{7,6},{8,11},{9,8},{10,9... | collective-permute-start | bytes 983048 | tf_op jit(solution)/shard_map/ppermute | solution.py:21
  158.1 15.4 %copy-start.5 = (f32[64,5120]{1,0:T(8,128)S(1)}, f32[64,5120]{1,0:T(8,128)}, u32[]{:S(2)}) copy-start(f32[64,5120]{1,0:T(8,128)} %param.8) | copy-start | bytes 3932164
